TPU v7x, 256 devices: a whole 4x4x8 slice. The times are simulated.
256 devices in a mesh: vocab: 64 (over y, x, z_lo, core), tokens: 4 (over z_hi).
Axes of the slice: x: 4, y: 4, z: 8 (z_hi: 4, z_lo: 2; z = z_hi * 2 + z_lo), core: 2. Of those that a mesh axis runs over, the one named last changes fastest.
Arguments:
- teacher_hidden: bfloat16 [256, 4096], P('vocab', 'tokens'), may hold values from -80 to 80
- student_hidden: bfloat16 [256, 5120], P('vocab', 'tokens'), may hold values from -10 to 10
- teacher_head: bfloat16 [4096, 151936], P('tokens', 'vocab'), may hold values from -1.1 to 1.1
- student_head: bfloat16 [5120, 151936], P('tokens', 'vocab'), may hold values from -6 to 6
- token_ids: int32 [256], P('vocab'), may hold values from 0 to 151935
- valid: int32 [256], P('vocab'), may hold values from 0 to 1, as said below
Outputs:
- loss: float32 [], replicated
- student_grad: bfloat16 [256, 5120], P('vocab', 'tokens')
Inputs may be any that keep to these rules, and one draw needn't show every extreme that they name: The last row is always valid.
All inputs are finite; a program needn't handle non-finite values.
Results may differ from a plain program's by a relative error of at most 0.005.
Values may be sent and summed in bfloat16 or wider, within the bound.
No kernel may reach another device: no remote copies, remote signals or barrier semaphores. Data moves between devices by JAX's collectives and lax.ppermute only.
A program may use at most 64 MiB of HBM per device.

v0:
```python
import jax
import jax.numpy as jnp
from jax import lax
from jax.sharding import PartitionSpec as P


def on_device(teacher_hidden, student_hidden, teacher_head, student_head, token_ids, valid):
    teacher_logits = jnp.dot(
        lax.all_gather(teacher_hidden, "vocab", axis=0, tiled=True),
        teacher_head,
        preferred_element_type=jnp.float32,
    )
    student_logits = jnp.dot(
        lax.all_gather(student_hidden, "vocab", axis=0, tiled=True),
        student_head,
        preferred_element_type=jnp.float32,
    )
    labels = lax.all_gather(jnp.stack([token_ids, valid]), "vocab", axis=1, tiled=True)
    shard_width = teacher_head.shape[1]
    offset = lax.axis_index("vocab") * shard_width
    teacher_logits, student_logits = (
        lax.psum_scatter(teacher_logits, "tokens", scatter_dimension=0, tiled=True),
        lax.psum_scatter(student_logits, "tokens", scatter_dimension=0, tiled=True),
    )
    group = teacher_logits.shape[0]
    first_row = lax.axis_index("tokens") * group
    labels_here = lax.dynamic_slice_in_dim(labels, first_row, group, 1)
    sampled = labels_here[0]
    mask = labels_here[1].astype(jnp.float32)
    columns = offset + jnp.arange(shard_width, dtype=jnp.int32)
    onehot = columns[None, :] == sampled[:, None]
    local_pick = jnp.sum(jnp.where(onehot, student_logits, jnp.float32(0.0)), axis=1)
    teacher_top, student_top = lax.pmax(
        (jnp.max(teacher_logits, axis=1), jnp.max(student_logits, axis=1)), "vocab"
    )
    teacher_exp = jnp.exp(teacher_logits - teacher_top[:, None])
    student_exp = jnp.exp(student_logits - student_top[:, None])
    teacher_total, student_total, cross_term, picked = lax.psum(
        (
            jnp.sum(teacher_exp, axis=1),
            jnp.sum(student_exp, axis=1),
            jnp.sum(teacher_exp * (teacher_logits - student_logits), axis=1),
            local_pick,
        ),
        "vocab",
    )
    teacher_lse = teacher_top + jnp.log(teacher_total)
    student_lse = student_top + jnp.log(student_total)
    per_row = cross_term / teacher_total - teacher_lse + 2.0 * student_lse - picked
    teacher_prob = jnp.exp(teacher_logits - teacher_lse[:, None])
    student_prob = jnp.exp(student_logits - student_lse[:, None])
    logit_grad = (
        mask[:, None] * (2.0 * student_prob - teacher_prob - onehot.astype(jnp.float32))
    ).astype(jnp.bfloat16)
    loss_part = jnp.sum(mask * per_row)
    valid_count = jnp.sum(mask)
    grad_full = lax.all_gather(logit_grad, "tokens", axis=0, tiled=True)
    loss_part, valid_count = lax.psum((loss_part, valid_count), "tokens")
    loss = loss_part / valid_count
    student_grad = lax.psum_scatter(
        lax.dot_general(
            grad_full, student_head, (((1,), (1,)), ((), ())), preferred_element_type=jnp.float32
        ),
        "vocab",
        scatter_dimension=0,
        tiled=True,
    )
    return (loss, student_grad.astype(jnp.bfloat16))


def solution(mesh):
    in_specs = (
        P("vocab", "tokens"),
        P("vocab", "tokens"),
        P("tokens", "vocab"),
        P("tokens", "vocab"),
        P("vocab"),
        P("vocab"),
    )
    out_specs = (P(), P("vocab", "tokens"))
    return jax.shard_map(
        on_device, mesh=mesh, in_specs=in_specs, out_specs=out_specs, check_vma=False
    )
```

profile of v0, /device:TPU:1, one launch (start us, length us, event | category | flops | bytes accessed | tf_op | source)
XLA Modules:
  0.0 907.6 jit_solution(17165812275864855569)
XLA Ops:
  7.2 86.9 %all-gather.2 = bf16[64,4,1280]{2,1,0:T(4,128)(2,1)S(1)} all-gather(bf16[1,4,1280]{2,1,0:T(4,128)(2,1)} %bitcast.25), channel_id=1, replica_groups=mesh['vocab'=64,'tokens'=4] {'vocab'}, dimensions={0}, use_global_device_ids=true | all-gather | bytes 665600 | tf_op jit(solution)/shard_map/all_gather | solution.py:14
  94.1 0.2 reshape.24
  94.2 6.1 fusion.6
  100.3 0.0 reduce-scatter.3.cloned.1.call-start
  100.4 87.3 %all-gather.1 = bf16[64,4,1024]{2,1,0:T(4,128)(2,1)S(1)} all-gather(bf16[1,4,1024]{2,1,0:T(4,128)(2,1)S(1)} %bitcast.26), channel_id=1, replica_groups=mesh['vocab'=64,'tokens'=4] {'vocab'}, dimensions={0}, use_global_device_ids=true | all-gather | bytes 532480 | tf_op jit(solution)/shard_map/all_gather | solution.py:9
  187.7 0.1 reshape.22
  187.8 5.4 fusion.5
  193.3 83.7 %all-gather = s32[64,4,2]{1,2,0:T(2,128)S(1)} all-gather(s32[1,4,2]{1,2,0:T(2,128)S(1)} %add_bitcast_fusion), channel_id=1, replica_groups=mesh['vocab'=64,'tokens'=4] {'vocab'}, dimensions={0}, use_global_device_ids=true | all-gather | bytes 2080 | tf_op jit(solution)/shard_map/all_gather | solution.py:18
  277.1 0.1 reshape.20
  277.2 0.1 dynamic-slice_bitcast_fusion
  277.3 1.2 reduce_max.19
  278.5 1.2 reduce_max.18
  279.7 138.0 %all-reduce.3 = (f32[64]{0:T(128)S(1)}, f32[64]{0:T(128)S(1)}) all-reduce(f32[64]{0:T(128)S(1)} %reduce_max.18, f32[64]{0:T(128)S(1)} %reduce_max.19), channel_id=1, replica_groups=mesh['vocab'=64,'tokens'=4] {'vocab'}, use_global_device_ids=true, to_apply=%region_2.3 | all-reduce | flops 128 | bytes 1024 | tf_op jit(solution)/shard_map/pmax | solution.py:33
  417.7 1.8 multiply_reduce_fusion
  419.5 138.7 %all-reduce.2 = (f32[64]{0:T(128)S(1)}, f32[64]{0:T(128)S(1)}) all-reduce(f32[64]{0:T(128)S(1)} %get-tuple-element.5, f32[64]{0:T(128)S(1)} %get-tuple-element.3), channel_id=1, replica_groups=mesh['vocab'=64,'tokens'=4] {'vocab'}, use_global_device_ids=true, to_apply=%region_11.12 | all-reduce | flops 128 | bytes 1024 | tf_op jit(solution)/shard_map/psum | solution.py:38
  558.2 2.4 fusion.3
  560.7 0.6 dynamic-slice.1
  561.9 0.6 convert_reduce_fusion
  562.5 33.4 %all-gather.5.cloned.1.call-done = bf16[256,2374]{1,0:T(8,128)(2,1)} async-done(((bf16[64,2374]{1,0:T(8,128)(2,1)}), bf16[256,2374]{1,0:T(8,128)(2,1)}) %all-gather.5.cloned.1.call-update) | async-done | bytes 1215504 | tf_op jit(solution)/shard_map/all_gather | solution.py:57
  595.9 5.0 fusion.7
  600.9 286.8 %all-reduce.6 = (f32[64]{0:T(128)S(1)}, f32[64]{0:T(128)S(1)}, bf16[256,1280]{1,0:T(8,128)(2,1)S(1)}) all-reduce(f32[64]{0:T(128)S(1)} %get-tuple-element.4, f32[64]{0:T(128)S(1)} %get-tuple-element.2, f32[256,1280]{1,0:T(8,128)S(1)} %fusion.7), channel_id=1, replica_groups=mesh['vocab'=64,'tokens'=4] {'vocab'}, use_global_device_ids=true, to_apply=%region_13.14 | all-reduce | flops 327808 | bytes 1967104 | tf_op jit(solution)/shard_map/psum | solution.py:38
  887.6 0.6 multiply_reduce_fusion.1
  888.2 0.6 dynamic-slice_convert_fusion
  888.8 9.9 %all-reduce.4 = (f32[]{:T(128)}, f32[]{:T(128)}) all-reduce(f32[]{:T(128)} %multiply_reduce_fusion.1, f32[]{:T(128)} %convert_reduce_fusion), channel_id=1, replica_groups=mesh['vocab'=64,'tokens'=4] {'tokens'}, use_global_device_ids=true, to_apply=%region_15.16 | all-reduce | flops 2 | bytes 16 | tf_op jit(solution)/shard_map/psum | solution.py:58
  (20 shorter events, 0.2 us)
Async XLA Ops:
  7.2 270.1 %reduce-scatter.5.cloned.1.call-start = ((), (), s32[]{:S(2)}) async-start(), calls=%async_computation.3 | async-start | bytes 3112960 | tf_op jit(solution)/shard_map/reduce_scatter | solution.py:23
  94.2 6.2 copy-start
  100.3 178.2 %reduce-scatter.3.cloned.1.call-start = ((), (), s32[]{:S(2)}) async-start(), calls=%async_computation.2 | async-start | bytes 3112960 | tf_op jit(solution)/shard_map/reduce_scatter | solution.py:22
  187.8 5.5 copy-start.1
  187.8 5.5 copy-start.2
  193.2 367.4 %copy-start.3 = (u32[256]{0:T(256)S(1)}, u32[256]{0:T(256)}, u32[]{:S(2)}) copy-start(u32[256]{0:T(256)} %constant.32) | copy-start | bytes 3076
  193.2 402.6 %all-gather.5.cloned.1.call-start = ((), (), s32[]{:S(2)}) async-start(), calls=%async_computation.4 | async-start | bytes 1556480 | tf_op jit(solution)/shard_map/all_gather | solution.py:57
Sparse Core Ops, SparseCore 0:
  100.4 56.2 reduce-scatter.4
  193.4 55.5 reduce-scatter.2
  560.8 35.0 all-gather.4
where the time goes:
time: 913 us; the launch traced here: 908 us
  blocking collectives  831 us (91%)
  waiting for transfers between devices  33.5 us (4%)
  between operations  16.9 us (2%)
  matrix products  16.4 us (2%)
    psum x2, blocking collectives, on_device(): lax.psum((jnp.sum(teacher_exp, axis=1), jnp.sum(student_exp, axis=1), jnp...  426 us
    pmax x1, blocking collectives, on_device(): lax.pmax((jnp.max(teacher_logits, axis=1), jnp.max(student_logits, axis=1...  138 us
    all_gather x1, blocking collectives, on_device(): lax.all_gather(teacher_hidden, 'vocab', axis=0, tiled=True)  87.3 us
    all_gather x1, blocking collectives, on_device(): lax.all_gather(student_hidden, 'vocab', axis=0, tiled=True)  86.9 us
    all_gather x1, blocking collectives, on_device(): lax.all_gather(jnp.stack([token_ids, valid]), 'vocab', axis=1, tiled=True)  83.7 us
    all_gather x1, waiting for transfers between devices, on_device(): grad_full = lax.all_gather(logit_grad, 'tokens', axis=0, tiled=True)  33.4 us
  transfers between devices with their start and end apart: 3, of which 1 were waited for; matrix products, arithmetic and copies ran while one was open for 1% of the time, Pallas kernels for 0%

commit v1 on v0

v1 whole, which is shorter than its diff:
```python
import functools

import jax
import jax.numpy as jnp
from jax import lax
from jax.experimental import pallas as pl
from jax.experimental.pallas import tpu as pltpu
from jax.sharding import Mesh, PartitionSpec as P

VOCAB = ("y", "x", "zl", "c")
CHIPS = ("y", "x", "zl")
ROWS = 256
LIVE = 192
GROUP = LIVE // 4
LEFT = 1280
BLOCK = 512
STEP = 512.0
BOUND = 63.9
F32 = jnp.float32
BF16 = jnp.bfloat16
I16 = jnp.int16
NT = (((1,), (1,)), ((), ()))
VMEM = pl.BlockSpec(memory_space=pltpu.VMEM)
SMEM = pl.BlockSpec(memory_space=pltpu.SMEM)


def struct(shape, dtype):
    return jax.ShapeDtypeStruct(shape, dtype)


def call(body, outs, *args, scratch=(), mb=32):
    return pl.pallas_call(
        body,
        out_shape=outs,
        in_specs=[SMEM] + [VMEM] * (len(args) - 1),
        out_specs=[VMEM] * len(outs),
        scratch_shapes=scratch,
        compiler_params=pltpu.CompilerParams(vmem_limit_bytes=mb << 20),
    )(*args)


def padded(width):
    return -(-width // 128) * 128


def coded(x):
    return jnp.clip(jnp.round(x * STEP), -32767.0, 32767.0).astype(jnp.int32).astype(I16)


def decoded(x):
    return x.astype(jnp.int32).astype(F32) * (1.0 / STEP)


def iota(shape, axis):
    return lax.broadcasted_iota(jnp.int32, shape, axis)


def order_kernel(scal, own, other, pick_own, pick_other, back_own, back_other, sampled, total):
    me, core = scal[0], scal[1].astype(F32)
    wide = own.shape[0]
    line, lane = iota((wide, wide), 0), iota((wide, wide), 1)
    even = lane - lane % 2
    before = (line < even).astype(F32).astype(BF16)
    same = (line == even).astype(F32).astype(BF16)
    found = []
    for ref in (own, other):
        labels = ref[:, ref.shape[1] - 128 :].astype(F32).T[:8].astype(BF16)
        earlier = jnp.dot(labels, before, preferred_element_type=F32)[3:4]
        here = jnp.dot(labels, same, preferred_element_type=F32)
        ids = here[0:1] + 256.0 * here[1:2] + 65536.0 * here[2:3]
        found.append((here[3:4] > 0.5, earlier, ids, 0.5 * jnp.sum(here[3:4], keepdims=True)))
    start = (core * found[1][3], (1.0 - core) * found[0][3])
    shift = (me * GROUP).astype(F32)
    picked = jnp.zeros((GROUP, 1), F32)
    for (ok, earlier, ids, _), base, pick, back in zip(
        found, start, (pick_own, pick_other), (back_own, back_other)
    ):
        slot = base + earlier
        near = slot - shift
        near = jnp.where(near < 0.0, near + LIVE, near)
        near = jnp.where(ok & (slot < LIVE), near, -1.0)
        column = jnp.broadcast_to(near, (8, wide)).T[:, 0:1]
        row = iota((LIVE, wide), 0).astype(F32)
        odd = iota((LIVE, wide), 1) % 2
        hit = row == near
        slots = iota((wide, LIVE), 1).astype(F32)
        turn = iota((wide, LIVE), 0) % 2
        back_hit = slots == column
        for half in (0, 1):
            pick[half] = (hit & (odd == half)).astype(F32).astype(BF16)
            back[half] = (back_hit & (turn == half)).astype(F32).astype(BF16)
        chosen = (hit & (odd == 0))[:GROUP]
        picked += jnp.sum(jnp.where(chosen, ids, 0.0), axis=1, keepdims=True)
    sampled[...] = jnp.broadcast_to(picked, sampled.shape)
    total[...] = jnp.broadcast_to(found[0][3] + found[1][3], total.shape)


def logits_kernel(
    width, half, scal, pick_own, pick_other, own, other, head,
    up, down, mine, next_left, last_right, peak, rows, logits,
):
    step = pl.program_id(0)

    @pl.when(step == 0)
    def _():
        for k in (0, 1):
            rows[:, k * half : (k + 1) * half] = (
                jnp.dot(pick_own[k], own[:, :half], preferred_element_type=F32)
                + jnp.dot(pick_other[k], other[:, :half], preferred_element_type=F32)
            ).astype(BF16)

    start = pl.multiple_of(step * BLOCK, BLOCK)
    logits[:, pl.ds(start, BLOCK)] = lax.dot_general(
        rows[...], head[...], NT, preferred_element_type=F32
    )

    @pl.when(step == pl.num_programs(0) - 1)
    def _():
        full = padded(width)
        edge = full - 128
        tail = logits[:, edge:full]
        logits[:, edge:full] = jnp.where(iota(tail.shape, 1) < width - edge, tail, 0.0)
        g = GROUP
        up[:, :LEFT] = coded(logits[2 * g : 3 * g, :LEFT])
        up[:, LEFT:] = coded(logits[g : 2 * g, LEFT:full])
        down[:, :LEFT] = coded(logits[3 * g : 4 * g, :LEFT])
        down[:, LEFT:] = coded(logits[2 * g : 3 * g, LEFT:full])
        mine[...] = logits[:g, :full]
        next_left[...] = logits[g : 2 * g, :LEFT]
        last_right[...] = logits[3 * g : 4 * g, LEFT:full]
        peak[...] = jnp.broadcast_to(
            jnp.max(jnp.abs(logits[g:, :full]), keepdims=True), peak.shape
        )


def partial_logits(scal, picks, own, other, head_t, half):
    width, depth = head_t.shape
    full = padded(width)
    outs = (
        struct((GROUP, full), I16),
        struct((GROUP, full), I16),
        struct((GROUP, full), F32),
        struct((GROUP, LEFT), F32),
        struct((GROUP, full - LEFT), F32),
        struct((8, 128), F32),
    )
    steps = pl.cdiv(width, BLOCK)

    def whole(x):
        return pl.BlockSpec(x.shape, lambda i: (0,) * len(x.shape))

    return pl.pallas_call(
        functools.partial(logits_kernel, width, half),
        grid=(steps,),
        out_shape=outs,
        in_specs=[SMEM]
        + [whole(x) for x in (*picks, own, other)]
        + [pl.BlockSpec((BLOCK, depth), lambda i: (i, 0))],
        out_specs=[whole(x) for x in outs],
        scratch_shapes=[
            pltpu.VMEM((LIVE, depth), BF16),
            pltpu.VMEM((LIVE, steps * BLOCK), F32),
        ],
        compiler_params=pltpu.CompilerParams(vmem_limit_bytes=32 << 20),
    )(scal, *picks, own, other, head_t)


def relay_kernel(scal, got_up, got_down, mine, next_left, last_right, up, down, sums, peak):
    left = next_left[...] + decoded(got_up[:, :LEFT])
    right = last_right[...] + decoded(got_down[:, LEFT:])
    up[...] = coded(left)
    down[...] = coded(right)
    sums[:, :LEFT] = mine[:, :LEFT] + decoded(got_down[:, :LEFT])
    sums[:, LEFT:] = mine[:, LEFT:] + decoded(got_up[:, LEFT:])
    top = jnp.maximum(
        jnp.max(jnp.abs(left), keepdims=True), jnp.max(jnp.abs(right), keepdims=True)
    )
    peak[...] = jnp.broadcast_to(top, peak.shape)


def stats_kernel(
    width, scal, t_sum, t_up, t_down, s_sum, s_up, s_down, sampled, p0, p1, p2, p3,
    t_out, s_out, stats, square,
):
    for total, up, down, out in ((t_sum, t_up, t_down, t_out), (s_sum, s_up, s_down, s_out)):
        out[:, :LEFT] = total[:, :LEFT] + decoded(up[...])
        out[:, LEFT:] = total[:, LEFT:] + decoded(down[...])
    t, s = t_out[...], s_out[...]
    column = iota(t.shape, 1)
    inside = column < width
    onehot = (column + scal[2] == sampled[:, 0:1].astype(jnp.int32)) & inside
    t_top = jnp.max(jnp.where(inside, t, -jnp.inf), axis=1, keepdims=True)
    s_top = jnp.max(jnp.where(inside, s, -jnp.inf), axis=1, keepdims=True)
    t_exp = jnp.where(inside, jnp.exp(t - t_top), 0.0)
    s_exp = jnp.where(inside, jnp.exp(s - s_top), 0.0)
    values = (
        t_top,
        s_top,
        jnp.sum(t_exp, axis=1, keepdims=True),
        jnp.sum(s_exp, axis=1, keepdims=True),
        jnp.sum(t_exp * (t - s), axis=1, keepdims=True),
        jnp.sum(jnp.where(onehot, s, 0.0), axis=1, keepdims=True),
    )
    lane = iota((GROUP, 128), 1)
    board = jnp.zeros((GROUP, 128), F32)
    for k, value in enumerate(values):
        board = jnp.where(lane == k, value, board)
    square[...] = jnp.zeros(square.shape, F32)
    square[:GROUP] = board
    flipped = square[...].T[:8]
    peak = jnp.maximum(jnp.maximum(p0[...], p1[...]), jnp.maximum(p2[...], p3[...]))
    stats[...] = jnp.where(iota((8, 128), 0) == 6, peak, flipped)


def grad_kernel(width, scal, every, t_ref, s_ref, sampled, total, left, right, tally):
    e = every[...]
    most = jnp.max(e, axis=0)
    t_top, s_top, peak = most[0:1], most[1:2], most[6:7]
    t_scale = jnp.exp(e[:, 0:1] - t_top[None])
    s_scale = jnp.exp(e[:, 1:2] - s_top[None])
    t_total = jnp.sum(e[:, 2:3] * t_scale, axis=0)
    s_total = jnp.sum(e[:, 3:4] * s_scale, axis=0)
    cross = jnp.sum(e[:, 4:5] * t_scale, axis=0)
    picked = jnp.sum(e[:, 5:6], axis=0)
    t_lse = t_top + jnp.log(t_total)
    s_lse = s_top + jnp.log(s_total)
    per_row = cross / t_total - t_lse + 2.0 * s_lse - picked
    first = scal[0] * GROUP
    count = total[0:1, 0:1].astype(jnp.int32)
    lane = iota((1, 128), 1)
    live = (lane < GROUP) & (lane + first < count)
    part = jnp.sum(jnp.where(live, per_row, 0.0), axis=1, keepdims=True)
    spot = iota((8, 128), 1)
    tally[...] = jnp.where(spot == 0, part, jnp.where(spot == 1, jnp.max(peak, keepdims=True), 0.0))
    line = iota((8, 128), 0)
    turned = jnp.where(line == 0, t_lse, s_lse).T
    t_col, s_col = turned[:GROUP, 0:1], turned[:GROUP, 1:2]
    t, s = t_ref[...], s_ref[...]
    column = iota(t.shape, 1)
    onehot = (column + scal[2] == sampled[:, 0:1].astype(jnp.int32)).astype(F32)
    grad = 2.0 * jnp.exp(s - s_col) - jnp.exp(t - t_col) - onehot
    keep = (column < width) & (iota(t.shape, 0) + first < count)
    grad = jnp.where(keep, grad, 0.0)
    left[...] = grad[:, :LEFT].astype(BF16)
    right[...] = grad[:, LEFT:].astype(BF16)


def back_kernel(
    width, half, a0, b0, a1, b1, a2, b2, a3, b3, back_own, back_other, head,
    mine, theirs, grads, total,
):
    step = pl.program_id(0)
    full = padded(width)

    @pl.when(step == 0)
    def _():
        for k, (a, b) in enumerate(((a0, b0), (a1, b1), (a2, b2), (a3, b3))):
            grads[k * GROUP : (k + 1) * GROUP, :LEFT] = a[...]
            grads[k * GROUP : (k + 1) * GROUP, LEFT:full] = b[...]
        grads[:, full:] = jnp.zeros((LIVE, grads.shape[1] - full), BF16)
        total[...] = jnp.zeros(total.shape, F32)

    start = pl.multiple_of(step * BLOCK, BLOCK)
    block = head[...]
    block = jnp.where(iota(block.shape, 0) + start < width, block, jnp.zeros_like(block))
    total[...] += jnp.dot(grads[:, pl.ds(start, BLOCK)], block, preferred_element_type=F32)

    @pl.when(step == pl.num_programs(0) - 1)
    def _():
        x = total[...]
        high = x.astype(BF16)
        low = (x - high.astype(F32)).astype(BF16)
        for back, out in ((back_own, mine), (back_other, theirs)):
            y = jnp.zeros(out.shape, F32)
            for k in (0, 1):
                cut = slice(k * half, (k + 1) * half)
                y += jnp.dot(back[k], high[:, cut], preferred_element_type=F32)
                y += jnp.dot(back[k], low[:, cut], preferred_element_type=F32)
            out[...] = y


def hidden_grad(pieces, backs, head_t):
    width, depth = head_t.shape
    steps = pl.cdiv(width, BLOCK)
    outs = (struct((ROWS, depth // 2), F32),) * 2

    def whole(x):
        return pl.BlockSpec(x.shape, lambda i: (0,) * len(x.shape))

    return pl.pallas_call(
        functools.partial(back_kernel, width, depth // 2),
        grid=(steps,),
        out_shape=outs,
        in_specs=[whole(x) for x in (*pieces, *backs)]
        + [pl.BlockSpec((BLOCK, depth), lambda i: (i, 0))],
        out_specs=[whole(x) for x in outs],
        scratch_shapes=[
            pltpu.VMEM((LIVE, steps * BLOCK), BF16),
            pltpu.VMEM((LIVE, depth), F32),
        ],
        compiler_params=pltpu.CompilerParams(vmem_limit_bytes=32 << 20),
    )(*pieces, *backs, head_t)


def hop(x, by):
    return lax.ppermute(x, "t", [(i, (i + by) % 4) for i in range(4)])


def swap_cores(x):
    return lax.ppermute(x, "c", [(0, 1), (1, 0)])


def spread(x, axes, n):
    return lax.all_to_all(
        jnp.broadcast_to(x[None], (n,) + x.shape), axes, split_axis=0, concat_axis=0, tiled=True
    )


def pack_labels(token_ids, valid):
    parts = (token_ids % 256, (token_ids // 256) % 256, token_ids // 65536, valid)
    rows = jnp.stack(parts, axis=1).astype(BF16)
    return jnp.pad(rows[:, None], ((0, 0), (0, 1), (0, 124))).reshape(8, 128)


def short_way(teacher_hidden, student_hidden, teacher_head, student_head, token_ids, valid):
    dt, ds = teacher_hidden.shape[1], student_hidden.shape[1]
    width = teacher_head.shape[1]
    full = padded(width)
    scal = jnp.stack(
        [lax.axis_index("t"), lax.axis_index("c"), lax.axis_index(VOCAB) * width]
    ).astype(jnp.int32)
    first = jnp.concatenate(
        [teacher_hidden.reshape(8, dt // 2), pack_labels(token_ids, valid)], axis=1
    )
    t_own = spread(first, CHIPS, 32).reshape(ROWS, dt // 2 + 128)
    t_other = swap_cores(t_own)
    s_own = spread(student_hidden.reshape(8, ds // 2), CHIPS, 32).reshape(ROWS, ds // 2)
    s_other = swap_cores(s_own)
    pick_own, pick_other, back_own, back_other, sampled, total = call(
        order_kernel,
        (struct((2, LIVE, ROWS), BF16),) * 2
        + (struct((2, ROWS, LIVE), BF16),) * 2
        + (struct((GROUP, 128), F32), struct((8, 128), F32)),
        scal, t_own, t_other,
    )
    sums, peaks = [], []
    for own, other, head, depth in (
        (t_own, t_other, teacher_head, dt),
        (s_own, s_other, student_head, ds),
    ):
        up, down, mine, next_left, last_right, peak = partial_logits(
            scal, (pick_own, pick_other), own, other, head.T, depth // 2
        )
        got_up, got_down = hop(up, 1), hop(down, -1)
        up, down, mine, late = call(
            relay_kernel,
            (
                struct((GROUP, LEFT), I16),
                struct((GROUP, full - LEFT), I16),
                struct((GROUP, full), F32),
                struct((8, 128), F32),
            ),
            scal, got_up, got_down, mine, next_left, last_right,
        )
        sums += [mine, hop(up, 1), hop(down, -1)]
        peaks += [peak, late]
    t_logits, s_logits, stats = call(
        functools.partial(stats_kernel, width),
        (struct((GROUP, full), F32),) * 2 + (struct((8, 128), F32),),
        scal, *sums, sampled, *peaks,
        scratch=[pltpu.VMEM((128, 128), F32)],
    )
    every = spread(stats, VOCAB, 64)
    a0, b0, tally = call(
        functools.partial(grad_kernel, width),
        (
            struct((GROUP, LEFT), BF16),
            struct((GROUP, full - LEFT), BF16),
            struct((8, 128), F32),
        ),
        scal, every, t_logits, s_logits, sampled, total,
    )
    a3, b1 = hop(a0, 1), hop(b0, -1)
    b3, a1 = hop(b0, 1), hop(a0, -1)
    a2, b2 = hop(a3, 1), hop(b1, -1)
    tallies = (tally, hop(tally, 2), hop(tally, 1), hop(tally, -1))
    mine, theirs = hidden_grad((a0, b0, a1, b1, a2, b2, a3, b3), (back_own, back_other), student_head.T)
    pair = (mine + swap_cores(theirs)).astype(BF16).reshape(32, 8, ds // 2)
    got = lax.all_to_all(pair, CHIPS, split_axis=0, concat_axis=0, tiled=True)
    grad = jnp.sum(got.astype(F32), axis=0).astype(BF16).reshape(4, ds)
    count = total[0, 0]
    part = (tallies[0][0, 0] + tallies[1][0, 0]) + (tallies[2][0, 0] + tallies[3][0, 0])
    peak = jnp.maximum(
        jnp.maximum(tallies[0][0, 1], tallies[1][0, 1]),
        jnp.maximum(tallies[2][0, 1], tallies[3][0, 1]),
    )
    return part / count, grad, (count <= LIVE) & (peak < BOUND)


def long_way(teacher_hidden, student_hidden, teacher_head, student_head, token_ids, valid):
    ds = student_hidden.shape[1]
    width = teacher_head.shape[1]
    group = ROWS // 4
    labels = jnp.pad(jnp.stack([token_ids, valid]), ((0, 6), (0, 124)))
    labels = spread(labels, VOCAB, 64)[:, :2, :4].transpose(1, 0, 2).reshape(2, ROWS)

    def logits(hidden, head):
        rows = spread(hidden, VOCAB, 64).reshape(ROWS, hidden.shape[1])
        part = jnp.dot(rows, head, preferred_element_type=F32).reshape(4, group, width)
        return jnp.sum(lax.all_to_all(part, "t", split_axis=0, concat_axis=0, tiled=True), axis=0)

    teacher_logits = logits(teacher_hidden, teacher_head)
    student_logits = logits(student_hidden, student_head)
    here = lax.dynamic_slice_in_dim(labels, lax.axis_index("t") * group, group, 1)
    sampled, mask = here[0], here[1].astype(F32)
    columns = lax.axis_index(VOCAB) * width + jnp.arange(width, dtype=jnp.int32)
    onehot = columns[None, :] == sampled[:, None]
    t_top = jnp.max(teacher_logits, axis=1)
    s_top = jnp.max(student_logits, axis=1)
    t_exp = jnp.exp(teacher_logits - t_top[:, None])
    s_exp = jnp.exp(student_logits - s_top[:, None])
    stats = jnp.stack(
        [
            t_top,
            s_top,
            jnp.sum(t_exp, axis=1),
            jnp.sum(s_exp, axis=1),
            jnp.sum(t_exp * (teacher_logits - student_logits), axis=1),
            jnp.sum(jnp.where(onehot, student_logits, F32(0.0)), axis=1),
        ]
    )
    every = spread(jnp.pad(stats, ((0, 2), (0, 128 - group))), VOCAB, 64)[:, :, :group]
    teacher_top = jnp.max(every[:, 0], axis=0)
    student_top = jnp.max(every[:, 1], axis=0)
    t_scale = jnp.exp(every[:, 0] - teacher_top)
    s_scale = jnp.exp(every[:, 1] - student_top)
    teacher_total = jnp.sum(every[:, 2] * t_scale, axis=0)
    student_total = jnp.sum(every[:, 3] * s_scale, axis=0)
    cross_term = jnp.sum(every[:, 4] * t_scale, axis=0)
    picked = jnp.sum(every[:, 5], axis=0)
    teacher_lse = teacher_top + jnp.log(teacher_total)
    student_lse = student_top + jnp.log(student_total)
    per_row = cross_term / teacher_total - teacher_lse + 2.0 * student_lse - picked
    loss = lax.psum(jnp.sum(mask * per_row), "t") / jnp.sum(labels[1]).astype(F32)
    teacher_prob = jnp.exp(teacher_logits - teacher_lse[:, None])
    student_prob = jnp.exp(student_logits - student_lse[:, None])
    logit_grad = (
        mask[:, None] * (2.0 * student_prob - teacher_prob - onehot.astype(F32))
    ).astype(BF16)
    part = lax.dot_general(
        lax.all_gather(logit_grad, "t", axis=0, tiled=True), student_head, NT,
        preferred_element_type=F32,
    )
    got = lax.all_to_all(part.reshape(64, 4, ds), VOCAB, split_axis=0, concat_axis=0, tiled=True)
    return loss, jnp.sum(got, axis=0).astype(BF16)


def on_device(*args):
    loss, grad, fits = short_way(*args)
    return lax.cond(fits, lambda *_: (loss, grad), long_way, *args)


def solution(mesh):
    fine = Mesh(mesh.devices.reshape(4, 4, 2, 2, 4), VOCAB + ("t",))
    in_specs = (
        P(VOCAB, "t"),
        P(VOCAB, "t"),
        P("t", VOCAB),
        P("t", VOCAB),
        P(VOCAB),
        P(VOCAB),
    )
    return jax.shard_map(
        on_device, mesh=fine, in_specs=in_specs, out_specs=(P(), P(VOCAB, "t")), check_vma=False
    )
```

time: 913 us -> 436 us (0.48)
  blocking collectives: 831 us -> 91 us
  waiting for transfers between devices: 33.5 us -> 188 us
  starting transfers between devices: 0.12 us -> 80.6 us
  Pallas kernels: 0 us -> 19.3 us
  local copies, waits for them, and re-layouts: 1.68 us -> 12.1 us
    psum x3 -> x1, blocking collectives: 435 us -> 18.4 us  [long_way(): lax.psum(jnp.sum(mask * per_row), 't') / jnp.sum(labels[1]).astype(F32)]
    all_gather x3 -> x0, blocking collectives: 258 us -> none  [the longest x1 87.3 us: on_device(): lax.all_gather(teacher_hidden, 'vocab', axis=0, tiled=True)]
    pmax x1 -> x0, blocking collectives: 138 us -> none  [on_device(): lax.pmax((jnp.max(teacher_logits, axis=1), jnp.max(student_logits, axis=1...]
    all_to_all x0 -> x7, waiting for transfers between devices: none -> 123 us  [the longest x2 98.1 us: logits(): lax.all_to_all(part, 't', split_axis=0, concat_axis=0, tiled=True)]
    all_to_all x0 -> x4, blocking collectives: none -> 72.6 us  [spread(): lax.all_to_all(jnp.broadcast_to(x[None], (n,) + x.shape), axes, split_axi...]
    all_to_all x0 -> x7, starting transfers between devices: none -> 40.7 us  [the longest x3 17.6 us: spread(): lax.all_to_all(jnp.broadcast_to(x[None], (n,) + x.shape), axes, split_axi...]
    ppermute x0 -> x20, starting transfers between devices: none -> 39.9 us  [the longest x17 34.5 us: hop(): return lax.ppermute(x, 't', [(i, (i + by) % 4) for i in range(4)])]
    ppermute x0 -> x20, waiting for transfers between devices: none -> 31.9 us  [the longest x17 30.2 us: hop(): return lax.ppermute(x, 't', [(i, (i + by) % 4) for i in range(4)])]
  transfers between devices with their start and end apart: 3 -> 28, of which waited for: 1 -> 16; matrix products, arithmetic and copies ran while one was open for 1% -> 4% of each run, Pallas kernels for 0% -> 3%
where the time goes in v1:
time: 436 us; the launch traced here: 435 us
  waiting for transfers between devices  188 us (43%)
  blocking collectives  91 us (21%)
  starting transfers between devices  80.6 us (18%)
  Pallas kernels  19.3 us (4%)
  between operations  18.5 us (4%)
  matrix products  16.6 us (4%)
  local copies, waits for them, and re-layouts  12.1 us (3%)
  other arithmetic  7.78 us (2%)
    all_to_all x2, waiting for transfers between devices, logits(): lax.all_to_all(part, 't', split_axis=0, concat_axis=0, tiled=True)  98.1 us
    all_to_all x4, blocking collectives, spread(): lax.all_to_all(jnp.broadcast_to(x[None], (n,) + x.shape), axes, split_axi...  72.6 us
    ppermute x17, starting transfers between devices, hop(): return lax.ppermute(x, 't', [(i, (i + by) % 4) for i in range(4)])  34.5 us
    all_gather x1, waiting for transfers between devices, long_way(): lax.all_gather(logit_grad, 't', axis=0, tiled=True)  32.8 us
    ppermute x17, waiting for transfers between devices, hop(): return lax.ppermute(x, 't', [(i, (i + by) % 4) for i in range(4)])  30.2 us
    all_to_all x3, waiting for transfers between devices, spread(): lax.all_to_all(jnp.broadcast_to(x[None], (n,) + x.shape), axes, split_axi...  24.1 us
    psum x1, blocking collectives, long_way(): lax.psum(jnp.sum(mask * per_row), 't') / jnp.sum(labels[1]).astype(F32)  18.4 us
    all_to_all x3, starting transfers between devices, spread(): lax.all_to_all(jnp.broadcast_to(x[None], (n,) + x.shape), axes, split_axi...  17.6 us
  transfers between devices with their start and end apart: 28, of which 16 were waited for; matrix products, arithmetic and copies ran while one was open for 4% of the time, Pallas kernels for 3%

profile of v1, /device:TPU:1, one launch (start us, length us, event | category | flops | bytes accessed | tf_op | source)
XLA Modules:
  0.0 435.2 jit_solution(14844732266212938361)
XLA Ops:
  9.5 9.2 %all-to-all-start.7 = ((bf16[32,8,640]{2,1,0:T(8,128)(2,1)}), bf16[32,8,640]{2,1,0:T(8,128)(2,1)S(1)}, u32[]{:S(2)}, u32[]{:S(2)}) async-start(bf16[32,8,640]{2,1,0:T(8,128)(2,1)} %broadcast_in_dim.19), calls=%async_computation.7 | async-start | bytes 655360 | tf_op jit(solution)/shard_map/all_to_all | solution.py:314
  19.4 8.5 %all-to-all-done.7 = bf16[32,8,640]{2,1,0:T(8,128)(2,1)S(1)} async-done(((bf16[32,8,640]{2,1,0:T(8,128)(2,1)}), bf16[32,8,640]{2,1,0:T(8,128)(2,1)S(1)}, u32[]{:S(2)}, u32[]{:S(2)}) %all-to-all-start.7) | async-done | bytes 327712 | tf_op jit(solution)/shard_map/all_to_all | solution.py:314
  34.5 6.8 %all-to-all-done.8 = bf16[32,8,640]{2,1,0:T(8,128)(2,1)S(1)} async-done(((bf16[32,8,640]{2,1,0:T(8,128)(2,1)}), bf16[32,8,640]{2,1,0:T(8,128)(2,1)S(1)}, u32[]{:S(2)}, u32[]{:S(2)}) %all-to-all-start.8) | async-done | bytes 327712 | tf_op jit(solution)/shard_map/all_to_all | solution.py:314
  45.4 6.5 %shard_map.82 = (s16[48,2432]{1,0:T(8,128)(2,1)S(1)}, s16[48,2432]{1,0:T(8,128)(2,1)S(1)}, f32[48,2432]{1,0:T(8,128)S(1)}, f32[48,1280]{1,0:T(8,128)S(1)}, f32[48,1152]{1,0:T(8,128)S(1)}, /*index=5*/f32[8,128]{1,0:T(8,128)S(1)}) custom-call(s32[3]{0:T(128)S(1)} %pad_add_fusion.1.scal, bf16[2,192,256]{2,1,0:T(8,128)(2,1)S(1)} %get-tuple-element.90.pick_own, ...), custom_call_target="tpu_custom_call" | custom-call | tf_op jit(solution)/shard_map/pallas_call | solution.py:152
  86.0 7.2 %collective-permute-done.4.t_down = s16[48,1152]{1,0:T(8,128)(2,1)S(1)} collective-permute-done((s16[48,1152]{1,0:T(8,128)(2,1)S(1)}, s16[48,1152]{1,0:T(8,128)(2,1)S(1)}, u32[]{:S(2)}, u32[]{:S(2)}) %collective-permute-start.4) | collective-permute-done | bytes 110624 | tf_op jit(solution)/shard_map/ppermute | solution.py:306
  97.3 14.5 %all_to_all.51.every = f32[64,8,128]{2,1,0:T(8,128)S(1)} all-to-all(f32[64,8,128]{2,1,0:T(8,128)S(1)} %broadcast_in_dim.22), channel_id=1, replica_groups=mesh['y'=4,'x'=4,'zl'=2,'c'=2,'t'=4] {'y','x','zl','c'}, dimensions={0} | all-to-all | bytes 524288 | tf_op jit(solution)/shard_map/all_to_all | solution.py:314
  118.0 4.7 %collective-permute-done.15.a3 = bf16[48,1280]{1,0:T(8,128)(2,1)S(1)} collective-permute-done((bf16[48,1280]{1,0:T(8,128)(2,1)S(1)}, bf16[48,1280]{1,0:T(8,128)(2,1)S(1)}, u32[]{:S(2)}, u32[]{:S(2)}) %collective-permute-start.15) | collective-permute-done | bytes 122912 | tf_op jit(solution)/shard_map/ppermute | solution.py:306
  127.8 5.9 %collective-permute-done.18.b3 = bf16[48,1152]{1,0:T(8,128)(2,1)S(1)} collective-permute-done((bf16[48,1152]{1,0:T(8,128)(2,1)S(1)}, bf16[48,1152]{1,0:T(8,128)(2,1)S(1)}, u32[]{:S(2)}, u32[]{:S(2)}) %collective-permute-start.18) | collective-permute-done | bytes 110624 | tf_op jit(solution)/shard_map/ppermute | solution.py:306
  140.2 5.1 %all-to-all-start.10 = ((bf16[32,8,640]{2,1,0:T(8,128)(2,1)}), bf16[32,8,640]{2,1,0:T(8,128)(2,1)S(1)}, u32[]{:S(2)}, u32[]{:S(2)}) async-start(bf16[32,8,640]{2,1,0:T(8,128)(2,1)} %fusion.9), calls=%async_computation.10 | async-start | bytes 655360 | tf_op jit(solution)/shard_map/all_to_all | solution.py:389
  157.1 270.1 %conditional.1 = (f32[]{:T(128)}, bf16[4,1280]{1,0:T(4,128)(2,1)}) conditional(s32[]{:T(128)} %convert_element_type.42, (s32[4]{0:T(128)S(1)}, s32[4]{0:T(128)S(1)}, bf16[4,1024]{1,0:T(4,128)(2,1)S(1)}, bf16[1024,2374]{0,1:T(8,128)(2,1)}, bf16[4,1280]{1,0:T(4,128)(2,1)S(1)}, /*index=5*/bf16[1280,2374]{0,1:T(8,128)(2,1)}) %tuple.45, ...), branch_computations={%region_0.19_spmd, %region_19.21_spmd} | conditional | flops 4360781312 | bytes 74072800 | solution.py:460
  157.2 19.7 %all_to_all.48 = s32[64,8,128]{2,1,0:T(8,128)S(1)} all-to-all(s32[64,8,128]{2,1,0:T(8,128)S(1)} %broadcast_in_dim.1), channel_id=1, replica_groups=mesh['y'=4,'x'=4,'zl'=2,'c'=2,'t'=4] {'y','x','zl','c'}, dimensions={0} | all-to-all | bytes 524288 | tf_op jit(solution)/shard_map/cond/branch_0_fun/all_to_all | solution.py:314
  177.1 16.9 %all_to_all.49 = bf16[64,4,1024]{2,1,0:T(4,128)(2,1)S(1)} all-to-all(bf16[64,4,1024]{2,1,0:T(4,128)(2,1)S(1)} %broadcast_in_dim.2), channel_id=1, replica_groups=mesh['y'=4,'x'=4,'zl'=2,'c'=2,'t'=4] {'y','x','zl','c'}, dimensions={0} | all-to-all | bytes 1048576 | tf_op jit(solution)/shard_map/cond/branch_0_fun/all_to_all | solution.py:314
  199.7 5.4 %fusion.2 = f32[4,64,2374]{2,1,0:T(8,128)} fusion(bf16[4,64,1024]{2,1,0:T(8,128)(2,1)S(1)} %dot_general.1, bf16[1024,2374]{0,1:T(8,128)(2,1)} %get-tuple-element.44), kind=kOutput, calls=%fused_computation.2 | convolution fusion | flops 1244659712 | bytes 7817216 | tf_op jit(solution)/shard_map/cond/branch_0_fun/dot_general | solution.py:409
  205.1 8.8 %all-to-all-done.3 = bf16[64,4,1280]{2,1,0:T(4,128)(2,1)S(1)} async-done(((bf16[64,4,1280]{2,1,0:T(4,128)(2,1)}), bf16[64,4,1280]{2,1,0:T(4,128)(2,1)S(1)}, u32[]{:S(2)}, u32[]{:S(2)}) %all-to-all-start.3) | async-done | bytes 655392 | tf_op jit(solution)/shard_map/cond/branch_0_fun/all_to_all | solution.py:314
  214.7 4.6 %all-to-all-start.2 = ((f32[4,64,2374]{2,1,0:T(8,128)}), f32[4,64,2374]{2,1,0:T(8,128)S(1)}, u32[]{:S(2)}, u32[]{:S(2)}) async-start(f32[4,64,2374]{2,1,0:T(8,128)} %fusion.2), calls=%async_computation.2 | async-start | bytes 4980736 | tf_op jit(solution)/shard_map/cond/branch_0_fun/all_to_all | solution.py:410
  221.6 6.3 %fusion = f32[4,64,2374]{2,1,0:T(8,128)} fusion(bf16[4,64,1280]{2,1,0:T(8,128)(2,1)} %dot_general.10, bf16[1280,2374]{0,1:T(8,128)(2,1)} %get-tuple-element.46), kind=kOutput, calls=%fused_computation | convolution fusion | flops 1555824640 | bytes 9163776 | tf_op jit(solution)/shard_map/cond/branch_0_fun/dot_general | solution.py:409
  227.8 47.9 %all-to-all-done.2 = f32[4,64,2374]{2,1,0:T(8,128)S(1)} async-done(((f32[4,64,2374]{2,1,0:T(8,128)}), f32[4,64,2374]{2,1,0:T(8,128)S(1)}, u32[]{:S(2)}, u32[]{:S(2)}) %all-to-all-start.2) | async-done | bytes 2431008 | tf_op jit(solution)/shard_map/cond/branch_0_fun/all_to_all | solution.py:410
  275.7 5.4 %all-to-all-start.4 = ((f32[4,64,2374]{2,1,0:T(8,128)}), f32[4,64,2374]{2,1,0:T(8,128)}, u32[]{:S(2)}, u32[]{:S(2)}) async-start(f32[4,64,2374]{2,1,0:T(8,128)} %fusion), calls=%async_computation.4 | async-start | bytes 4980736 | tf_op jit(solution)/shard_map/cond/branch_0_fun/all_to_all | solution.py:410
  281.7 50.2 %all-to-all-done.4 = f32[4,64,2374]{2,1,0:T(8,128)} async-done(((f32[4,64,2374]{2,1,0:T(8,128)}), f32[4,64,2374]{2,1,0:T(8,128)}, u32[]{:S(2)}, u32[]{:S(2)}) %all-to-all-start.4) | async-done | bytes 2431008 | tf_op jit(solution)/shard_map/cond/branch_0_fun/all_to_all | solution.py:410
  334.5 21.5 %all_to_all.50 = f32[64,8,128]{2,1,0:T(8,128)S(1)} all-to-all(f32[64,8,128]{2,1,0:T(8,128)S(1)} %broadcast_in_dim.5), channel_id=1, replica_groups=mesh['y'=4,'x'=4,'zl'=2,'c'=2,'t'=4] {'y','x','zl','c'}, dimensions={0} | all-to-all | bytes 524288 | tf_op jit(solution)/shard_map/cond/branch_0_fun/all_to_all | solution.py:314
  358.0 32.8 %all-gather.2.cloned.1.call-done = bf16[256,2374]{1,0:T(8,128)(2,1)} async-done(((bf16[64,2374]{1,0:T(8,128)(2,1)}), bf16[256,2374]{1,0:T(8,128)(2,1)}) %all-gather.2.cloned.1.call-update) | async-done | bytes 1215504 | tf_op jit(solution)/shard_map/cond/branch_0_fun/all_gather | solution.py:451
  390.8 5.0 %fusion.16 = f32[256,1280]{1,0:T(8,128)S(1)} fusion(bf16[256,2374]{1,0:T(8,128)(2,1)} %all-gather.2.cloned.1.call-done, bf16[1280,2374]{0,1:T(8,128)(2,1)} %get-tuple-element.46), kind=kOutput, calls=%fused_computation.53 | convolution fusion | flops 1555824640 | bytes 8603648 | tf_op jit(solution)/shard_map/cond/branch_0_fun/dot_general | solution.py:450
  397.2 7.9 %all-to-all-start.6 = ((f32[64,4,1280]{2,1,0:T(4,128)}), f32[64,4,1280]{2,1,0:T(4,128)S(1)}, u32[]{:S(2)}, u32[]{:S(2)}) async-start(f32[64,4,1280]{2,1,0:T(4,128)} %reshape.137), calls=%async_computation.6 | async-start | bytes 2621440 | tf_op jit(solution)/shard_map/cond/branch_0_fun/all_to_all | solution.py:454
  406.5 18.4 %psum.6 = f32[]{:T(128)} all-reduce(f32[]{:T(128)} %get-tuple-element.131), channel_id=1, replica_groups=mesh['y'=4,'x'=4,'zl'=2,'c'=2,'t'=4] {'t'}, use_global_device_ids=true, to_apply=%region_16.16 | all-reduce | flops 1 | bytes 8 | tf_op jit(solution)/shard_map/cond/branch_0_fun/psum | solution.py:444
  (110 shorter events, 96.2 us)
Async XLA Ops:
  9.5 18.4 %all-to-all-start.7 = ((bf16[32,8,640]{2,1,0:T(8,128)(2,1)}), bf16[32,8,640]{2,1,0:T(8,128)(2,1)S(1)}, u32[]{:S(2)}, u32[]{:S(2)}) async-start(bf16[32,8,640]{2,1,0:T(8,128)(2,1)} %broadcast_in_dim.19), calls=%async_computation.7 | async-start | bytes 655360 | tf_op jit(solution)/shard_map/all_to_all | solution.py:314
  28.6 12.6 %all-to-all-start.8 = ((bf16[32,8,640]{2,1,0:T(8,128)(2,1)}), bf16[32,8,640]{2,1,0:T(8,128)(2,1)S(1)}, u32[]{:S(2)}, u32[]{:S(2)}) async-start(bf16[32,8,640]{2,1,0:T(8,128)(2,1)} %broadcast_in_dim.21), calls=%async_computation.8 | async-start | bytes 655360 | tf_op jit(solution)/shard_map/all_to_all | solution.py:314
  32.5 11.7 %collective-permute-start = (bf16[256,640]{1,0:T(8,128)(2,1)S(1)}, bf16[256,640]{1,0:T(8,128)(2,1)S(1)}, u32[]{:S(2)}, u32[]{:S(2)}) collective-permute-start(bf16[256,640]{1,0:T(8,128)(2,1)S(1)} %bitcast.59), channel_id=1, source_target_pairs={{0,4},{4,0},{1,5},{5,1},{2,6},{6,2},{3,7},{7,3},{8,12},{12,8},{9,1... | collective-permute-start | bytes 983048 | tf_op jit(solution)/shard_map/ppermute | solution.py:310
  41.3 15.9 %collective-permute-start.5 = (bf16[256,640]{1,0:T(8,128)(2,1)S(1)}, bf16[256,640]{1,0:T(8,128)(2,1)S(1)}, u32[]{:S(2)}, u32[]{:S(2)}) collective-permute-start(bf16[256,640]{1,0:T(8,128)(2,1)S(1)} %bitcast.62), channel_id=1, source_target_pairs={{0,4},{4,0},{1,5},{5,1},{2,6},{6,2},{3,7},{7,3},{8,12},{12,8},{9,1... | collective-permute-start | bytes 983048 | tf_op jit(solution)/shard_map/ppermute | solution.py:310
  51.9 14.9 %collective-permute-start.1 = (s16[48,2432]{1,0:T(8,128)(2,1)S(1)}, s16[48,2432]{1,0:T(8,128)(2,1)S(1)}, u32[]{:S(2)}, u32[]{:S(2)}) collective-permute-start(s16[48,2432]{1,0:T(8,128)(2,1)S(1)} %get-tuple-element.92), channel_id=1, source_target_pairs={{0,1},{1,2},{2,3},{3,0},{4,5},{5,6},{6,7},{7,4},{8,9},{9,10},{10,1... | collective-permute-start | bytes 700424 | tf_op jit(solution)/shard_map/ppermute | solution.py:306
  55.0 14.7 %collective-permute-start.2 = (s16[48,2432]{1,0:T(8,128)(2,1)S(1)}, s16[48,2432]{1,0:T(8,128)(2,1)S(1)}, u32[]{:S(2)}, u32[]{:S(2)}) collective-permute-start(s16[48,2432]{1,0:T(8,128)(2,1)S(1)} %get-tuple-element.93), channel_id=1, source_target_pairs={{0,3},{1,0},{2,1},{3,2},{4,7},{5,4},{6,5},{7,6},{8,11},{9,8},{10,9... | collective-permute-start | bytes 700424 | tf_op jit(solution)/shard_map/ppermute | solution.py:306
  61.5 16.0 %collective-permute-start.6 = (s16[48,2432]{1,0:T(8,128)(2,1)S(1)}, s16[48,2432]{1,0:T(8,128)(2,1)S(1)}, u32[]{:S(2)}, u32[]{:S(2)}) collective-permute-start(s16[48,2432]{1,0:T(8,128)(2,1)S(1)} %get-tuple-element.100), channel_id=1, source_target_pairs={{0,1},{1,2},{2,3},{3,0},{4,5},{5,6},{6,7},{7,4},{8,9},{9,10},{10,1... | collective-permute-start | bytes 700424 | tf_op jit(solution)/shard_map/ppermute | solution.py:306
  62.7 14.8 %collective-permute-start.7 = (s16[48,2432]{1,0:T(8,128)(2,1)S(1)}, s16[48,2432]{1,0:T(8,128)(2,1)S(1)}, u32[]{:S(2)}, u32[]{:S(2)}) collective-permute-start(s16[48,2432]{1,0:T(8,128)(2,1)S(1)} %get-tuple-element.101), channel_id=1, source_target_pairs={{0,3},{1,0},{2,1},{3,2},{4,7},{5,4},{6,5},{7,6},{8,11},{9,8},{10,9... | collective-permute-start | bytes 700424 | tf_op jit(solution)/shard_map/ppermute | solution.py:306
  70.5 25.7 %collective-permute-start.3 = (s16[48,1280]{1,0:T(8,128)(2,1)S(1)}, s16[48,1280]{1,0:T(8,128)(2,1)S(1)}, u32[]{:S(2)}, u32[]{:S(2)}) collective-permute-start(s16[48,1280]{1,0:T(8,128)(2,1)S(1)} %get-tuple-element.98), channel_id=1, source_target_pairs={{0,1},{1,2},{2,3},{3,0},{4,5},{5,6},{6,7},{7,4},{8,9},{9,10},{10,1... | collective-permute-start | bytes 368648 | tf_op jit(solution)/shard_map/ppermute | solution.py:306
  78.4 17.8 %collective-permute-start.8 = (s16[48,1280]{1,0:T(8,128)(2,1)S(1)}, s16[48,1280]{1,0:T(8,128)(2,1)S(1)}, u32[]{:S(2)}, u32[]{:S(2)}) collective-permute-start(s16[48,1280]{1,0:T(8,128)(2,1)S(1)} %get-tuple-element.106), channel_id=1, source_target_pairs={{0,1},{1,2},{2,3},{3,0},{4,5},{5,6},{6,7},{7,4},{8,9},{9,10},{10,1... | collective-permute-start | bytes 368648 | tf_op jit(solution)/shard_map/ppermute | solution.py:306
  81.5 11.7 %collective-permute-start.4 = (s16[48,1152]{1,0:T(8,128)(2,1)S(1)}, s16[48,1152]{1,0:T(8,128)(2,1)S(1)}, u32[]{:S(2)}, u32[]{:S(2)}) collective-permute-start(s16[48,1152]{1,0:T(8,128)(2,1)S(1)} %get-tuple-element.99), channel_id=1, source_target_pairs={{0,3},{1,0},{2,1},{3,2},{4,7},{5,4},{6,5},{7,6},{8,11},{9,8},{10,9... | collective-permute-start | bytes 331784 | tf_op jit(solution)/shard_map/ppermute | solution.py:306
  82.0 14.2 %collective-permute-start.9 = (s16[48,1152]{1,0:T(8,128)(2,1)S(1)}, s16[48,1152]{1,0:T(8,128)(2,1)S(1)}, u32[]{:S(2)}, u32[]{:S(2)}) collective-permute-start(s16[48,1152]{1,0:T(8,128)(2,1)S(1)} %get-tuple-element.107), channel_id=1, source_target_pairs={{0,3},{1,0},{2,1},{3,2},{4,7},{5,4},{6,5},{7,6},{8,11},{9,8},{10,9... | collective-permute-start | bytes 331784 | tf_op jit(solution)/shard_map/ppermute | solution.py:306
  112.9 9.8 %collective-permute-start.15 = (bf16[48,1280]{1,0:T(8,128)(2,1)S(1)}, bf16[48,1280]{1,0:T(8,128)(2,1)S(1)}, u32[]{:S(2)}, u32[]{:S(2)}) collective-permute-start(bf16[48,1280]{1,0:T(8,128)(2,1)S(1)} %get-tuple-element.117.a0), channel_id=1, source_target_pairs={{0,1},{1,2},{2,3},{3,0},{4,5},{5,6},{6,7},{7,4},{8,9},{9,10},{10,1... | collective-permute-start | bytes 368648 | tf_op jit(solution)/shard_map/ppermute | solution.py:306
  115.6 10.8 %collective-permute-start.14 = (bf16[48,1152]{1,0:T(8,128)(2,1)S(1)}, bf16[48,1152]{1,0:T(8,128)(2,1)S(1)}, u32[]{:S(2)}, u32[]{:S(2)}) collective-permute-start(bf16[48,1152]{1,0:T(8,128)(2,1)S(1)} %get-tuple-element.118.b0), channel_id=1, source_target_pairs={{0,3},{1,0},{2,1},{3,2},{4,7},{5,4},{6,5},{7,6},{8,11},{9,8},{10,9... | collective-permute-start | bytes 331784 | tf_op jit(solution)/shard_map/ppermute | solution.py:306
  116.5 17.1 %collective-permute-start.13 = (bf16[48,1280]{1,0:T(8,128)(2,1)S(1)}, bf16[48,1280]{1,0:T(8,128)(2,1)S(1)}, u32[]{:S(2)}, u32[]{:S(2)}) collective-permute-start(bf16[48,1280]{1,0:T(8,128)(2,1)S(1)} %get-tuple-element.117.a0), channel_id=1, source_target_pairs={{0,3},{1,0},{2,1},{3,2},{4,7},{5,4},{6,5},{7,6},{8,11},{9,8},{10,9... | collective-permute-start | bytes 368648 | tf_op jit(solution)/shard_map/ppermute | solution.py:306
  122.7 11.0 %collective-permute-start.16 = (bf16[48,1280]{1,0:T(8,128)(2,1)S(1)}, bf16[48,1280]{1,0:T(8,128)(2,1)S(1)}, u32[]{:S(2)}, u32[]{:S(2)}) collective-permute-start(bf16[48,1280]{1,0:T(8,128)(2,1)S(1)} %collective-permute-done.15.a3), channel_id=1, source_target_pairs={{0,1},{1,2},{2,3},{3,0},{4,5},{5,6},{6,7},{7,4},{8,9},{9,10},{10,1... | collective-permute-start | bytes 368648 | tf_op jit(solution)/shard_map/ppermute | solution.py:306
  123.5 10.1 %collective-permute-start.18 = (bf16[48,1152]{1,0:T(8,128)(2,1)S(1)}, bf16[48,1152]{1,0:T(8,128)(2,1)S(1)}, u32[]{:S(2)}, u32[]{:S(2)}) collective-permute-start(bf16[48,1152]{1,0:T(8,128)(2,1)S(1)} %get-tuple-element.118.b0), channel_id=1, source_target_pairs={{0,1},{1,2},{2,3},{3,0},{4,5},{5,6},{6,7},{7,4},{8,9},{9,10},{10,1... | collective-permute-start | bytes 331784 | tf_op jit(solution)/shard_map/ppermute | solution.py:306
  140.2 16.9 %all-to-all-start.10 = ((bf16[32,8,640]{2,1,0:T(8,128)(2,1)}), bf16[32,8,640]{2,1,0:T(8,128)(2,1)S(1)}, u32[]{:S(2)}, u32[]{:S(2)}) async-start(bf16[32,8,640]{2,1,0:T(8,128)(2,1)} %fusion.9), calls=%async_computation.10 | async-start | bytes 655360 | tf_op jit(solution)/shard_map/all_to_all | solution.py:389
  145.3 7.4 %collective-permute-start.10 = (f32[8,128]{1,0:T(8,128)S(1)}, f32[8,128]{1,0:T(8,128)S(1)}, u32[]{:S(2)}, u32[]{:S(2)}) collective-permute-start(f32[8,128]{1,0:T(8,128)S(1)} %get-tuple-element.116), channel_id=1, source_target_pairs={{0,2},{1,3},{2,0},{3,1},{4,6},{5,7},{6,4},{7,5},{8,10},{9,11},{10,... | collective-permute-start | bytes 12296 | tf_op jit(solution)/shard_map/ppermute | solution.py:306
  195.0 18.8 %all-to-all-start.3 = ((bf16[64,4,1280]{2,1,0:T(4,128)(2,1)}), bf16[64,4,1280]{2,1,0:T(4,128)(2,1)S(1)}, u32[]{:S(2)}, u32[]{:S(2)}) async-start(bf16[64,4,1280]{2,1,0:T(4,128)(2,1)} %broadcast_in_dim.3), calls=%async_computation.3 | async-start | bytes 1310720 | tf_op jit(solution)/shard_map/cond/branch_0_fun/all_to_all | solution.py:314
  214.7 61.0 %all-to-all-start.2 = ((f32[4,64,2374]{2,1,0:T(8,128)}), f32[4,64,2374]{2,1,0:T(8,128)S(1)}, u32[]{:S(2)}, u32[]{:S(2)}) async-start(f32[4,64,2374]{2,1,0:T(8,128)} %fusion.2), calls=%async_computation.2 | async-start | bytes 4980736 | tf_op jit(solution)/shard_map/cond/branch_0_fun/all_to_all | solution.py:410
  275.7 56.2 %all-to-all-start.4 = ((f32[4,64,2374]{2,1,0:T(8,128)}), f32[4,64,2374]{2,1,0:T(8,128)}, u32[]{:S(2)}, u32[]{:S(2)}) async-start(f32[4,64,2374]{2,1,0:T(8,128)} %fusion), calls=%async_computation.4 | async-start | bytes 4980736 | tf_op jit(solution)/shard_map/cond/branch_0_fun/all_to_all | solution.py:410
  281.2 109.6 %all-gather.2.cloned.1.call-start = ((), (), s32[]{:S(2)}) async-start(), calls=%async_computation.11 | async-start | bytes 1556480 | tf_op jit(solution)/shard_map/cond/branch_0_fun/all_gather | solution.py:451
  397.2 29.2 %all-to-all-start.6 = ((f32[64,4,1280]{2,1,0:T(4,128)}), f32[64,4,1280]{2,1,0:T(4,128)S(1)}, u32[]{:S(2)}, u32[]{:S(2)}) async-start(f32[64,4,1280]{2,1,0:T(4,128)} %reshape.137), calls=%async_computation.6 | async-start | bytes 2621440 | tf_op jit(solution)/shard_map/cond/branch_0_fun/all_to_all | solution.py:454
  (10 other events, 130.1 us)
Sparse Core Ops, SparseCore 0:
  358.1 32.6 all-gather.1

commit v2 on v1

v2 whole, which is shorter than its diff:
```python
import functools

import jax
import jax.numpy as jnp
from jax import lax
from jax.experimental import pallas as pl
from jax.experimental.pallas import tpu as pltpu
from jax.sharding import Mesh, PartitionSpec as P

VOCAB = ("y", "x", "zl", "c")
CHIPS = ("y", "x", "zl")
ROWS = 256
LIVE = 192
GROUP = LIVE // 4
LEFT = 1280
BLOCK = 512
STEP = 1024.0
BOUND = 31.9
F32 = jnp.float32
BF16 = jnp.bfloat16
I16 = jnp.int16
NT = (((1,), (1,)), ((), ()))
VMEM = pl.BlockSpec(memory_space=pltpu.VMEM)
SMEM = pl.BlockSpec(memory_space=pltpu.SMEM)


def struct(shape, dtype):
    return jax.ShapeDtypeStruct(shape, dtype)


def call(body, outs, *args, scratch=(), scalars=0):
    return pl.pallas_call(
        body,
        out_shape=outs,
        in_specs=[SMEM] + [VMEM] * (len(args) - 1),
        out_specs=[VMEM] * (len(outs) - scalars) + [SMEM] * scalars,
        scratch_shapes=scratch,
        compiler_params=pltpu.CompilerParams(vmem_limit_bytes=32 << 20),
    )(*args)


def padded(width):
    return -(-width // 128) * 128


def coded(x):
    return jnp.clip(jnp.round(x * STEP), -32767.0, 32767.0).astype(jnp.int32).astype(I16)


def decoded(x):
    return x.astype(jnp.int32).astype(F32) * (1.0 / STEP)


def iota(shape, axis):
    return lax.broadcasted_iota(jnp.int32, shape, axis)


def order_kernel(at, scal, own, other, pick_own, pick_other, back_own, back_other, sampled, total):
    me, core = scal[0], scal[1].astype(F32)
    wide = own.shape[0]
    line, lane = iota((wide, wide), 0), iota((wide, wide), 1)
    even = lane - lane % 2
    before = (line < even).astype(F32).astype(BF16)
    same = (line == even).astype(F32).astype(BF16)
    found = []
    for ref in (own, other):
        labels = ref[:, at : at + 128].astype(F32).T[:8].astype(BF16)
        earlier = jnp.dot(labels, before, preferred_element_type=F32)[3:4]
        here = jnp.dot(labels, same, preferred_element_type=F32)
        ids = here[0:1] + 256.0 * here[1:2] + 65536.0 * here[2:3]
        found.append((here[3:4] > 0.5, earlier, ids, 0.5 * jnp.sum(here[3:4], keepdims=True)))
    start = (core * found[1][3], (1.0 - core) * found[0][3])
    shift = (me * GROUP).astype(F32)
    picked = jnp.zeros((GROUP, 1), F32)
    for (ok, earlier, ids, _), base, pick, back in zip(
        found, start, (pick_own, pick_other), (back_own, back_other)
    ):
        slot = base + earlier
        near = slot - shift
        near = jnp.where(near < 0.0, near + LIVE, near)
        near = jnp.where(ok & (slot < LIVE), near, -1.0)
        column = jnp.broadcast_to(near, (8, wide)).T[:, 0:1]
        row = iota((LIVE, wide), 0).astype(F32)
        odd = iota((LIVE, wide), 1) % 2
        hit = row == near
        slots = iota((wide, LIVE), 1).astype(F32)
        turn = iota((wide, LIVE), 0) % 2
        back_hit = slots == column
        for half in (0, 1):
            pick[half] = (hit & (odd == half)).astype(F32).astype(BF16)
            back[half] = (back_hit & (turn == half)).astype(F32).astype(BF16)
        chosen = (hit & (odd == 0))[:GROUP]
        picked += jnp.sum(jnp.where(chosen, ids, 0.0), axis=1, keepdims=True)
    sampled[...] = jnp.broadcast_to(picked, sampled.shape)
    total[...] = jnp.broadcast_to(found[0][3] + found[1][3], total.shape)


def logits_kernel(
    width, half, at, far, near, relayed, scal, pick_own, pick_other, own, other, head,
    first, direct, mine, held, peak, rows, logits,
):
    for k in (0, 1):
        rows[:, k * half : (k + 1) * half] = (
            jnp.dot(pick_own[k], own[:, at : at + half], preferred_element_type=F32)
            + jnp.dot(pick_other[k], other[:, at : at + half], preferred_element_type=F32)
        ).astype(BF16)
    full = padded(width)
    edge = full - 128
    logits[:, edge:full] = jnp.zeros((LIVE, 128), F32)
    for start in range(0, width, BLOCK):
        stop = min(start + BLOCK, width)
        logits[:, start:stop] = lax.dot_general(
            rows[...], head[start:stop], NT, preferred_element_type=F32
        )
    g = GROUP
    first[...] = coded(logits[far * g : (far + 1) * g])
    direct[...] = coded(logits[near * g : (near + 1) * g])
    mine[...] = logits[:g]
    held[...] = logits[relayed * g : (relayed + 1) * g]
    peak[...] = jnp.broadcast_to(jnp.max(jnp.abs(logits[g:]), keepdims=True), peak.shape)


def partial_logits(scal, picks, own, other, head_t, at, near, relayed):
    width, depth = head_t.shape
    full = padded(width)
    outs = (
        struct((GROUP, full), I16),
        struct((GROUP, full), I16),
        struct((GROUP, full), F32),
        struct((GROUP, full), F32),
        struct((8, 128), F32),
    )
    return call(
        functools.partial(logits_kernel, width, depth // 2, at, 2, near, relayed),
        outs, scal, *picks, own, other, head_t,
        scratch=[pltpu.VMEM((LIVE, depth), BF16), pltpu.VMEM((LIVE, full), F32)],
    )


def relay_kernel(scal, got, held, out, peak):
    total = held[...] + decoded(got[...])
    out[...] = coded(total)
    peak[...] = jnp.broadcast_to(jnp.max(jnp.abs(total), keepdims=True), peak.shape)


def stats_kernel(
    width, scal, t_mine, t_direct, t_late, s_mine, s_direct, s_late, sampled, p0, p1, p2, p3,
    t_out, s_out, stats, square,
):
    t = t_mine[...] + decoded(t_direct[...]) + decoded(t_late[...])
    s = s_mine[...] + decoded(s_direct[...]) + decoded(s_late[...])
    t_out[...] = t
    s_out[...] = s
    column = iota(t.shape, 1)
    inside = column < width
    onehot = (column + scal[2] == sampled[:, 0:1].astype(jnp.int32)) & inside
    t_top = jnp.max(jnp.where(inside, t, -jnp.inf), axis=1, keepdims=True)
    s_top = jnp.max(jnp.where(inside, s, -jnp.inf), axis=1, keepdims=True)
    t_exp = jnp.where(inside, jnp.exp(t - t_top), 0.0)
    s_exp = jnp.where(inside, jnp.exp(s - s_top), 0.0)
    values = (
        t_top,
        s_top,
        jnp.sum(t_exp, axis=1, keepdims=True),
        jnp.sum(s_exp, axis=1, keepdims=True),
        jnp.sum(t_exp * (t - s), axis=1, keepdims=True),
        jnp.sum(jnp.where(onehot, s, 0.0), axis=1, keepdims=True),
    )
    lane = iota((GROUP, 128), 1)
    board = jnp.zeros((GROUP, 128), F32)
    for k, value in enumerate(values):
        board = jnp.where(lane == k, value, board)
    square[...] = jnp.zeros(square.shape, F32)
    square[:GROUP] = board
    flipped = square[...].T[:8]
    peak = jnp.maximum(jnp.maximum(p0[...], p1[...]), jnp.maximum(p2[...], p3[...]))
    stats[...] = jnp.where(iota((8, 128), 0) == 6, peak, flipped)


def grad_kernel(width, scal, every, t_ref, s_ref, sampled, total, left, right):
    e = every[...]
    most = jnp.max(e, axis=0)
    t_top, s_top, peak = most[0:1], most[1:2], most[6:7]
    t_scale = jnp.exp(e[:, 0:1] - t_top[None])
    s_scale = jnp.exp(e[:, 1:2] - s_top[None])
    t_total = jnp.sum(e[:, 2:3] * t_scale, axis=0)
    s_total = jnp.sum(e[:, 3:4] * s_scale, axis=0)
    cross = jnp.sum(e[:, 4:5] * t_scale, axis=0)
    picked = jnp.sum(e[:, 5:6], axis=0)
    t_lse = t_top + jnp.log(t_total)
    s_lse = s_top + jnp.log(s_total)
    per_row = cross / t_total - t_lse + 2.0 * s_lse - picked
    first = scal[0] * GROUP
    count = total[0:1, 0:1].astype(jnp.int32)
    lane = iota((1, 128), 1)
    live = (lane < GROUP) & (lane + first < count)
    part = jnp.sum(jnp.where(live, per_row, 0.0), axis=1, keepdims=True)
    line = iota((8, 128), 0)
    turned = jnp.where(line == 0, t_lse, s_lse).T
    t_col, s_col = turned[:GROUP, 0:1], turned[:GROUP, 1:2]
    t, s = t_ref[...], s_ref[...]
    column = iota(t.shape, 1)
    onehot = (column + scal[2] == sampled[:, 0:1].astype(jnp.int32)).astype(F32)
    grad = 2.0 * jnp.exp(s - s_col) - jnp.exp(t - t_col) - onehot
    keep = (column < width) & (iota(t.shape, 0) + first < count)
    grad = jnp.where(keep, grad, 0.0)
    left[...] = grad[:, :LEFT].astype(BF16)
    right[...] = grad[:, LEFT:].astype(BF16)
    spare = width - LEFT
    block = spare // 128 * 128
    line, lane = iota((16, 128), 0), iota((16, 128), 1) + block - spare
    tail = grad[:16, LEFT + block : LEFT + block + 128]
    for k, value in enumerate((part, jnp.max(peak, keepdims=True))):
        for piece in range(3):
            rounded = value.astype(BF16).astype(F32)
            tail = jnp.where((line == 0) & (lane == 3 * k + piece), rounded, tail)
            value = value - rounded
    right[:16, block : block + 128] = tail.astype(BF16)


def back_kernel(
    width, half, scal, a0, b0, a1, b1, a2, b2, a3, b3, total, back_own, back_other, head,
    mine, theirs, loss, fits, grads,
):
    full = padded(width)
    for k, (a, b) in enumerate(((a0, b0), (a1, b1), (a2, b2), (a3, b3))):
        grads[k * GROUP : (k + 1) * GROUP, :LEFT] = a[...]
        grads[k * GROUP : (k + 1) * GROUP, LEFT:full] = b[...]
    x = jnp.zeros((LIVE, 2 * half), F32)
    for start in range(0, width, BLOCK):
        stop = min(start + BLOCK, width)
        x += jnp.dot(grads[:, start:stop], head[start:stop], preferred_element_type=F32)
    high = x.astype(BF16)
    low = (x - high.astype(F32)).astype(BF16)
    for back, out in ((back_own, mine), (back_other, theirs)):
        y = jnp.zeros(out.shape, F32)
        for k in (0, 1):
            cut = slice(k * half, (k + 1) * half)
            y += jnp.dot(back[k], high[:, cut], preferred_element_type=F32)
            y += jnp.dot(back[k], low[:, cut], preferred_element_type=F32)
        out[...] = y
    spare = width - LEFT
    block = spare // 128 * 128
    line, lane = iota((16, 128), 0), iota((16, 128), 1) + block - spare
    parts, peaks = [], []
    for b in (b0, b1, b2, b3):
        tail = jnp.where(line == 0, b[:16, block : block + 128].astype(F32), 0.0)
        parts.append(jnp.sum(jnp.where((lane >= 0) & (lane < 3), tail, 0.0), keepdims=True))
        peaks.append(jnp.sum(jnp.where((lane >= 3) & (lane < 6), tail, 0.0), keepdims=True))
    count = total[0:1, 0:1]
    value = ((parts[0] + parts[2]) + (parts[1] + parts[3])) / count
    peak = jnp.maximum(jnp.maximum(peaks[0], peaks[1]), jnp.maximum(peaks[2], peaks[3]))
    good = jnp.where((count <= LIVE) & (peak < BOUND), 1.0, 0.0)
    loss[0, 0] = jnp.sum(value)
    fits[0, 0] = jnp.sum(good).astype(jnp.int32)


def hidden_grad(scal, pieces, total, backs, head_t):
    width, depth = head_t.shape
    outs = (struct((ROWS, depth // 2), F32),) * 2 + (
        struct((1, 1), F32),
        struct((1, 1), jnp.int32),
    )
    return call(
        functools.partial(back_kernel, width, depth // 2),
        outs, scal, *pieces, total, *backs, head_t,
        scratch=[pltpu.VMEM((LIVE, padded(width)), BF16)],
        scalars=2,
    )


def final_kernel(scal, got, out, square):
    total = jnp.sum(got[...], axis=0)
    half = total.shape[1]
    for row in range(4):
        for k in (0, 1):
            square[row : row + 1, k * half : (k + 1) * half] = total[2 * row + k : 2 * row + k + 1]
    out[...] = square[...].astype(BF16)


def pack_kernel(ids, valid, teacher, student, out):
    dt, ds = teacher.shape[1] // 2, student.shape[1] // 2
    line = iota((8, dt), 0)
    t = jnp.zeros((8, dt), F32)
    for row in range(4):
        for k in (0, 1):
            t = jnp.where(line == 2 * row + k, teacher[row : row + 1, k * dt : (k + 1) * dt].astype(F32), t)
    out[:, :, :dt] = jnp.broadcast_to(t.astype(BF16)[None], (32, 8, dt))
    line = iota((8, ds), 0)
    s = jnp.zeros((8, ds), F32)
    for row in range(4):
        for k in (0, 1):
            s = jnp.where(line == 2 * row + k, student[row : row + 1, k * ds : (k + 1) * ds].astype(F32), s)
    out[:, :, dt + 128 :] = jnp.broadcast_to(s.astype(BF16)[None], (32, 8, ds))
    line, lane = iota((8, 128), 0), iota((8, 128), 1)
    labels = jnp.zeros((8, 128), jnp.int32)
    for row in range(4):
        token = ids[row]
        for k, value in enumerate((token & 255, (token >> 8) & 255, token >> 16, valid[row])):
            labels = jnp.where((line == 2 * row) & (lane == k), value, labels)
    out[:, :, dt : dt + 128] = jnp.broadcast_to(labels.astype(F32).astype(BF16)[None], (32, 8, 128))


def hop(x, by):
    return lax.ppermute(x, "t", [(i, (i + by) % 4) for i in range(4)])


def swap_cores(x):
    return lax.ppermute(x, "c", [(0, 1), (1, 0)])


def spread(x, axes, n):
    return lax.all_to_all(
        jnp.broadcast_to(x[None], (n,) + x.shape), axes, split_axis=0, concat_axis=0, tiled=True
    )


def short_way(teacher_hidden, student_hidden, teacher_head, student_head, token_ids, valid):
    dt, ds = teacher_hidden.shape[1], student_hidden.shape[1]
    width = teacher_head.shape[1]
    full = padded(width)
    scal = jnp.stack(
        [lax.axis_index("t"), lax.axis_index("c"), lax.axis_index(VOCAB) * width]
    ).astype(jnp.int32)
    packed = pl.pallas_call(
        pack_kernel,
        out_shape=struct((32, 8, dt // 2 + 128 + ds // 2), BF16),
        in_specs=[SMEM, SMEM, VMEM, VMEM],
        out_specs=VMEM,
    )(token_ids, valid, teacher_hidden, student_hidden)
    own = lax.all_to_all(packed, CHIPS, split_axis=0, concat_axis=0, tiled=True)
    own = own.reshape(ROWS, packed.shape[2])
    other = swap_cores(own)
    pick_own, pick_other, back_own, back_other, sampled, total = call(
        functools.partial(order_kernel, dt // 2),
        (struct((2, LIVE, ROWS), BF16),) * 2
        + (struct((2, ROWS, LIVE), BF16),) * 2
        + (struct((GROUP, 128), F32), struct((8, 128), F32)),
        scal, own, other,
    )
    sums, peaks = [], []
    for head, at, near, relayed, by in (
        (teacher_head, 0, 3, 1, 1),
        (student_head, dt // 2 + 128, 1, 3, -1),
    ):
        first, direct, mine, held, peak = partial_logits(
            scal, (pick_own, pick_other), own, other, head.T, at, near, relayed
        )
        got = hop(first, by)
        late, late_peak = call(
            relay_kernel, (struct((GROUP, full), I16), struct((8, 128), F32)), scal, got, held
        )
        sums += [mine, hop(direct, -by), hop(late, by)]
        peaks += [peak, late_peak]
    t_logits, s_logits, stats = call(
        functools.partial(stats_kernel, width),
        (struct((GROUP, full), F32),) * 2 + (struct((8, 128), F32),),
        scal, *sums, sampled, *peaks,
        scratch=[pltpu.VMEM((128, 128), F32)],
    )
    every = spread(stats, VOCAB, 64)
    a0, b0 = call(
        functools.partial(grad_kernel, width),
        (struct((GROUP, LEFT), BF16), struct((GROUP, full - LEFT), BF16)),
        scal, every, t_logits, s_logits, sampled, total,
    )
    a3, b1 = hop(a0, 1), hop(b0, -1)
    b3, a1 = hop(b0, 1), hop(a0, -1)
    a2, b2 = hop(a3, 1), hop(b1, -1)
    mine, theirs, loss, fits = hidden_grad(
        scal, (a0, b0, a1, b1, a2, b2, a3, b3), total, (back_own, back_other), student_head.T
    )
    pair = (mine + swap_cores(theirs)).reshape(32, 8, ds // 2)
    got = lax.all_to_all(pair, CHIPS, split_axis=0, concat_axis=0, tiled=True)
    (grad,) = call(
        final_kernel, (struct((4, ds), BF16),), scal, got, scratch=[pltpu.VMEM((4, ds), F32)]
    )
    return loss.reshape(()), grad, fits.reshape(()) > 0


def long_way(teacher_hidden, student_hidden, teacher_head, student_head, token_ids, valid):
    ds = student_hidden.shape[1]
    width = teacher_head.shape[1]
    group = ROWS // 4
    labels = jnp.pad(jnp.stack([token_ids, valid]), ((0, 6), (0, 124)))
    labels = spread(labels, VOCAB, 64)[:, :2, :4].transpose(1, 0, 2).reshape(2, ROWS)

    def logits(hidden, head):
        rows = spread(hidden, VOCAB, 64).reshape(ROWS, hidden.shape[1])
        part = jnp.dot(rows, head, preferred_element_type=F32).reshape(4, group, width)
        return jnp.sum(lax.all_to_all(part, "t", split_axis=0, concat_axis=0, tiled=True), axis=0)

    teacher_logits = logits(teacher_hidden, teacher_head)
    student_logits = logits(student_hidden, student_head)
    here = lax.dynamic_slice_in_dim(labels, lax.axis_index("t") * group, group, 1)
    sampled, mask = here[0], here[1].astype(F32)
    columns = lax.axis_index(VOCAB) * width + jnp.arange(width, dtype=jnp.int32)
    onehot = columns[None, :] == sampled[:, None]
    t_top = jnp.max(teacher_logits, axis=1)
    s_top = jnp.max(student_logits, axis=1)
    t_exp = jnp.exp(teacher_logits - t_top[:, None])
    s_exp = jnp.exp(student_logits - s_top[:, None])
    stats = jnp.stack(
        [
            t_top,
            s_top,
            jnp.sum(t_exp, axis=1),
            jnp.sum(s_exp, axis=1),
            jnp.sum(t_exp * (teacher_logits - student_logits), axis=1),
            jnp.sum(jnp.where(onehot, student_logits, F32(0.0)), axis=1),
        ]
    )
    every = spread(jnp.pad(stats, ((0, 2), (0, 128 - group))), VOCAB, 64)[:, :, :group]
    teacher_top = jnp.max(every[:, 0], axis=0)
    student_top = jnp.max(every[:, 1], axis=0)
    t_scale = jnp.exp(every[:, 0] - teacher_top)
    s_scale = jnp.exp(every[:, 1] - student_top)
    teacher_total = jnp.sum(every[:, 2] * t_scale, axis=0)
    student_total = jnp.sum(every[:, 3] * s_scale, axis=0)
    cross_term = jnp.sum(every[:, 4] * t_scale, axis=0)
    picked = jnp.sum(every[:, 5], axis=0)
    teacher_lse = teacher_top + jnp.log(teacher_total)
    student_lse = student_top + jnp.log(student_total)
    per_row = cross_term / teacher_total - teacher_lse + 2.0 * student_lse - picked
    loss = lax.psum(jnp.sum(mask * per_row), "t") / jnp.sum(labels[1]).astype(F32)
    teacher_prob = jnp.exp(teacher_logits - teacher_lse[:, None])
    student_prob = jnp.exp(student_logits - student_lse[:, None])
    logit_grad = (
        mask[:, None] * (2.0 * student_prob - teacher_prob - onehot.astype(F32))
    ).astype(BF16)
    part = lax.dot_general(
        lax.all_gather(logit_grad, "t", axis=0, tiled=True), student_head, NT,
        preferred_element_type=F32,
    )
    got = lax.all_to_all(part.reshape(64, 4, ds), VOCAB, split_axis=0, concat_axis=0, tiled=True)
    return loss, jnp.sum(got, axis=0).astype(BF16)


def on_device(*args):
    loss, grad, fits = short_way(*args)
    return lax.cond(fits, lambda *_: (loss, grad), long_way, *args)


def solution(mesh):
    fine = Mesh(mesh.devices.reshape(4, 4, 2, 2, 4), VOCAB + ("t",))
    in_specs = (
        P(VOCAB, "t"),
        P(VOCAB, "t"),
        P("t", VOCAB),
        P("t", VOCAB),
        P(VOCAB),
        P(VOCAB),
    )
    return jax.shard_map(
        on_device, mesh=fine, in_specs=in_specs, out_specs=(P(), P(VOCAB, "t")), check_vma=False
    )
```

time: 436 us -> 420 us (0.963)
  starting transfers between devices: 80.6 us -> 54.1 us
  blocking collectives: 91 us -> 110 us
  local copies, waits for them, and re-layouts: 12.1 us -> 6.28 us
    all_to_all x0 -> x1, blocking collectives: none -> 21.7 us  [short_way(): own = lax.all_to_all(packed, CHIPS, split_axis=0, concat_axis=0, tiled=True)]
    all_to_all x3 -> x1, waiting for transfers between devices: 24.1 us -> 8.78 us  [spread(): lax.all_to_all(jnp.broadcast_to(x[None], (n,) + x.shape), axes, split_axi...]
    all_to_all x3 -> x1, starting transfers between devices: 17.6 us -> 4.54 us  [spread(): lax.all_to_all(jnp.broadcast_to(x[None], (n,) + x.shape), axes, split_axi...]
    pallas_call x3 -> x1, Pallas kernels: 14.2 us -> 1.63 us  [short_way(): pl.pallas_call(pack_kernel, out_shape=struct((32, 8, dt // 2 + 128 + ds /...]
    pallas_call x5 -> x9, Pallas kernels: 5.05 us -> 17.5 us  [call(): pl.pallas_call(body, out_shape=outs, in_specs=[SMEM] + [VMEM] * (len(args...]
    all_to_all x1, waiting for transfers between devices: 0.01 us -> 12.1 us  [short_way(): got = lax.all_to_all(pair, CHIPS, split_axis=0, concat_axis=0, tiled=True)]
    ppermute x17 -> x12, starting transfers between devices: 34.5 us -> 23.5 us  [hop(): return lax.ppermute(x, 't', [(i, (i + by) % 4) for i in range(4)])]
    ppermute x17 -> x12, waiting for transfers between devices: 30.2 us -> 32.6 us  [hop(): return lax.ppermute(x, 't', [(i, (i + by) % 4) for i in range(4)])]
  transfers between devices with their start and end apart: 28 -> 20, of which waited for: 16 -> 16; matrix products, arithmetic and copies ran while one was open for 4% -> 4% of each run, Pallas kernels for 3% -> 1%
where the time goes in v2:
time: 420 us; the launch traced here: 419 us
  waiting for transfers between devices  189 us (45%)
  blocking collectives  110 us (26%)
  starting transfers between devices  54.1 us (13%)
  Pallas kernels  19.1 us (5%)
  matrix products  16.7 us (4%)
  between operations  15.9 us (4%)
  other arithmetic  7.21 us (2%)
  local copies, waits for them, and re-layouts  6.28 us (1%)
    all_to_all x2, waiting for transfers between devices, logits(): lax.all_to_all(part, 't', split_axis=0, concat_axis=0, tiled=True)  98 us
    all_to_all x4, blocking collectives, spread(): lax.all_to_all(jnp.broadcast_to(x[None], (n,) + x.shape), axes, split_axi...  69.9 us
    all_gather x1, waiting for transfers between devices, long_way(): lax.all_gather(logit_grad, 't', axis=0, tiled=True)  32.8 us
    ppermute x12, waiting for transfers between devices, hop(): return lax.ppermute(x, 't', [(i, (i + by) % 4) for i in range(4)])  32.6 us
    ppermute x12, starting transfers between devices, hop(): return lax.ppermute(x, 't', [(i, (i + by) % 4) for i in range(4)])  23.5 us
    all_to_all x1, blocking collectives, short_way(): own = lax.all_to_all(packed, CHIPS, split_axis=0, concat_axis=0, tiled=True)  21.7 us
    psum x1, blocking collectives, long_way(): lax.psum(jnp.sum(mask * per_row), 't') / jnp.sum(labels[1]).astype(F32)  18.4 us
    pallas_call x9, Pallas kernels, call(): pl.pallas_call(body, out_shape=outs, in_specs=[SMEM] + [VMEM] * (len(args...  17.5 us
  transfers between devices with their start and end apart: 20, of which 16 were waited for; matrix products, arithmetic and copies ran while one was open for 4% of the time, Pallas kernels for 1%

profile of v2, /device:TPU:1, one launch (start us, length us, event | category | flops | bytes accessed | tf_op | source)
XLA Modules:
  0.0 419.3 jit_solution(3143444907942557402)
XLA Ops:
  8.8 21.7 %all_to_all.46 = bf16[32,8,1280]{2,1,0:T(8,128)(2,1)S(1)} all-to-all(bf16[32,8,1280]{2,1,0:T(8,128)(2,1)} %shard_map.81), channel_id=1, replica_groups=mesh['y'=4,'x'=4,'zl'=2,'c'=2,'t'=4] {'y','x','zl'}, dimensions={0} | all-to-all | bytes 1310720 | tf_op jit(solution)/shard_map/all_to_all | solution.py:331
  35.6 4.8 %shard_map.83 = (s16[48,2432]{1,0:T(8,128)(2,1)S(1)}, s16[48,2432]{1,0:T(8,128)(2,1)S(1)}, f32[48,2432]{1,0:T(8,128)S(1)}, f32[48,2432]{1,0:T(8,128)S(1)}, f32[8,128]{1,0:T(8,128)S(1)}) custom-call(s32[3]{0:T(128)S(1)} %pad_add_fusion.1.scal, bf16[2,192,256]{2,1,0:T(8,128)(2,1)S(1)} %get-tuple-element.58.pick_own, ...), custom_call_target="tpu_custom_call" | custom-call | tf_op jit(solution)/shard_map/pallas_call | solution.py:32
  51.0 4.5 %collective-permute-done.2.got = s16[48,2432]{1,0:T(8,128)(2,1)S(1)} collective-permute-done((s16[48,2432]{1,0:T(8,128)(2,1)S(1)}, s16[48,2432]{1,0:T(8,128)(2,1)S(1)}, u32[]{:S(2)}, u32[]{:S(2)}) %collective-permute-start.2) | collective-permute-done | bytes 233504 | tf_op jit(solution)/shard_map/ppermute | solution.py:305
  60.0 11.0 %collective-permute-done.5.got = s16[48,2432]{1,0:T(8,128)(2,1)S(1)} collective-permute-done((s16[48,2432]{1,0:T(8,128)(2,1)S(1)}, s16[48,2432]{1,0:T(8,128)(2,1)S(1)}, u32[]{:S(2)}, u32[]{:S(2)}) %collective-permute-start.5) | collective-permute-done | bytes 233504 | tf_op jit(solution)/shard_map/ppermute | solution.py:305
  81.9 16.1 %all_to_all.47.every = f32[64,8,128]{2,1,0:T(8,128)S(1)} all-to-all(f32[64,8,128]{2,1,0:T(8,128)S(1)} %broadcast_in_dim.13), channel_id=1, replica_groups=mesh['y'=4,'x'=4,'zl'=2,'c'=2,'t'=4] {'y','x','zl','c'}, dimensions={0} | all-to-all | bytes 524288 | tf_op jit(solution)/shard_map/all_to_all | solution.py:313
  103.3 4.6 %collective-permute-done.9.a3 = bf16[48,1280]{1,0:T(8,128)(2,1)S(1)} collective-permute-done((bf16[48,1280]{1,0:T(8,128)(2,1)S(1)}, bf16[48,1280]{1,0:T(8,128)(2,1)S(1)}, u32[]{:S(2)}, u32[]{:S(2)}) %collective-permute-start.9) | collective-permute-done | bytes 122912 | tf_op jit(solution)/shard_map/ppermute | solution.py:305
  114.3 5.0 %collective-permute-done.12.b3 = bf16[48,1152]{1,0:T(8,128)(2,1)S(1)} collective-permute-done((bf16[48,1152]{1,0:T(8,128)(2,1)S(1)}, bf16[48,1152]{1,0:T(8,128)(2,1)S(1)}, u32[]{:S(2)}, u32[]{:S(2)}) %collective-permute-start.12) | collective-permute-done | bytes 110624 | tf_op jit(solution)/shard_map/ppermute | solution.py:305
  126.2 5.7 %all-to-all-start.9 = ((f32[32,8,640]{2,1,0:T(8,128)}), f32[32,8,640]{2,1,0:T(8,128)S(1)}, u32[]{:S(2)}, u32[]{:S(2)}) async-start(f32[32,8,640]{2,1,0:T(8,128)} %add_bitcast_fusion), calls=%async_computation.9 | async-start | bytes 1310720 | tf_op jit(solution)/shard_map/all_to_all | solution.py:374
  132.6 12.1 %all-to-all-done.9.got = f32[32,8,640]{2,1,0:T(8,128)S(1)} async-done(((f32[32,8,640]{2,1,0:T(8,128)}), f32[32,8,640]{2,1,0:T(8,128)S(1)}, u32[]{:S(2)}, u32[]{:S(2)}) %all-to-all-start.9) | async-done | bytes 655392 | tf_op jit(solution)/shard_map/all_to_all | solution.py:374
  145.9 265.4 %conditional.1 = (f32[]{:T(128)}, bf16[4,1280]{1,0:T(4,128)(2,1)}) conditional(s32[]{:T(128)} %bitcast.26, (s32[4]{0:T(128)S(1)}, s32[4]{0:T(128)S(1)}, bf16[4,1024]{1,0:T(4,128)(2,1)S(1)}, bf16[1024,2374]{0,1:T(8,128)(2,1)}, bf16[4,1280]{1,0:T(4,128)(2,1)S(1)}, /*index=5*/bf16[1280,2374]{0,1:T(8,128)(2,1)}) %tuple.43, (f32[1,1]{1,0:T(1,128)}, ...), branch_computations={%region_0.19_spmd, %region_19.20_spmd} | conditional | flops 4360781312 | bytes 74072800 | solution.py:441
  146.0 15.5 %all_to_all.43 = s32[64,8,128]{2,1,0:T(8,128)S(1)} all-to-all(s32[64,8,128]{2,1,0:T(8,128)S(1)} %broadcast_in_dim.1), channel_id=1, replica_groups=mesh['y'=4,'x'=4,'zl'=2,'c'=2,'t'=4] {'y','x','zl','c'}, dimensions={0} | all-to-all | bytes 524288 | tf_op jit(solution)/shard_map/cond/branch_0_fun/all_to_all | solution.py:313
  161.6 16.9 %all_to_all.44 = bf16[64,4,1024]{2,1,0:T(4,128)(2,1)S(1)} all-to-all(bf16[64,4,1024]{2,1,0:T(4,128)(2,1)S(1)} %broadcast_in_dim.2), channel_id=1, replica_groups=mesh['y'=4,'x'=4,'zl'=2,'c'=2,'t'=4] {'y','x','zl','c'}, dimensions={0} | all-to-all | bytes 1048576 | tf_op jit(solution)/shard_map/cond/branch_0_fun/all_to_all | solution.py:313
  179.6 4.5 %all-to-all-start.3 = ((bf16[64,4,1280]{2,1,0:T(4,128)(2,1)}), bf16[64,4,1280]{2,1,0:T(4,128)(2,1)S(1)}, u32[]{:S(2)}, u32[]{:S(2)}) async-start(bf16[64,4,1280]{2,1,0:T(4,128)(2,1)} %broadcast_in_dim.3), calls=%async_computation.3 | async-start | bytes 1310720 | tf_op jit(solution)/shard_map/cond/branch_0_fun/all_to_all | solution.py:313
  184.3 5.4 %fusion.2 = f32[4,64,2374]{2,1,0:T(8,128)} fusion(bf16[4,64,1024]{2,1,0:T(8,128)(2,1)S(1)} %dot_general.1, bf16[1024,2374]{0,1:T(8,128)(2,1)} %get-tuple-element.22), kind=kOutput, calls=%fused_computation.2 | convolution fusion | flops 1244659712 | bytes 7817216 | tf_op jit(solution)/shard_map/cond/branch_0_fun/dot_general | solution.py:390
  189.6 8.8 %all-to-all-done.3 = bf16[64,4,1280]{2,1,0:T(4,128)(2,1)S(1)} async-done(((bf16[64,4,1280]{2,1,0:T(4,128)(2,1)}), bf16[64,4,1280]{2,1,0:T(4,128)(2,1)S(1)}, u32[]{:S(2)}, u32[]{:S(2)}) %all-to-all-start.3) | async-done | bytes 655392 | tf_op jit(solution)/shard_map/cond/branch_0_fun/all_to_all | solution.py:313
  205.7 6.3 %fusion = f32[4,64,2374]{2,1,0:T(8,128)} fusion(bf16[4,64,1280]{2,1,0:T(8,128)(2,1)} %dot_general.10, bf16[1280,2374]{0,1:T(8,128)(2,1)} %get-tuple-element.24), kind=kOutput, calls=%fused_computation | convolution fusion | flops 1555824640 | bytes 9163776 | tf_op jit(solution)/shard_map/cond/branch_0_fun/dot_general | solution.py:390
  212.0 47.9 %all-to-all-done.2 = f32[4,64,2374]{2,1,0:T(8,128)S(1)} async-done(((f32[4,64,2374]{2,1,0:T(8,128)}), f32[4,64,2374]{2,1,0:T(8,128)S(1)}, u32[]{:S(2)}, u32[]{:S(2)}) %all-to-all-start.2) | async-done | bytes 2431008 | tf_op jit(solution)/shard_map/cond/branch_0_fun/all_to_all | solution.py:391
  259.9 5.5 %all-to-all-start.4 = ((f32[4,64,2374]{2,1,0:T(8,128)}), f32[4,64,2374]{2,1,0:T(8,128)}, u32[]{:S(2)}, u32[]{:S(2)}) async-start(f32[4,64,2374]{2,1,0:T(8,128)} %fusion), calls=%async_computation.4 | async-start | bytes 4980736 | tf_op jit(solution)/shard_map/cond/branch_0_fun/all_to_all | solution.py:391
  265.9 50.2 %all-to-all-done.4 = f32[4,64,2374]{2,1,0:T(8,128)} async-done(((f32[4,64,2374]{2,1,0:T(8,128)}), f32[4,64,2374]{2,1,0:T(8,128)}, u32[]{:S(2)}, u32[]{:S(2)}) %all-to-all-start.4) | async-done | bytes 2431008 | tf_op jit(solution)/shard_map/cond/branch_0_fun/all_to_all | solution.py:391
  318.7 21.5 %all_to_all.45 = f32[64,8,128]{2,1,0:T(8,128)S(1)} all-to-all(f32[64,8,128]{2,1,0:T(8,128)S(1)} %broadcast_in_dim.5), channel_id=1, replica_groups=mesh['y'=4,'x'=4,'zl'=2,'c'=2,'t'=4] {'y','x','zl','c'}, dimensions={0} | all-to-all | bytes 524288 | tf_op jit(solution)/shard_map/cond/branch_0_fun/all_to_all | solution.py:313
  342.1 32.8 %all-gather.2.cloned.1.call-done = bf16[256,2374]{1,0:T(8,128)(2,1)} async-done(((bf16[64,2374]{1,0:T(8,128)(2,1)}), bf16[256,2374]{1,0:T(8,128)(2,1)}) %all-gather.2.cloned.1.call-update) | async-done | bytes 1215504 | tf_op jit(solution)/shard_map/cond/branch_0_fun/all_gather | solution.py:432
  374.9 5.0 %fusion.10 = f32[256,1280]{1,0:T(8,128)S(1)} fusion(bf16[256,2374]{1,0:T(8,128)(2,1)} %all-gather.2.cloned.1.call-done, bf16[1280,2374]{0,1:T(8,128)(2,1)} %get-tuple-element.24), kind=kOutput, calls=%fused_computation.31 | convolution fusion | flops 1555824640 | bytes 8603648 | tf_op jit(solution)/shard_map/cond/branch_0_fun/dot_general | solution.py:431
  381.4 7.9 %all-to-all-start.6 = ((f32[64,4,1280]{2,1,0:T(4,128)}), f32[64,4,1280]{2,1,0:T(4,128)S(1)}, u32[]{:S(2)}, u32[]{:S(2)}) async-start(f32[64,4,1280]{2,1,0:T(4,128)} %reshape.63), calls=%async_computation.6 | async-start | bytes 2621440 | tf_op jit(solution)/shard_map/cond/branch_0_fun/all_to_all | solution.py:435
  390.7 18.4 %psum.6 = f32[]{:T(128)} all-reduce(f32[]{:T(128)} %get-tuple-element.95), channel_id=1, replica_groups=mesh['y'=4,'x'=4,'zl'=2,'c'=2,'t'=4] {'t'}, use_global_device_ids=true, to_apply=%region_16.16 | all-reduce | flops 1 | bytes 8 | tf_op jit(solution)/shard_map/cond/branch_0_fun/psum | solution.py:425
  (83 shorter events, 70.0 us)
Async XLA Ops:
  30.5 3.8 collective-permute-start
  40.3 15.1 %collective-permute-start.2 = (s16[48,2432]{1,0:T(8,128)(2,1)S(1)}, s16[48,2432]{1,0:T(8,128)(2,1)S(1)}, u32[]{:S(2)}, u32[]{:S(2)}) collective-permute-start(s16[48,2432]{1,0:T(8,128)(2,1)S(1)} %get-tuple-element.62), channel_id=1, source_target_pairs={{0,1},{1,2},{2,3},{3,0},{4,5},{5,6},{6,7},{7,4},{8,9},{9,10},{10,1... | collective-permute-start | bytes 700424 | tf_op jit(solution)/shard_map/ppermute | solution.py:305
  46.4 24.6 %collective-permute-start.5 = (s16[48,2432]{1,0:T(8,128)(2,1)S(1)}, s16[48,2432]{1,0:T(8,128)(2,1)S(1)}, u32[]{:S(2)}, u32[]{:S(2)}) collective-permute-start(s16[48,2432]{1,0:T(8,128)(2,1)S(1)} %get-tuple-element.67), channel_id=1, source_target_pairs={{0,3},{1,0},{2,1},{3,2},{4,7},{5,4},{6,5},{7,6},{8,11},{9,8},{10,9... | collective-permute-start | bytes 700424 | tf_op jit(solution)/shard_map/ppermute | solution.py:305
  48.6 27.3 %collective-permute-start.1 = (s16[48,2432]{1,0:T(8,128)(2,1)S(1)}, s16[48,2432]{1,0:T(8,128)(2,1)S(1)}, u32[]{:S(2)}, u32[]{:S(2)}) collective-permute-start(s16[48,2432]{1,0:T(8,128)(2,1)S(1)} %get-tuple-element.61), channel_id=1, source_target_pairs={{0,3},{1,0},{2,1},{3,2},{4,7},{5,4},{6,5},{7,6},{8,11},{9,8},{10,9... | collective-permute-start | bytes 700424 | tf_op jit(solution)/shard_map/ppermute | solution.py:305
  50.9 25.0 %collective-permute-start.4 = (s16[48,2432]{1,0:T(8,128)(2,1)S(1)}, s16[48,2432]{1,0:T(8,128)(2,1)S(1)}, u32[]{:S(2)}, u32[]{:S(2)}) collective-permute-start(s16[48,2432]{1,0:T(8,128)(2,1)S(1)} %get-tuple-element.66), channel_id=1, source_target_pairs={{0,1},{1,2},{2,3},{3,0},{4,5},{5,6},{6,7},{7,4},{8,9},{9,10},{10,1... | collective-permute-start | bytes 700424 | tf_op jit(solution)/shard_map/ppermute | solution.py:305
  56.3 20.3 %collective-permute-start.3 = (s16[48,2432]{1,0:T(8,128)(2,1)S(1)}, s16[48,2432]{1,0:T(8,128)(2,1)S(1)}, u32[]{:S(2)}, u32[]{:S(2)}) collective-permute-start(s16[48,2432]{1,0:T(8,128)(2,1)S(1)} %get-tuple-element.64), channel_id=1, source_target_pairs={{0,1},{1,2},{2,3},{3,0},{4,5},{5,6},{6,7},{7,4},{8,9},{9,10},{10,1... | collective-permute-start | bytes 700424 | tf_op jit(solution)/shard_map/ppermute | solution.py:305
  71.7 8.9 %collective-permute-start.6 = (s16[48,2432]{1,0:T(8,128)(2,1)S(1)}, s16[48,2432]{1,0:T(8,128)(2,1)S(1)}, u32[]{:S(2)}, u32[]{:S(2)}) collective-permute-start(s16[48,2432]{1,0:T(8,128)(2,1)S(1)} %get-tuple-element.69), channel_id=1, source_target_pairs={{0,3},{1,0},{2,1},{3,2},{4,7},{5,4},{6,5},{7,6},{8,11},{9,8},{10,9... | collective-permute-start | bytes 700424 | tf_op jit(solution)/shard_map/ppermute | solution.py:305
  99.0 9.0 %collective-permute-start.9 = (bf16[48,1280]{1,0:T(8,128)(2,1)S(1)}, bf16[48,1280]{1,0:T(8,128)(2,1)S(1)}, u32[]{:S(2)}, u32[]{:S(2)}) collective-permute-start(bf16[48,1280]{1,0:T(8,128)(2,1)S(1)} %get-tuple-element.79.a0), channel_id=1, source_target_pairs={{0,1},{1,2},{2,3},{3,0},{4,5},{5,6},{6,7},{7,4},{8,9},{9,10},{10,1... | collective-permute-start | bytes 368648 | tf_op jit(solution)/shard_map/ppermute | solution.py:305
  101.4 10.1 %collective-permute-start.8 = (bf16[48,1152]{1,0:T(8,128)(2,1)S(1)}, bf16[48,1152]{1,0:T(8,128)(2,1)S(1)}, u32[]{:S(2)}, u32[]{:S(2)}) collective-permute-start(bf16[48,1152]{1,0:T(8,128)(2,1)S(1)} %get-tuple-element.80.b0), channel_id=1, source_target_pairs={{0,3},{1,0},{2,1},{3,2},{4,7},{5,4},{6,5},{7,6},{8,11},{9,8},{10,9... | collective-permute-start | bytes 331784 | tf_op jit(solution)/shard_map/ppermute | solution.py:305
  102.8 16.5 %collective-permute-start.7 = (bf16[48,1280]{1,0:T(8,128)(2,1)S(1)}, bf16[48,1280]{1,0:T(8,128)(2,1)S(1)}, u32[]{:S(2)}, u32[]{:S(2)}) collective-permute-start(bf16[48,1280]{1,0:T(8,128)(2,1)S(1)} %get-tuple-element.79.a0), channel_id=1, source_target_pairs={{0,3},{1,0},{2,1},{3,2},{4,7},{5,4},{6,5},{7,6},{8,11},{9,8},{10,9... | collective-permute-start | bytes 368648 | tf_op jit(solution)/shard_map/ppermute | solution.py:305
  108.0 11.3 %collective-permute-start.10 = (bf16[48,1280]{1,0:T(8,128)(2,1)S(1)}, bf16[48,1280]{1,0:T(8,128)(2,1)S(1)}, u32[]{:S(2)}, u32[]{:S(2)}) collective-permute-start(bf16[48,1280]{1,0:T(8,128)(2,1)S(1)} %collective-permute-done.9.a3), channel_id=1, source_target_pairs={{0,1},{1,2},{2,3},{3,0},{4,5},{5,6},{6,7},{7,4},{8,9},{9,10},{10,1... | collective-permute-start | bytes 368648 | tf_op jit(solution)/shard_map/ppermute | solution.py:305
  109.8 9.5 %collective-permute-start.12 = (bf16[48,1152]{1,0:T(8,128)(2,1)S(1)}, bf16[48,1152]{1,0:T(8,128)(2,1)S(1)}, u32[]{:S(2)}, u32[]{:S(2)}) collective-permute-start(bf16[48,1152]{1,0:T(8,128)(2,1)S(1)} %get-tuple-element.80.b0), channel_id=1, source_target_pairs={{0,1},{1,2},{2,3},{3,0},{4,5},{5,6},{6,7},{7,4},{8,9},{9,10},{10,1... | collective-permute-start | bytes 331784 | tf_op jit(solution)/shard_map/ppermute | solution.py:305
  111.5 7.8 %collective-permute-start.11 = (bf16[48,1152]{1,0:T(8,128)(2,1)S(1)}, bf16[48,1152]{1,0:T(8,128)(2,1)S(1)}, u32[]{:S(2)}, u32[]{:S(2)}) collective-permute-start(bf16[48,1152]{1,0:T(8,128)(2,1)S(1)} %collective-permute-done.8.b1), channel_id=1, source_target_pairs={{0,3},{1,0},{2,1},{3,2},{4,7},{5,4},{6,5},{7,6},{8,11},{9,8},{10,9... | collective-permute-start | bytes 331784 | tf_op jit(solution)/shard_map/ppermute | solution.py:305
  122.9 23.0 %copy-start.2 = (bf16[4,1280]{1,0:T(4,128)(2,1)S(1)}, bf16[4,1280]{1,0:T(4,128)(2,1)}, u32[]{:S(2)}) copy-start(bf16[4,1280]{1,0:T(4,128)(2,1)} %student.1) | copy-start | bytes 30724
  122.9 23.0 %copy-start.3 = (bf16[4,1024]{1,0:T(4,128)(2,1)S(1)}, bf16[4,1024]{1,0:T(4,128)(2,1)}, u32[]{:S(2)}) copy-start(bf16[4,1024]{1,0:T(4,128)(2,1)} %teacher.1) | copy-start | bytes 24580
  122.9 23.0 %copy-start.4 = (s32[4]{0:T(128)S(1)}, s32[4]{0:T(128)}, u32[]{:S(2)}) copy-start(s32[4]{0:T(128)} %ids.1) | copy-start | bytes 52
  123.0 23.0 %copy-start.5 = (s32[4]{0:T(128)S(1)}, s32[4]{0:T(128)}, u32[]{:S(2)}) copy-start(s32[4]{0:T(128)} %valid.1) | copy-start | bytes 52
  123.0 2.3 collective-permute-start.13
  126.2 18.5 %all-to-all-start.9 = ((f32[32,8,640]{2,1,0:T(8,128)}), f32[32,8,640]{2,1,0:T(8,128)S(1)}, u32[]{:S(2)}, u32[]{:S(2)}) async-start(f32[32,8,640]{2,1,0:T(8,128)} %add_bitcast_fusion), calls=%async_computation.9 | async-start | bytes 1310720 | tf_op jit(solution)/shard_map/all_to_all | solution.py:374
  179.6 18.8 %all-to-all-start.3 = ((bf16[64,4,1280]{2,1,0:T(4,128)(2,1)}), bf16[64,4,1280]{2,1,0:T(4,128)(2,1)S(1)}, u32[]{:S(2)}, u32[]{:S(2)}) async-start(bf16[64,4,1280]{2,1,0:T(4,128)(2,1)} %broadcast_in_dim.3), calls=%async_computation.3 | async-start | bytes 1310720 | tf_op jit(solution)/shard_map/cond/branch_0_fun/all_to_all | solution.py:313
  199.3 60.6 %all-to-all-start.2 = ((f32[4,64,2374]{2,1,0:T(8,128)}), f32[4,64,2374]{2,1,0:T(8,128)S(1)}, u32[]{:S(2)}, u32[]{:S(2)}) async-start(f32[4,64,2374]{2,1,0:T(8,128)} %fusion.2), calls=%async_computation.2 | async-start | bytes 4980736 | tf_op jit(solution)/shard_map/cond/branch_0_fun/all_to_all | solution.py:391
  259.9 56.2 %all-to-all-start.4 = ((f32[4,64,2374]{2,1,0:T(8,128)}), f32[4,64,2374]{2,1,0:T(8,128)}, u32[]{:S(2)}, u32[]{:S(2)}) async-start(f32[4,64,2374]{2,1,0:T(8,128)} %fusion), calls=%async_computation.4 | async-start | bytes 4980736 | tf_op jit(solution)/shard_map/cond/branch_0_fun/all_to_all | solution.py:391
  265.4 109.6 %all-gather.2.cloned.1.call-start = ((), (), s32[]{:S(2)}) async-start(), calls=%async_computation.10 | async-start | bytes 1556480 | tf_op jit(solution)/shard_map/cond/branch_0_fun/all_gather | solution.py:432
  381.4 29.2 %all-to-all-start.6 = ((f32[64,4,1280]{2,1,0:T(4,128)}), f32[64,4,1280]{2,1,0:T(4,128)S(1)}, u32[]{:S(2)}, u32[]{:S(2)}) async-start(f32[64,4,1280]{2,1,0:T(4,128)} %reshape.63), calls=%async_computation.6 | async-start | bytes 2621440 | tf_op jit(solution)/shard_map/cond/branch_0_fun/all_to_all | solution.py:435
  (2 other events, 8.7 us)
Sparse Core Ops, SparseCore 0:
  342.3 32.6 all-gather.1

commit v3 on v2

--- a/solution.py
+++ b/solution.py
@@ -22,17 +22,18 @@
 NT = (((1,), (1,)), ((), ()))
 VMEM = pl.BlockSpec(memory_space=pltpu.VMEM)
 SMEM = pl.BlockSpec(memory_space=pltpu.SMEM)
+ANY = pl.BlockSpec(memory_space=pl.ANY)
 
 
 def struct(shape, dtype):
     return jax.ShapeDtypeStruct(shape, dtype)
 
 
-def call(body, outs, *args, scratch=(), scalars=0):
+def call(body, outs, *args, scratch=(), scalars=0, streamed=0):
     return pl.pallas_call(
         body,
         out_shape=outs,
-        in_specs=[SMEM] + [VMEM] * (len(args) - 1),
+        in_specs=[SMEM] + [VMEM] * (len(args) - 1 - streamed) + [ANY] * streamed,
         out_specs=[VMEM] * (len(outs) - scalars) + [SMEM] * scalars,
         scratch_shapes=scratch,
         compiler_params=pltpu.CompilerParams(vmem_limit_bytes=32 << 20),
@@ -55,7 +56,7 @@
     return lax.broadcasted_iota(jnp.int32, shape, axis)
 
 
-def order_kernel(at, scal, own, other, pick_own, pick_other, back_own, back_other, sampled, total):
+def order(scal, own, other, at, pick_own, pick_other, back_own, back_other, sampled, total):
     me, core = scal[0], scal[1].astype(F32)
     wide = own.shape[0]
     line, lane = iota((wide, wide), 0), iota((wide, wide), 1)
@@ -95,46 +96,55 @@
     total[...] = jnp.broadcast_to(found[0][3] + found[1][3], total.shape)
 
 
-def logits_kernel(
-    width, half, at, far, near, relayed, scal, pick_own, pick_other, own, other, head,
-    first, direct, mine, held, peak, rows, logits,
+def front_kernel(
+    width, places, scal, own, other, t_head, s_head,
+    back_own, back_other, sampled, total,
+    t_first, t_direct, t_mine, t_held, t_peak, s_first, s_direct, s_mine, s_held, s_peak,
+    pick_own, pick_other, t_rows, s_rows, t_loaded, s_loaded, logits, sems,
 ):
-    for k in (0, 1):
-        rows[:, k * half : (k + 1) * half] = (
-            jnp.dot(pick_own[k], own[:, at : at + half], preferred_element_type=F32)
-            + jnp.dot(pick_other[k], other[:, at : at + half], preferred_element_type=F32)
-        ).astype(BF16)
     full = padded(width)
     edge = full - 128
+    g = GROUP
+    blocks = [(start, min(start + BLOCK, width)) for start in range(0, width, BLOCK)]
+    copies = [
+        [
+            pltpu.make_async_copy(
+                head.at[start:stop], loaded.at[start:stop], sems.at[k * len(blocks) + n]
+            )
+            for n, (start, stop) in enumerate(blocks)
+        ]
+        for k, (head, loaded) in enumerate(((t_head, t_loaded), (s_head, s_loaded)))
+    ]
+    for copy in copies[0] + copies[1]:
+        copy.start()
+    order(
+        scal, own, other, t_rows.shape[1] // 2,
+        pick_own, pick_other, back_own, back_other, sampled, total,
+    )
     logits[:, edge:full] = jnp.zeros((LIVE, 128), F32)
-    for start in range(0, width, BLOCK):
-        stop = min(start + BLOCK, width)
-        logits[:, start:stop] = lax.dot_general(
-            rows[...], head[start:stop], NT, preferred_element_type=F32
-        )
-    g = GROUP
-    first[...] = coded(logits[far * g : (far + 1) * g])
-    direct[...] = coded(logits[near * g : (near + 1) * g])
-    mine[...] = logits[:g]
-    held[...] = logits[relayed * g : (relayed + 1) * g]
-    peak[...] = jnp.broadcast_to(jnp.max(jnp.abs(logits[g:]), keepdims=True), peak.shape)
-
-
-def partial_logits(scal, picks, own, other, head_t, at, near, relayed):
-    width, depth = head_t.shape
-    full = padded(width)
-    outs = (
-        struct((GROUP, full), I16),
-        struct((GROUP, full), I16),
-        struct((GROUP, full), F32),
-        struct((GROUP, full), F32),
-        struct((8, 128), F32),
-    )
-    return call(
-        functools.partial(logits_kernel, width, depth // 2, at, 2, near, relayed),
-        outs, scal, *picks, own, other, head_t,
-        scratch=[pltpu.VMEM((LIVE, depth), BF16), pltpu.VMEM((LIVE, full), F32)],
-    )
+    for (at, near, relayed), waits, rows, loaded, (first, direct, mine, held, peak) in zip(
+        places,
+        copies,
+        (t_rows, s_rows),
+        (t_loaded, s_loaded),
+        ((t_first, t_direct, t_mine, t_held, t_peak), (s_first, s_direct, s_mine, s_held, s_peak)),
+    ):
+        half = rows.shape[1] // 2
+        for k in (0, 1):
+            rows[:, k * half : (k + 1) * half] = (
+                jnp.dot(pick_own[k], own[:, at : at + half], preferred_element_type=F32)
+                + jnp.dot(pick_other[k], other[:, at : at + half], preferred_element_type=F32)
+            ).astype(BF16)
+        for (start, stop), wait in zip(blocks, waits):
+            wait.wait()
+            logits[:, start:stop] = lax.dot_general(
+                rows[...], loaded[start:stop], NT, preferred_element_type=F32
+            )
+        first[...] = coded(logits[2 * g : 3 * g])
+        direct[...] = coded(logits[near * g : (near + 1) * g])
+        mine[...] = logits[:g]
+        held[...] = logits[relayed * g : (relayed + 1) * g]
+        peak[...] = jnp.broadcast_to(jnp.max(jnp.abs(logits[g:]), keepdims=True), peak.shape)
 
 
 def relay_kernel(scal, got, held, out, peak):
@@ -206,26 +216,24 @@
     grad = jnp.where(keep, grad, 0.0)
     left[...] = grad[:, :LEFT].astype(BF16)
     right[...] = grad[:, LEFT:].astype(BF16)
-    spare = width - LEFT
-    block = spare // 128 * 128
-    line, lane = iota((16, 128), 0), iota((16, 128), 1) + block - spare
-    tail = grad[:16, LEFT + block : LEFT + block + 128]
+    block = width // 128 * 128
+    line, lane = iota((16, 128), 0), iota((16, 128), 1) + block - width
+    tail = grad[:16, block : block + 128]
     for k, value in enumerate((part, jnp.max(peak, keepdims=True))):
         for piece in range(3):
             rounded = value.astype(BF16).astype(F32)
             tail = jnp.where((line == 0) & (lane == 3 * k + piece), rounded, tail)
             value = value - rounded
-    right[:16, block : block + 128] = tail.astype(BF16)
+    right[:16, block - LEFT : block - LEFT + 128] = tail.astype(BF16)
 
 
 def back_kernel(
     width, half, scal, a0, b0, a1, b1, a2, b2, a3, b3, total, back_own, back_other, head,
     mine, theirs, loss, fits, grads,
 ):
-    full = padded(width)
     for k, (a, b) in enumerate(((a0, b0), (a1, b1), (a2, b2), (a3, b3))):
         grads[k * GROUP : (k + 1) * GROUP, :LEFT] = a[...]
-        grads[k * GROUP : (k + 1) * GROUP, LEFT:full] = b[...]
+        grads[k * GROUP : (k + 1) * GROUP, LEFT:] = b[...]
     x = jnp.zeros((LIVE, 2 * half), F32)
     for start in range(0, width, BLOCK):
         stop = min(start + BLOCK, width)
@@ -239,12 +247,12 @@
             y += jnp.dot(back[k], high[:, cut], preferred_element_type=F32)
             y += jnp.dot(back[k], low[:, cut], preferred_element_type=F32)
         out[...] = y
-    spare = width - LEFT
-    block = spare // 128 * 128
-    line, lane = iota((16, 128), 0), iota((16, 128), 1) + block - spare
+    block = width // 128 * 128
+    line, lane = iota((16, 128), 0), iota((16, 128), 1) + block - width
+    block -= LEFT
     parts, peaks = [], []
-    for b in (b0, b1, b2, b3):
-        tail = jnp.where(line == 0, b[:16, block : block + 128].astype(F32), 0.0)
+    for ref in (b0, b1, b2, b3):
+        tail = jnp.where(line == 0, ref[:16, block : block + 128].astype(F32), 0.0)
         parts.append(jnp.sum(jnp.where((lane >= 0) & (lane < 3), tail, 0.0), keepdims=True))
         peaks.append(jnp.sum(jnp.where((lane >= 3) & (lane < 6), tail, 0.0), keepdims=True))
     count = total[0:1, 0:1]
@@ -255,23 +263,40 @@
     fits[0, 0] = jnp.sum(good).astype(jnp.int32)
 
 
-def hidden_grad(scal, pieces, total, backs, head_t):
+def hidden_grad(scal, a0, b0, total, backs, head_t):
     width, depth = head_t.shape
+    full = padded(width)
+    a3, b1 = hop(a0, 1), hop(b0, -1)
+    b3, a1 = hop(b0, 1), hop(a0, -1)
+    a2, b2 = hop(a3, 1), hop(b1, -1)
     outs = (struct((ROWS, depth // 2), F32),) * 2 + (
         struct((1, 1), F32),
         struct((1, 1), jnp.int32),
     )
     return call(
         functools.partial(back_kernel, width, depth // 2),
-        outs, scal, *pieces, total, *backs, head_t,
-        scratch=[pltpu.VMEM((LIVE, padded(width)), BF16)],
+        outs, scal, a0, b0, a1, b1, a2, b2, a3, b3, total, *backs, head_t,
+        scratch=[pltpu.VMEM((LIVE, full), BF16)],
         scalars=2,
     )
 
 
+def pair_kernel(scal, mine, theirs, out):
+    x = mine[...] + theirs[...]
+    top = jnp.maximum(jnp.max(jnp.abs(x), axis=1, keepdims=True), 1e-30)
+    power = jnp.ceil(jnp.log2(top) + 0.001)
+    codes = jnp.round(x * jnp.exp2(15.0 - power))
+    half = x.shape[1]
+    out[:, :half] = jnp.clip(codes, -32767.0, 32767.0).astype(jnp.int32).astype(I16)
+    out[:, half:] = jnp.broadcast_to(power, (x.shape[0], 128)).astype(jnp.int32).astype(I16)
+
+
 def final_kernel(scal, got, out, square):
-    total = jnp.sum(got[...], axis=0)
-    half = total.shape[1]
+    half = got.shape[2] - 128
+    total = jnp.zeros((8, half), F32)
+    for chip in range(got.shape[0]):
+        power = got[chip, :, half : half + 128].astype(jnp.int32).astype(F32)[:, 0:1]
+        total += got[chip, :, :half].astype(jnp.int32).astype(F32) * jnp.exp2(power - 15.0)
     for row in range(4):
         for k in (0, 1):
             square[row : row + 1, k * half : (k + 1) * half] = total[2 * row + k : 2 * row + k + 1]
@@ -327,28 +352,43 @@
         out_shape=struct((32, 8, dt // 2 + 128 + ds // 2), BF16),
         in_specs=[SMEM, SMEM, VMEM, VMEM],
         out_specs=VMEM,
+        compiler_params=pltpu.CompilerParams(vmem_limit_bytes=8 << 20),
     )(token_ids, valid, teacher_hidden, student_hidden)
+    t_head, s_head = teacher_head.T, student_head.T
     own = lax.all_to_all(packed, CHIPS, split_axis=0, concat_axis=0, tiled=True)
     own = own.reshape(ROWS, packed.shape[2])
     other = swap_cores(own)
-    pick_own, pick_other, back_own, back_other, sampled, total = call(
-        functools.partial(order_kernel, dt // 2),
-        (struct((2, LIVE, ROWS), BF16),) * 2
-        + (struct((2, ROWS, LIVE), BF16),) * 2
-        + (struct((GROUP, 128), F32), struct((8, 128), F32)),
-        scal, own, other,
+    one = (
+        struct((GROUP, full), I16),
+        struct((GROUP, full), I16),
+        struct((GROUP, full), F32),
+        struct((GROUP, full), F32),
+        struct((8, 128), F32),
+    )
+    back_own, back_other, sampled, total, *made = call(
+        functools.partial(front_kernel, width, ((0, 3, 1), (dt // 2 + 128, 1, 3))),
+        (struct((2, ROWS, LIVE), BF16),) * 2
+        + (struct((GROUP, 128), F32), struct((8, 128), F32))
+        + one + one,
+        scal, own, other, t_head, s_head,
+        scratch=[
+            pltpu.VMEM((2, LIVE, ROWS), BF16),
+            pltpu.VMEM((2, LIVE, ROWS), BF16),
+            pltpu.VMEM((LIVE, dt), BF16),
+            pltpu.VMEM((LIVE, ds), BF16),
+            pltpu.VMEM(t_head.shape, BF16),
+            pltpu.VMEM(s_head.shape, BF16),
+            pltpu.VMEM((LIVE, full), F32),
+            pltpu.SemaphoreType.DMA((2 * pl.cdiv(width, BLOCK),)),
+        ],
+        streamed=2,
     )
     sums, peaks = [], []
-    for head, at, near, relayed, by in (
-        (teacher_head, 0, 3, 1, 1),
-        (student_head, dt // 2 + 128, 1, 3, -1),
-    ):
-        first, direct, mine, held, peak = partial_logits(
-            scal, (pick_own, pick_other), own, other, head.T, at, near, relayed
-        )
-        got = hop(first, by)
+    for (first, direct, mine, held, peak), by in ((made[:5], 1), (made[5:], -1)):
         late, late_peak = call(
-            relay_kernel, (struct((GROUP, full), I16), struct((8, 128), F32)), scal, got, held
+            relay_kernel,
+            (struct((GROUP, full), I16), struct((8, 128), F32)),
+            scal, hop(first, by), held,
         )
         sums += [mine, hop(direct, -by), hop(late, by)]
         peaks += [peak, late_peak]
@@ -364,13 +404,13 @@
         (struct((GROUP, LEFT), BF16), struct((GROUP, full - LEFT), BF16)),
         scal, every, t_logits, s_logits, sampled, total,
     )
-    a3, b1 = hop(a0, 1), hop(b0, -1)
-    b3, a1 = hop(b0, 1), hop(a0, -1)
-    a2, b2 = hop(a3, 1), hop(b1, -1)
     mine, theirs, loss, fits = hidden_grad(
-        scal, (a0, b0, a1, b1, a2, b2, a3, b3), total, (back_own, back_other), student_head.T
-    )
-    pair = (mine + swap_cores(theirs)).reshape(32, 8, ds // 2)
+        scal, a0, b0, total, (back_own, back_other), s_head
+    )
+    (pair,) = call(
+        pair_kernel, (struct((ROWS, ds // 2 + 128), I16),), scal, mine, swap_cores(theirs)
+    )
+    pair = pair.reshape(32, 8, ds // 2 + 128)
     got = lax.all_to_all(pair, CHIPS, split_axis=0, concat_axis=0, tiled=True)
     (grad,) = call(
         final_kernel, (struct((4, ds), BF16),), scal, got, scratch=[pltpu.VMEM((4, ds), F32)]
@@ -422,14 +462,15 @@
     teacher_lse = teacher_top + jnp.log(teacher_total)
     student_lse = student_top + jnp.log(student_total)
     per_row = cross_term / teacher_total - teacher_lse + 2.0 * student_lse - picked
-    loss = lax.psum(jnp.sum(mask * per_row), "t") / jnp.sum(labels[1]).astype(F32)
+    parts = spread(jnp.full((8, 128), jnp.sum(mask * per_row)), "t", 4)[:, 0, 0]
+    loss = jnp.sum(parts) / jnp.sum(labels[1]).astype(F32)
     teacher_prob = jnp.exp(teacher_logits - teacher_lse[:, None])
     student_prob = jnp.exp(student_logits - student_lse[:, None])
     logit_grad = (
         mask[:, None] * (2.0 * student_prob - teacher_prob - onehot.astype(F32))
     ).astype(BF16)
     part = lax.dot_general(
-        lax.all_gather(logit_grad, "t", axis=0, tiled=True), student_head, NT,
+        spread(logit_grad, "t", 4).reshape(ROWS, width), student_head, NT,
         preferred_element_type=F32,
     )
     got = lax.all_to_all(part.reshape(64, 4, ds), VOCAB, split_axis=0, concat_axis=0, tiled=True)

time: 420 us -> 409 us (0.974)
  waiting for transfers between devices: 189 us -> 168 us
  blocking collectives: 110 us -> 128 us
  between operations: 15.9 us -> 2.56 us
    all_to_all x4 -> x5, blocking collectives: 69.9 us -> 106 us  [spread(): lax.all_to_all(jnp.broadcast_to(x[None], (n,) + x.shape), axes, split_axi...]
    all_gather x1 -> x0, waiting for transfers between devices: 32.8 us -> none  [long_way(): lax.all_gather(logit_grad, 't', axis=0, tiled=True)]
    psum x1 -> x0, blocking collectives: 18.4 us -> none  [long_way(): lax.psum(jnp.sum(mask * per_row), 't') / jnp.sum(labels[1]).astype(F32)]
    all_to_all x1, waiting for transfers between devices: 0.84 us -> 18.5 us  [long_way(): lax.all_to_all(part.reshape(64, 4, ds), VOCAB, split_axis=0, concat_axis=...]
    all_to_all x1 -> x2, starting transfers between devices: 4.54 us -> 8.47 us  [spread(): lax.all_to_all(jnp.broadcast_to(x[None], (n,) + x.shape), axes, split_axi...]
    pallas_call x9 -> x8, Pallas kernels: 17.5 us -> 18.6 us  [call(): pl.pallas_call(body, out_shape=outs, in_specs=[SMEM] + [VMEM] * (len(args...]
    all_to_all x1 -> x2, waiting for transfers between devices: 8.78 us -> 8.77 us  [spread(): lax.all_to_all(jnp.broadcast_to(x[None], (n,) + x.shape), axes, split_axi...]
  transfers between devices with their start and end apart: 20 -> 20, of which waited for: 16 -> 15; matrix products, arithmetic and copies ran while one was open for 4% -> 6% of each run, Pallas kernels for 1% -> 0%
where the time goes in v3:
time: 409 us; the launch traced here: 408 us
  waiting for transfers between devices  168 us (41%)
  blocking collectives  128 us (31%)
  starting transfers between devices  57.6 us (14%)
  Pallas kernels  19.4 us (5%)
  matrix products  16.3 us (4%)
  local copies, waits for them, and re-layouts  8.44 us (2%)
  other arithmetic  6.3 us (2%)
    all_to_all x5, blocking collectives, spread(): lax.all_to_all(jnp.broadcast_to(x[None], (n,) + x.shape), axes, split_axi...  106 us
    all_to_all x2, waiting for transfers between devices, logits(): lax.all_to_all(part, 't', split_axis=0, concat_axis=0, tiled=True)  98.2 us
    ppermute x12, waiting for transfers between devices, hop(): return lax.ppermute(x, 't', [(i, (i + by) % 4) for i in range(4)])  30.3 us
    ppermute x12, starting transfers between devices, hop(): return lax.ppermute(x, 't', [(i, (i + by) % 4) for i in range(4)])  24 us
    all_to_all x1, blocking collectives, short_way(): own = lax.all_to_all(packed, CHIPS, split_axis=0, concat_axis=0, tiled=True)  21.5 us
    pallas_call x8, Pallas kernels, call(): pl.pallas_call(body, out_shape=outs, in_specs=[SMEM] + [VMEM] * (len(args...  18.6 us
    all_to_all x1, waiting for transfers between devices, long_way(): lax.all_to_all(part.reshape(64, 4, ds), VOCAB, split_axis=0, concat_axis=...  18.5 us
    dot_general x2, matrix products, logits(): jnp.dot(rows, head, preferred_element_type=F32).reshape(4, group, width)  11.7 us
  transfers between devices with their start and end apart: 20, of which 15 were waited for; matrix products, arithmetic and copies ran while one was open for 6% of the time, Pallas kernels for 0%

profile of v3, /device:TPU:1, one launch (start us, length us, event | category | flops | bytes accessed | tf_op | source)
XLA Modules:
  0.0 408.2 jit_solution(3393407023760486632)
XLA Ops:
  1.4 21.5 %all_to_all.55 = bf16[32,8,1280]{2,1,0:T(8,128)(2,1)S(1)} all-to-all(bf16[32,8,1280]{2,1,0:T(8,128)(2,1)S(1)} %shard_map.81), channel_id=1, replica_groups=mesh['y'=4,'x'=4,'zl'=2,'c'=2,'t'=4] {'y','x','zl'}, dimensions={0} | all-to-all | bytes 1310720 | tf_op jit(solution)/shard_map/all_to_all | solution.py:358
  26.8 8.4 %shard_map.82 = (bf16[2,256,192]{2,1,0:T(8,128)(2,1)S(1)}, bf16[2,256,192]{2,1,0:T(8,128)(2,1)S(1)}, f32[48,128]{1,0:T(8,128)S(1)}, f32[8,128]{1,0:T(8,128)S(1)}...) custom-call(s32[3]{0:T(128)S(1)} %pad_add_fusion.1.scal, ...), custom_call_target="tpu_custom_call" | custom-call | tf_op jit(solution)/shard_map/pallas_call | solution.py:33
  42.8 7.5 %collective-permute-done.2.got = s16[48,2432]{1,0:T(8,128)(2,1)S(1)} collective-permute-done((s16[48,2432]{1,0:T(8,128)(2,1)S(1)}, s16[48,2432]{1,0:T(8,128)(2,1)S(1)}, u32[]{:S(2)}, u32[]{:S(2)}) %collective-permute-start.2) | collective-permute-done | bytes 233504 | tf_op jit(solution)/shard_map/ppermute | solution.py:330
  63.8 7.6 %collective-permute-done.3.t_late = s16[48,2432]{1,0:T(8,128)(2,1)S(1)} collective-permute-done((s16[48,2432]{1,0:T(8,128)(2,1)S(1)}, s16[48,2432]{1,0:T(8,128)(2,1)S(1)}, u32[]{:S(2)}, u32[]{:S(2)}) %collective-permute-start.3) | collective-permute-done | bytes 233504 | tf_op jit(solution)/shard_map/ppermute | solution.py:330
  72.6 18.0 %all_to_all.56.every = f32[64,8,128]{2,1,0:T(8,128)S(1)} all-to-all(f32[64,8,128]{2,1,0:T(8,128)S(1)} %broadcast_in_dim.17), channel_id=1, replica_groups=mesh['y'=4,'x'=4,'zl'=2,'c'=2,'t'=4] {'y','x','zl','c'}, dimensions={0} | all-to-all | bytes 524288 | tf_op jit(solution)/shard_map/all_to_all | solution.py:338
  95.5 4.6 %collective-permute-done.9.a3 = bf16[48,1280]{1,0:T(8,128)(2,1)S(1)} collective-permute-done((bf16[48,1280]{1,0:T(8,128)(2,1)S(1)}, bf16[48,1280]{1,0:T(8,128)(2,1)S(1)}, u32[]{:S(2)}, u32[]{:S(2)}) %collective-permute-start.9) | collective-permute-done | bytes 122912 | tf_op jit(solution)/shard_map/ppermute | solution.py:330
  107.1 4.2 %collective-permute-done.12.b3 = bf16[48,1152]{1,0:T(8,128)(2,1)S(1)} collective-permute-done((bf16[48,1152]{1,0:T(8,128)(2,1)S(1)}, bf16[48,1152]{1,0:T(8,128)(2,1)S(1)}, u32[]{:S(2)}, u32[]{:S(2)}) %collective-permute-start.12) | collective-permute-done | bytes 110624 | tf_op jit(solution)/shard_map/ppermute | solution.py:330
  118.9 6.2 %all-to-all-start.11 = ((s16[32,8,768]{2,1,0:T(8,128)(2,1)}), s16[32,8,768]{2,1,0:T(8,128)(2,1)S(1)}, u32[]{:S(2)}, u32[]{:S(2)}) async-start(s16[32,8,768]{2,1,0:T(8,128)(2,1)} %bitcast.27), calls=%async_computation.11 | async-start | bytes 786432 | tf_op jit(solution)/shard_map/all_to_all | solution.py:414
  125.7 9.3 %all-to-all-done.11.got = s16[32,8,768]{2,1,0:T(8,128)(2,1)S(1)} async-done(((s16[32,8,768]{2,1,0:T(8,128)(2,1)}), s16[32,8,768]{2,1,0:T(8,128)(2,1)S(1)}, u32[]{:S(2)}, u32[]{:S(2)}) %all-to-all-start.11) | async-done | bytes 393248 | tf_op jit(solution)/shard_map/all_to_all | solution.py:414
  136.3 270.8 %conditional.1 = (f32[]{:T(128)}, bf16[4,1280]{1,0:T(4,128)(2,1)}) conditional(s32[]{:T(128)} %bitcast.26, (s32[4]{0:T(128)S(1)}, s32[4]{0:T(128)S(1)}, bf16[4,1024]{1,0:T(4,128)(2,1)S(1)}, bf16[1024,2374]{0,1:T(8,128)(2,1)}, bf16[4,1280]{1,0:T(4,128)(2,1)S(1)}, /*index=5*/bf16[1280,2374]{0,1:T(8,128)(2,1)}) %tuple.41, (f32[1,1]{1,0:T(1,128)}, ...), branch_computations={%region_0.19_spmd, %region_19.20_spmd} | conditional | flops 4360781312 | bytes 75924464 | solution.py:482
  136.4 15.5 %all_to_all.51 = s32[64,8,128]{2,1,0:T(8,128)S(1)} all-to-all(s32[64,8,128]{2,1,0:T(8,128)S(1)} %broadcast_in_dim.1), channel_id=1, replica_groups=mesh['y'=4,'x'=4,'zl'=2,'c'=2,'t'=4] {'y','x','zl','c'}, dimensions={0} | all-to-all | bytes 524288 | tf_op jit(solution)/shard_map/cond/branch_0_fun/all_to_all | solution.py:338
  152.0 16.9 %all_to_all.52 = bf16[64,4,1024]{2,1,0:T(4,128)(2,1)S(1)} all-to-all(bf16[64,4,1024]{2,1,0:T(4,128)(2,1)S(1)} %broadcast_in_dim.2), channel_id=1, replica_groups=mesh['y'=4,'x'=4,'zl'=2,'c'=2,'t'=4] {'y','x','zl','c'}, dimensions={0} | all-to-all | bytes 1048576 | tf_op jit(solution)/shard_map/cond/branch_0_fun/all_to_all | solution.py:338
  170.0 4.5 %all-to-all-start.3 = ((bf16[64,4,1280]{2,1,0:T(4,128)(2,1)}), bf16[64,4,1280]{2,1,0:T(4,128)(2,1)S(1)}, u32[]{:S(2)}, u32[]{:S(2)}) async-start(bf16[64,4,1280]{2,1,0:T(4,128)(2,1)} %broadcast_in_dim.3), calls=%async_computation.3 | async-start | bytes 1310720 | tf_op jit(solution)/shard_map/cond/branch_0_fun/all_to_all | solution.py:338
  174.7 5.4 %fusion.4 = f32[4,64,2374]{2,1,0:T(8,128)} fusion(bf16[4,64,1024]{2,1,0:T(8,128)(2,1)S(1)} %dot_general.0, bf16[1024,2374]{0,1:T(8,128)(2,1)} %get-tuple-element.22), kind=kOutput, calls=%fused_computation.4 | convolution fusion | flops 1244659712 | bytes 7817216 | tf_op jit(solution)/shard_map/cond/branch_0_fun/dot_general | solution.py:430
  180.0 8.8 %all-to-all-done.3 = bf16[64,4,1280]{2,1,0:T(4,128)(2,1)S(1)} async-done(((bf16[64,4,1280]{2,1,0:T(4,128)(2,1)}), bf16[64,4,1280]{2,1,0:T(4,128)(2,1)S(1)}, u32[]{:S(2)}, u32[]{:S(2)}) %all-to-all-start.3) | async-done | bytes 655392 | tf_op jit(solution)/shard_map/cond/branch_0_fun/all_to_all | solution.py:338
  195.6 6.3 %fusion.2 = f32[4,64,2374]{2,1,0:T(8,128)} fusion(bf16[4,64,1280]{2,1,0:T(8,128)(2,1)} %dot_general.2, bf16[1280,2374]{0,1:T(8,128)(2,1)} %get-tuple-element.24), kind=kOutput, calls=%fused_computation.2 | convolution fusion | flops 1555824640 | bytes 9163776 | tf_op jit(solution)/shard_map/cond/branch_0_fun/dot_general | solution.py:430
  201.9 47.8 %all-to-all-done.2 = f32[4,64,2374]{2,1,0:T(8,128)S(1)} async-done(((f32[4,64,2374]{2,1,0:T(8,128)}), f32[4,64,2374]{2,1,0:T(8,128)S(1)}, u32[]{:S(2)}, u32[]{:S(2)}) %all-to-all-start.2) | async-done | bytes 2431008 | tf_op jit(solution)/shard_map/cond/branch_0_fun/all_to_all | solution.py:431
  249.7 5.3 %all-to-all-start.4 = ((f32[4,64,2374]{2,1,0:T(8,128)}), f32[4,64,2374]{2,1,0:T(8,128)}, u32[]{:S(2)}, u32[]{:S(2)}) async-start(f32[4,64,2374]{2,1,0:T(8,128)} %fusion.2), calls=%async_computation.4 | async-start | bytes 4980736 | tf_op jit(solution)/shard_map/cond/branch_0_fun/all_to_all | solution.py:431
  255.5 50.4 %all-to-all-done.4 = f32[4,64,2374]{2,1,0:T(8,128)} async-done(((f32[4,64,2374]{2,1,0:T(8,128)}), f32[4,64,2374]{2,1,0:T(8,128)}, u32[]{:S(2)}, u32[]{:S(2)}) %all-to-all-start.4) | async-done | bytes 2431008 | tf_op jit(solution)/shard_map/cond/branch_0_fun/all_to_all | solution.py:431
  308.5 21.8 %all_to_all.53 = f32[64,8,128]{2,1,0:T(8,128)S(1)} all-to-all(f32[64,8,128]{2,1,0:T(8,128)S(1)} %broadcast_in_dim.5), channel_id=1, replica_groups=mesh['y'=4,'x'=4,'zl'=2,'c'=2,'t'=4] {'y','x','zl','c'}, dimensions={0} | all-to-all | bytes 524288 | tf_op jit(solution)/shard_map/cond/branch_0_fun/all_to_all | solution.py:338
  331.7 34.0 %all_to_all.54 = bf16[4,64,2374]{2,1,0:T(8,128)(2,1)S(1)} all-to-all(bf16[4,64,2374]{2,1,0:T(8,128)(2,1)S(1)} %broadcast_in_dim.7), channel_id=1, replica_groups=mesh['y'=4,'x'=4,'zl'=2,'c'=2,'t'=4] {'t'}, dimensions={0} | all-to-all | bytes 2430976 | tf_op jit(solution)/shard_map/cond/branch_0_fun/all_to_all | solution.py:338
  371.3 4.6 %fusion = f32[64,4,1280]{2,0,1:T(8,128)S(1)} fusion(bf16[1280,2374]{0,1:T(8,128)(2,1)} %get-tuple-element.24, bf16[64,4,2374]{2,1,0:T(4,128)(2,1)S(1)} %dot_general.13), kind=kOutput, calls=%fused_computation | convolution fusion | flops 1555824640 | bytes 8603648 | tf_op jit(solution)/shard_map/cond/branch_0_fun/dot_general | solution.py:472
  377.8 7.4 %all-to-all-start.8 = ((f32[64,4,1280]{2,1,0:T(4,128)}), f32[64,4,1280]{2,1,0:T(4,128)S(1)}, u32[]{:S(2)}, u32[]{:S(2)}) async-start(f32[64,4,1280]{2,1,0:T(4,128)} %copy.35), calls=%async_computation.8 | async-start | bytes 2621440 | tf_op jit(solution)/shard_map/cond/branch_0_fun/all_to_all | solution.py:476
  387.8 18.5 %all-to-all-done.8 = f32[64,4,1280]{2,1,0:T(4,128)S(1)} async-done(((f32[64,4,1280]{2,1,0:T(4,128)}), f32[64,4,1280]{2,1,0:T(4,128)S(1)}, u32[]{:S(2)}, u32[]{:S(2)}) %all-to-all-start.8) | async-done | bytes 1310752 | tf_op jit(solution)/shard_map/cond/branch_0_fun/all_to_all | solution.py:476
  (87 shorter events, 69.8 us)
Async XLA Ops:
  23.0 3.8 collective-permute-start
  26.8 84.6 %slice-start = ((s8[6082560]{0:T(1024)(128)(4,1)}), s8[4194304]{0:T(1024)(128)(4,1)S(1)}, s32[]{:S(2)}) async-start(s8[6082560]{0:T(1024)(128)(4,1)} %bitcast.50), calls=%async_computation.12 | async-start | bytes 8388608
  26.8 84.6 %slice-start.1 = ((s8[6082560]{0:T(1024)(128)(4,1)}), s8[1888256]{0:T(1024)(128)(4,1)S(1)}, s32[]{:S(2)}) async-start(s8[6082560]{0:T(1024)(128)(4,1)} %bitcast.50), calls=%async_computation.13 | async-start | bytes 3776512
  35.2 15.1 %collective-permute-start.2 = (s16[48,2432]{1,0:T(8,128)(2,1)S(1)}, s16[48,2432]{1,0:T(8,128)(2,1)S(1)}, u32[]{:S(2)}, u32[]{:S(2)}) collective-permute-start(s16[48,2432]{1,0:T(8,128)(2,1)S(1)} %get-tuple-element.58), channel_id=1, source_target_pairs={{0,1},{1,2},{2,3},{3,0},{4,5},{5,6},{6,7},{7,4},{8,9},{9,10},{10,1... | collective-permute-start | bytes 700424 | tf_op jit(solution)/shard_map/ppermute | solution.py:330
  38.2 19.6 %collective-permute-start.5 = (s16[48,2432]{1,0:T(8,128)(2,1)S(1)}, s16[48,2432]{1,0:T(8,128)(2,1)S(1)}, u32[]{:S(2)}, u32[]{:S(2)}) collective-permute-start(s16[48,2432]{1,0:T(8,128)(2,1)S(1)} %get-tuple-element.63), channel_id=1, source_target_pairs={{0,3},{1,0},{2,1},{3,2},{4,7},{5,4},{6,5},{7,6},{8,11},{9,8},{10,9... | collective-permute-start | bytes 700424 | tf_op jit(solution)/shard_map/ppermute | solution.py:330
  40.5 22.5 %collective-permute-start.1 = (s16[48,2432]{1,0:T(8,128)(2,1)S(1)}, s16[48,2432]{1,0:T(8,128)(2,1)S(1)}, u32[]{:S(2)}, u32[]{:S(2)}) collective-permute-start(s16[48,2432]{1,0:T(8,128)(2,1)S(1)} %get-tuple-element.57), channel_id=1, source_target_pairs={{0,3},{1,0},{2,1},{3,2},{4,7},{5,4},{6,5},{7,6},{8,11},{9,8},{10,9... | collective-permute-start | bytes 700424 | tf_op jit(solution)/shard_map/ppermute | solution.py:330
  42.7 21.1 %collective-permute-start.4 = (s16[48,2432]{1,0:T(8,128)(2,1)S(1)}, s16[48,2432]{1,0:T(8,128)(2,1)S(1)}, u32[]{:S(2)}, u32[]{:S(2)}) collective-permute-start(s16[48,2432]{1,0:T(8,128)(2,1)S(1)} %get-tuple-element.62), channel_id=1, source_target_pairs={{0,1},{1,2},{2,3},{3,0},{4,5},{5,6},{6,7},{7,4},{8,9},{9,10},{10,1... | collective-permute-start | bytes 700424 | tf_op jit(solution)/shard_map/ppermute | solution.py:330
  51.1 20.3 %collective-permute-start.3 = (s16[48,2432]{1,0:T(8,128)(2,1)S(1)}, s16[48,2432]{1,0:T(8,128)(2,1)S(1)}, u32[]{:S(2)}, u32[]{:S(2)}) collective-permute-start(s16[48,2432]{1,0:T(8,128)(2,1)S(1)} %get-tuple-element.60), channel_id=1, source_target_pairs={{0,1},{1,2},{2,3},{3,0},{4,5},{5,6},{6,7},{7,4},{8,9},{9,10},{10,1... | collective-permute-start | bytes 700424 | tf_op jit(solution)/shard_map/ppermute | solution.py:330
  58.7 12.7 %collective-permute-start.6 = (s16[48,2432]{1,0:T(8,128)(2,1)S(1)}, s16[48,2432]{1,0:T(8,128)(2,1)S(1)}, u32[]{:S(2)}, u32[]{:S(2)}) collective-permute-start(s16[48,2432]{1,0:T(8,128)(2,1)S(1)} %get-tuple-element.65), channel_id=1, source_target_pairs={{0,3},{1,0},{2,1},{3,2},{4,7},{5,4},{6,5},{7,6},{8,11},{9,8},{10,9... | collective-permute-start | bytes 700424 | tf_op jit(solution)/shard_map/ppermute | solution.py:330
  91.7 8.5 %collective-permute-start.9 = (bf16[48,1280]{1,0:T(8,128)(2,1)S(1)}, bf16[48,1280]{1,0:T(8,128)(2,1)S(1)}, u32[]{:S(2)}, u32[]{:S(2)}) collective-permute-start(bf16[48,1280]{1,0:T(8,128)(2,1)S(1)} %get-tuple-element.75.a0), channel_id=1, source_target_pairs={{0,1},{1,2},{2,3},{3,0},{4,5},{5,6},{6,7},{7,4},{8,9},{9,10},{10,1... | collective-permute-start | bytes 368648 | tf_op jit(solution)/shard_map/ppermute | solution.py:330
  93.2 10.6 %collective-permute-start.8 = (bf16[48,1152]{1,0:T(8,128)(2,1)S(1)}, bf16[48,1152]{1,0:T(8,128)(2,1)S(1)}, u32[]{:S(2)}, u32[]{:S(2)}) collective-permute-start(bf16[48,1152]{1,0:T(8,128)(2,1)S(1)} %get-tuple-element.76.b0), channel_id=1, source_target_pairs={{0,3},{1,0},{2,1},{3,2},{4,7},{5,4},{6,5},{7,6},{8,11},{9,8},{10,9... | collective-permute-start | bytes 331784 | tf_op jit(solution)/shard_map/ppermute | solution.py:330
  95.5 15.9 %collective-permute-start.7 = (bf16[48,1280]{1,0:T(8,128)(2,1)S(1)}, bf16[48,1280]{1,0:T(8,128)(2,1)S(1)}, u32[]{:S(2)}, u32[]{:S(2)}) collective-permute-start(bf16[48,1280]{1,0:T(8,128)(2,1)S(1)} %get-tuple-element.75.a0), channel_id=1, source_target_pairs={{0,3},{1,0},{2,1},{3,2},{4,7},{5,4},{6,5},{7,6},{8,11},{9,8},{10,9... | collective-permute-start | bytes 368648 | tf_op jit(solution)/shard_map/ppermute | solution.py:330
  100.1 11.2 %collective-permute-start.10 = (bf16[48,1280]{1,0:T(8,128)(2,1)S(1)}, bf16[48,1280]{1,0:T(8,128)(2,1)S(1)}, u32[]{:S(2)}, u32[]{:S(2)}) collective-permute-start(bf16[48,1280]{1,0:T(8,128)(2,1)S(1)} %collective-permute-done.9.a3), channel_id=1, source_target_pairs={{0,1},{1,2},{2,3},{3,0},{4,5},{5,6},{6,7},{7,4},{8,9},{9,10},{10,1... | collective-permute-start | bytes 368648 | tf_op jit(solution)/shard_map/ppermute | solution.py:330
  101.2 10.1 %collective-permute-start.12 = (bf16[48,1152]{1,0:T(8,128)(2,1)S(1)}, bf16[48,1152]{1,0:T(8,128)(2,1)S(1)}, u32[]{:S(2)}, u32[]{:S(2)}) collective-permute-start(bf16[48,1152]{1,0:T(8,128)(2,1)S(1)} %get-tuple-element.76.b0), channel_id=1, source_target_pairs={{0,1},{1,2},{2,3},{3,0},{4,5},{5,6},{6,7},{7,4},{8,9},{9,10},{10,1... | collective-permute-start | bytes 331784 | tf_op jit(solution)/shard_map/ppermute | solution.py:330
  103.8 7.5 %collective-permute-start.11 = (bf16[48,1152]{1,0:T(8,128)(2,1)S(1)}, bf16[48,1152]{1,0:T(8,128)(2,1)S(1)}, u32[]{:S(2)}, u32[]{:S(2)}) collective-permute-start(bf16[48,1152]{1,0:T(8,128)(2,1)S(1)} %collective-permute-done.8.b1), channel_id=1, source_target_pairs={{0,3},{1,0},{2,1},{3,2},{4,7},{5,4},{6,5},{7,6},{8,11},{9,8},{10,9... | collective-permute-start | bytes 331784 | tf_op jit(solution)/shard_map/ppermute | solution.py:330
  115.0 21.3 %copy-start.1 = (bf16[4,1280]{1,0:T(4,128)(2,1)S(1)}, bf16[4,1280]{1,0:T(4,128)(2,1)}, u32[]{:S(2)}) copy-start(bf16[4,1280]{1,0:T(4,128)(2,1)} %student.1) | copy-start | bytes 30724
  115.0 21.3 %copy-start.2 = (bf16[4,1024]{1,0:T(4,128)(2,1)S(1)}, bf16[4,1024]{1,0:T(4,128)(2,1)}, u32[]{:S(2)}) copy-start(bf16[4,1024]{1,0:T(4,128)(2,1)} %teacher.1) | copy-start | bytes 24580
  115.1 2.3 collective-permute-start.13
  118.9 16.2 %all-to-all-start.11 = ((s16[32,8,768]{2,1,0:T(8,128)(2,1)}), s16[32,8,768]{2,1,0:T(8,128)(2,1)S(1)}, u32[]{:S(2)}, u32[]{:S(2)}) async-start(s16[32,8,768]{2,1,0:T(8,128)(2,1)} %bitcast.27), calls=%async_computation.11 | async-start | bytes 786432 | tf_op jit(solution)/shard_map/all_to_all | solution.py:414
  170.0 18.8 %all-to-all-start.3 = ((bf16[64,4,1280]{2,1,0:T(4,128)(2,1)}), bf16[64,4,1280]{2,1,0:T(4,128)(2,1)S(1)}, u32[]{:S(2)}, u32[]{:S(2)}) async-start(bf16[64,4,1280]{2,1,0:T(4,128)(2,1)} %broadcast_in_dim.3), calls=%async_computation.3 | async-start | bytes 1310720 | tf_op jit(solution)/shard_map/cond/branch_0_fun/all_to_all | solution.py:338
  189.7 60.0 %all-to-all-start.2 = ((f32[4,64,2374]{2,1,0:T(8,128)}), f32[4,64,2374]{2,1,0:T(8,128)S(1)}, u32[]{:S(2)}, u32[]{:S(2)}) async-start(f32[4,64,2374]{2,1,0:T(8,128)} %fusion.4), calls=%async_computation.2 | async-start | bytes 4980736 | tf_op jit(solution)/shard_map/cond/branch_0_fun/all_to_all | solution.py:431
  249.7 56.2 %all-to-all-start.4 = ((f32[4,64,2374]{2,1,0:T(8,128)}), f32[4,64,2374]{2,1,0:T(8,128)}, u32[]{:S(2)}, u32[]{:S(2)}) async-start(f32[4,64,2374]{2,1,0:T(8,128)} %fusion.2), calls=%async_computation.4 | async-start | bytes 4980736 | tf_op jit(solution)/shard_map/cond/branch_0_fun/all_to_all | solution.py:431
  367.0 10.8 %all-to-all-start.6 = ((f32[4,8,128]{2,1,0:T(8,128)}), f32[4,8,128]{2,1,0:T(8,128)S(1)}, u32[]{:S(2)}, u32[]{:S(2)}) async-start(f32[4,8,128]{2,1,0:T(8,128)} %broadcast_in_dim.6), calls=%async_computation.6 | async-start | bytes 32768 | tf_op jit(solution)/shard_map/cond/branch_0_fun/all_to_all | solution.py:338
  377.8 28.5 %all-to-all-start.8 = ((f32[64,4,1280]{2,1,0:T(4,128)}), f32[64,4,1280]{2,1,0:T(4,128)S(1)}, u32[]{:S(2)}, u32[]{:S(2)}) async-start(f32[64,4,1280]{2,1,0:T(4,128)} %copy.35), calls=%async_computation.8 | async-start | bytes 2621440 | tf_op jit(solution)/shard_map/cond/branch_0_fun/all_to_all | solution.py:476
  (3 other events, 43.4 us)

commit v4 on v3

--- a/solution.py
+++ b/solution.py
@@ -13,9 +13,9 @@
 LIVE = 192
 GROUP = LIVE // 4
 LEFT = 1280
-BLOCK = 512
 STEP = 1024.0
 BOUND = 31.9
+ROUND = 1.5 * 2.0**23
 F32 = jnp.float32
 BF16 = jnp.bfloat16
 I16 = jnp.int16
@@ -45,7 +45,7 @@
 
 
 def coded(x):
-    return jnp.clip(jnp.round(x * STEP), -32767.0, 32767.0).astype(jnp.int32).astype(I16)
+    return ((x * STEP + ROUND) - ROUND).astype(jnp.int32).astype(I16)
 
 
 def decoded(x):
@@ -63,6 +63,7 @@
     even = lane - lane % 2
     before = (line < even).astype(F32).astype(BF16)
     same = (line == even).astype(F32).astype(BF16)
+    evens = (iota((wide, wide // 2), 0) == 2 * iota((wide, wide // 2), 1)).astype(F32).astype(BF16)
     found = []
     for ref in (own, other):
         labels = ref[:, at : at + 128].astype(F32).T[:8].astype(BF16)
@@ -71,25 +72,26 @@
         ids = here[0:1] + 256.0 * here[1:2] + 65536.0 * here[2:3]
         found.append((here[3:4] > 0.5, earlier, ids, 0.5 * jnp.sum(here[3:4], keepdims=True)))
     start = (core * found[1][3], (1.0 - core) * found[0][3])
-    shift = (me * GROUP).astype(F32)
     picked = jnp.zeros((GROUP, 1), F32)
     for (ok, earlier, ids, _), base, pick, back in zip(
         found, start, (pick_own, pick_other), (back_own, back_other)
     ):
         slot = base + earlier
-        near = slot - shift
-        near = jnp.where(near < 0.0, near + LIVE, near)
+        group = jnp.floor(slot * (1.0 / GROUP) + 1e-3)
+        turn = (group - me.astype(F32)) * (1.0 - 2.0 * core)
+        turn = jnp.where(turn < 0.0, turn + 4.0, turn)
+        near = slot + GROUP * (turn - group)
         near = jnp.where(ok & (slot < LIVE), near, -1.0)
-        column = jnp.broadcast_to(near, (8, wide)).T[:, 0:1]
+        column = jnp.dot(
+            jnp.broadcast_to(near, (8, wide)).astype(BF16), evens, preferred_element_type=F32
+        ).T[:, 0:1]
         row = iota((LIVE, wide), 0).astype(F32)
         odd = iota((LIVE, wide), 1) % 2
         hit = row == near
-        slots = iota((wide, LIVE), 1).astype(F32)
-        turn = iota((wide, LIVE), 0) % 2
-        back_hit = slots == column
+        slots = (iota((wide // 2, 2 * ROWS), 1) % ROWS).astype(F32)
+        back[...] = (slots == column).astype(F32).astype(BF16)
         for half in (0, 1):
             pick[half] = (hit & (odd == half)).astype(F32).astype(BF16)
-            back[half] = (back_hit & (turn == half)).astype(F32).astype(BF16)
         chosen = (hit & (odd == 0))[:GROUP]
         picked += jnp.sum(jnp.where(chosen, ids, 0.0), axis=1, keepdims=True)
     sampled[...] = jnp.broadcast_to(picked, sampled.shape)
@@ -105,24 +107,18 @@
     full = padded(width)
     edge = full - 128
     g = GROUP
-    blocks = [(start, min(start + BLOCK, width)) for start in range(0, width, BLOCK)]
     copies = [
-        [
-            pltpu.make_async_copy(
-                head.at[start:stop], loaded.at[start:stop], sems.at[k * len(blocks) + n]
-            )
-            for n, (start, stop) in enumerate(blocks)
-        ]
+        pltpu.make_async_copy(head, loaded, sems.at[k])
         for k, (head, loaded) in enumerate(((t_head, t_loaded), (s_head, s_loaded)))
     ]
-    for copy in copies[0] + copies[1]:
+    for copy in copies:
         copy.start()
     order(
         scal, own, other, t_rows.shape[1] // 2,
         pick_own, pick_other, back_own, back_other, sampled, total,
     )
     logits[:, edge:full] = jnp.zeros((LIVE, 128), F32)
-    for (at, near, relayed), waits, rows, loaded, (first, direct, mine, held, peak) in zip(
+    for (at, near, relayed), copy, rows, loaded, (first, direct, mine, held, peak) in zip(
         places,
         copies,
         (t_rows, s_rows),
@@ -135,11 +131,10 @@
                 jnp.dot(pick_own[k], own[:, at : at + half], preferred_element_type=F32)
                 + jnp.dot(pick_other[k], other[:, at : at + half], preferred_element_type=F32)
             ).astype(BF16)
-        for (start, stop), wait in zip(blocks, waits):
-            wait.wait()
-            logits[:, start:stop] = lax.dot_general(
-                rows[...], loaded[start:stop], NT, preferred_element_type=F32
-            )
+        copy.wait()
+        logits[:, :width] = lax.dot_general(
+            rows[...], loaded[...], NT, preferred_element_type=F32
+        )
         first[...] = coded(logits[2 * g : 3 * g])
         direct[...] = coded(logits[near * g : (near + 1) * g])
         mine[...] = logits[:g]
@@ -185,6 +180,19 @@
     flipped = square[...].T[:8]
     peak = jnp.maximum(jnp.maximum(p0[...], p1[...]), jnp.maximum(p2[...], p3[...]))
     stats[...] = jnp.where(iota((8, 128), 0) == 6, peak, flipped)
+
+
+def merge_kernel(scal, mine, theirs, out):
+    a, b = mine[...], theirs[...]
+    top = jnp.maximum(a, b)
+    line = iota(a.shape, 0)
+    scaled = []
+    for x in (a, b):
+        scale = jnp.exp(x - top)
+        factor = jnp.where(line == 3, scale[1:2], jnp.where(line == 5, 1.0, scale[0:1]))
+        scaled.append(x * factor)
+    both = jnp.where((line < 2) | (line == 6), top, scaled[0] + scaled[1])
+    out[...] = jnp.broadcast_to(both[None], out.shape)
 
 
 def grad_kernel(width, scal, every, t_ref, s_ref, sampled, total, left, right):
@@ -228,35 +236,30 @@
 
 
 def back_kernel(
-    width, half, scal, a0, b0, a1, b1, a2, b2, a3, b3, total, back_own, back_other, head,
-    mine, theirs, loss, fits, grads,
+    width, scal, a0, b0, a1, b1, a2, b2, a3, b3, total, back_own, back_other, head,
+    mine, theirs, loss, fits, grads, parts,
 ):
     for k, (a, b) in enumerate(((a0, b0), (a1, b1), (a2, b2), (a3, b3))):
         grads[k * GROUP : (k + 1) * GROUP, :LEFT] = a[...]
         grads[k * GROUP : (k + 1) * GROUP, LEFT:] = b[...]
-    x = jnp.zeros((LIVE, 2 * half), F32)
-    for start in range(0, width, BLOCK):
-        stop = min(start + BLOCK, width)
-        x += jnp.dot(grads[:, start:stop], head[start:stop], preferred_element_type=F32)
+    x = jnp.dot(grads[:, :width], head[...], preferred_element_type=F32)
     high = x.astype(BF16)
     low = (x - high.astype(F32)).astype(BF16)
+    for k, part in enumerate((high, low)):
+        parts[k * ROWS : k * ROWS + LIVE] = part
+        parts[k * ROWS + LIVE : (k + 1) * ROWS] = jnp.zeros((ROWS - LIVE, x.shape[1]), BF16)
     for back, out in ((back_own, mine), (back_other, theirs)):
-        y = jnp.zeros(out.shape, F32)
-        for k in (0, 1):
-            cut = slice(k * half, (k + 1) * half)
-            y += jnp.dot(back[k], high[:, cut], preferred_element_type=F32)
-            y += jnp.dot(back[k], low[:, cut], preferred_element_type=F32)
-        out[...] = y
+        out[...] = jnp.dot(back[...], parts[...], preferred_element_type=F32)
     block = width // 128 * 128
     line, lane = iota((16, 128), 0), iota((16, 128), 1) + block - width
     block -= LEFT
-    parts, peaks = [], []
+    sums, peaks = [], []
     for ref in (b0, b1, b2, b3):
         tail = jnp.where(line == 0, ref[:16, block : block + 128].astype(F32), 0.0)
-        parts.append(jnp.sum(jnp.where((lane >= 0) & (lane < 3), tail, 0.0), keepdims=True))
+        sums.append(jnp.sum(jnp.where((lane >= 0) & (lane < 3), tail, 0.0), keepdims=True))
         peaks.append(jnp.sum(jnp.where((lane >= 3) & (lane < 6), tail, 0.0), keepdims=True))
     count = total[0:1, 0:1]
-    value = ((parts[0] + parts[2]) + (parts[1] + parts[3])) / count
+    value = ((sums[0] + sums[2]) + (sums[1] + sums[3])) / count
     peak = jnp.maximum(jnp.maximum(peaks[0], peaks[1]), jnp.maximum(peaks[2], peaks[3]))
     good = jnp.where((count <= LIVE) & (peak < BOUND), 1.0, 0.0)
     loss[0, 0] = jnp.sum(value)
@@ -269,26 +272,37 @@
     a3, b1 = hop(a0, 1), hop(b0, -1)
     b3, a1 = hop(b0, 1), hop(a0, -1)
     a2, b2 = hop(a3, 1), hop(b1, -1)
-    outs = (struct((ROWS, depth // 2), F32),) * 2 + (
+    outs = (struct((ROWS // 2, depth), F32),) * 2 + (
         struct((1, 1), F32),
         struct((1, 1), jnp.int32),
     )
     return call(
-        functools.partial(back_kernel, width, depth // 2),
+        functools.partial(back_kernel, width),
         outs, scal, a0, b0, a1, b1, a2, b2, a3, b3, total, *backs, head_t,
-        scratch=[pltpu.VMEM((LIVE, full), BF16)],
+        scratch=[pltpu.VMEM((LIVE, full), BF16), pltpu.VMEM((2 * ROWS, depth), BF16)],
         scalars=2,
     )
 
 
-def pair_kernel(scal, mine, theirs, out):
+def pair_kernel(scal, mine, theirs, out, tiles):
     x = mine[...] + theirs[...]
-    top = jnp.maximum(jnp.max(jnp.abs(x), axis=1, keepdims=True), 1e-30)
+    rows, half = x.shape[0], x.shape[1] // 2
+    count = half // 128
+    for k in (0, 1):
+        for j in range(count):
+            at = k * half + j * 128
+            tiles[j, pl.ds(k, rows, 2), :] = x[:, at : at + 128]
+    top = jnp.abs(tiles[0])
+    for j in range(1, count):
+        top = jnp.maximum(top, jnp.abs(tiles[j]))
+    top = jnp.maximum(jnp.max(top, axis=1, keepdims=True), 1e-30)
     power = jnp.ceil(jnp.log2(top) + 0.001)
-    codes = jnp.round(x * jnp.exp2(15.0 - power))
-    half = x.shape[1]
-    out[:, :half] = jnp.clip(codes, -32767.0, 32767.0).astype(jnp.int32).astype(I16)
-    out[:, half:] = jnp.broadcast_to(power, (x.shape[0], 128)).astype(jnp.int32).astype(I16)
+    scale = jnp.exp2(15.0 - power)
+    for j in range(count):
+        codes = (tiles[j] * scale + ROUND) - ROUND
+        codes = jnp.minimum(codes, 32767.0).astype(jnp.int32)
+        out[:, j * 128 : (j + 1) * 128] = codes.astype(I16)
+    out[:, half:] = jnp.broadcast_to(power, (2 * rows, 128)).astype(jnp.int32).astype(I16)
 
 
 def final_kernel(scal, got, out, square):
@@ -327,7 +341,8 @@
 
 
 def hop(x, by):
-    return lax.ppermute(x, "t", [(i, (i + by) % 4) for i in range(4)])
+    pairs = [(i, (i + by) % 4) for i in range(4)] + [(i + 4, (i - by) % 4 + 4) for i in range(4)]
+    return lax.ppermute(x, ("c", "t"), pairs)
 
 
 def swap_cores(x):
@@ -367,7 +382,7 @@
     )
     back_own, back_other, sampled, total, *made = call(
         functools.partial(front_kernel, width, ((0, 3, 1), (dt // 2 + 128, 1, 3))),
-        (struct((2, ROWS, LIVE), BF16),) * 2
+        (struct((ROWS // 2, 2 * ROWS), BF16),) * 2
         + (struct((GROUP, 128), F32), struct((8, 128), F32))
         + one + one,
         scal, own, other, t_head, s_head,
@@ -379,7 +394,7 @@
             pltpu.VMEM(t_head.shape, BF16),
             pltpu.VMEM(s_head.shape, BF16),
             pltpu.VMEM((LIVE, full), F32),
-            pltpu.SemaphoreType.DMA((2 * pl.cdiv(width, BLOCK),)),
+            pltpu.SemaphoreType.DMA((2,)),
         ],
         streamed=2,
     )
@@ -398,7 +413,8 @@
         scal, *sums, sampled, *peaks,
         scratch=[pltpu.VMEM((128, 128), F32)],
     )
-    every = spread(stats, VOCAB, 64)
+    (stats,) = call(merge_kernel, (struct((32, 8, 128), F32),), scal, stats, swap_cores(stats))
+    every = lax.all_to_all(stats, CHIPS, split_axis=0, concat_axis=0, tiled=True)
     a0, b0 = call(
         functools.partial(grad_kernel, width),
         (struct((GROUP, LEFT), BF16), struct((GROUP, full - LEFT), BF16)),
@@ -408,7 +424,8 @@
         scal, a0, b0, total, (back_own, back_other), s_head
     )
     (pair,) = call(
-        pair_kernel, (struct((ROWS, ds // 2 + 128), I16),), scal, mine, swap_cores(theirs)
+        pair_kernel, (struct((ROWS, ds // 2 + 128), I16),), scal, mine, swap_cores(theirs),
+        scratch=[pltpu.VMEM((ds // 256, ROWS, 128), F32)],
     )
     pair = pair.reshape(32, 8, ds // 2 + 128)
     got = lax.all_to_all(pair, CHIPS, split_axis=0, concat_axis=0, tiled=True)

time: 409 us -> 407 us (level)
  blocking collectives: 128 us -> 120 us
    all_to_all x5 -> x4, blocking collectives: 106 us -> 87.6 us  [spread(): lax.all_to_all(jnp.broadcast_to(x[None], (n,) + x.shape), axes, split_axi...]
    all_to_all x0 -> x1, blocking collectives: none -> 11.2 us  [short_way(): lax.all_to_all(stats, CHIPS, split_axis=0, concat_axis=0, tiled=True)]
    pallas_call x8 -> x9, Pallas kernels: 18.6 us -> 18.6 us  [call(): pl.pallas_call(body, out_shape=outs, in_specs=[SMEM] + [VMEM] * (len(args...]
  transfers between devices with their start and end apart: 20 -> 21, of which waited for: 15 -> 15; matrix products, arithmetic and copies ran while one was open for 6% -> 6% of each run, Pallas kernels for 0% -> 0%
where the time goes in v4:
time: 407 us; the launch traced here: 405 us
  waiting for transfers between devices  172 us (42%)
  blocking collectives  120 us (29%)
  starting transfers between devices  58.8 us (14%)
  Pallas kernels  19.4 us (5%)
  matrix products  16.3 us (4%)
  local copies, waits for them, and re-layouts  8.41 us (2%)
  other arithmetic  6.3 us (2%)
    all_to_all x2, waiting for transfers between devices, logits(): lax.all_to_all(part, 't', split_axis=0, concat_axis=0, tiled=True)  98 us
    all_to_all x4, blocking collectives, spread(): lax.all_to_all(jnp.broadcast_to(x[None], (n,) + x.shape), axes, split_axi...  87.6 us
    ppermute x12, waiting for transfers between devices, hop(): return lax.ppermute(x, ('c', 't'), pairs)  32.5 us
    ppermute x12, starting transfers between devices, hop(): return lax.ppermute(x, ('c', 't'), pairs)  23.6 us
    all_to_all x1, blocking collectives, short_way(): own = lax.all_to_all(packed, CHIPS, split_axis=0, concat_axis=0, tiled=True)  21.5 us
    pallas_call x9, Pallas kernels, call(): pl.pallas_call(body, out_shape=outs, in_specs=[SMEM] + [VMEM] * (len(args...  18.6 us
    all_to_all x1, waiting for transfers between devices, long_way(): lax.all_to_all(part.reshape(64, 4, ds), VOCAB, split_axis=0, concat_axis=...  18.5 us
    dot_general x2, matrix products, logits(): jnp.dot(rows, head, preferred_element_type=F32).reshape(4, group, width)  11.7 us
  transfers between devices with their start and end apart: 21, of which 15 were waited for; matrix products, arithmetic and copies ran while one was open for 6% of the time, Pallas kernels for 0%

profile of v4, /device:TPU:1, one launch (start us, length us, event | category | flops | bytes accessed | tf_op | source)
XLA Modules:
  0.0 405.5 jit_solution(2983610354945814092)
XLA Ops:
  1.4 21.5 %all_to_all.55 = bf16[32,8,1280]{2,1,0:T(8,128)(2,1)S(1)} all-to-all(bf16[32,8,1280]{2,1,0:T(8,128)(2,1)S(1)} %shard_map.81), channel_id=1, replica_groups=mesh['y'=4,'x'=4,'zl'=2,'c'=2,'t'=4] {'y','x','zl'}, dimensions={0} | all-to-all | bytes 1310720 | tf_op jit(solution)/shard_map/all_to_all | solution.py:373
  26.8 8.1 %shard_map.82 = (bf16[128,512]{1,0:T(8,128)(2,1)S(1)}, bf16[128,512]{1,0:T(8,128)(2,1)S(1)}, f32[48,128]{1,0:T(8,128)S(1)}, f32[8,128]{1,0:T(8,128)S(1)}, s16[48...) custom-call(s32[3]{0:T(128)S(1)} %pad_add_fusion.1.scal, ...), custom_call_target="tpu_custom_call" | custom-call | tf_op jit(solution)/shard_map/pallas_call | solution.py:33
  35.0 5.2 %collective-permute-start.2 = (s16[48,2432]{1,0:T(8,128)(2,1)S(1)}, s16[48,2432]{1,0:T(8,128)(2,1)S(1)}, u32[]{:S(2)}, u32[]{:S(2)}) collective-permute-start(s16[48,2432]{1,0:T(8,128)(2,1)S(1)} %get-tuple-element.58), channel_id=1, source_target_pairs={{0,1},{1,2},{2,3},{3,0},{4,7},{5,4},{6,5},{7,6},{8,9},{9,10},{10,1... | collective-permute-start | bytes 700424 | tf_op jit(solution)/shard_map/ppermute | solution.py:345
  47.9 4.4 %collective-permute-start.3 = (s16[48,2432]{1,0:T(8,128)(2,1)S(1)}, s16[48,2432]{1,0:T(8,128)(2,1)S(1)}, u32[]{:S(2)}, u32[]{:S(2)}) collective-permute-start(s16[48,2432]{1,0:T(8,128)(2,1)S(1)} %get-tuple-element.60), channel_id=1, source_target_pairs={{0,1},{1,2},{2,3},{3,0},{4,7},{5,4},{6,5},{7,6},{8,9},{9,10},{10,1... | collective-permute-start | bytes 700424 | tf_op jit(solution)/shard_map/ppermute | solution.py:345
  56.5 11.4 %collective-permute-done.1.t_direct = s16[48,2432]{1,0:T(8,128)(2,1)S(1)} collective-permute-done((s16[48,2432]{1,0:T(8,128)(2,1)S(1)}, s16[48,2432]{1,0:T(8,128)(2,1)S(1)}, u32[]{:S(2)}, u32[]{:S(2)}) %collective-permute-start.1) | collective-permute-done | bytes 233504 | tf_op jit(solution)/shard_map/ppermute | solution.py:345
  74.8 11.2 %all_to_all.56.every = f32[32,8,128]{2,1,0:T(8,128)S(1)} all-to-all(f32[32,8,128]{2,1,0:T(8,128)S(1)} %shard_map.86), channel_id=1, replica_groups=mesh['y'=4,'x'=4,'zl'=2,'c'=2,'t'=4] {'y','x','zl'}, dimensions={0} | all-to-all | bytes 262144 | tf_op jit(solution)/shard_map/all_to_all | solution.py:417
  99.9 6.1 %collective-permute-done.13.b3 = bf16[48,1152]{1,0:T(8,128)(2,1)S(1)} collective-permute-done((bf16[48,1152]{1,0:T(8,128)(2,1)S(1)}, bf16[48,1152]{1,0:T(8,128)(2,1)S(1)}, u32[]{:S(2)}, u32[]{:S(2)}) %collective-permute-start.13) | collective-permute-done | bytes 110624 | tf_op jit(solution)/shard_map/ppermute | solution.py:345
  121.7 9.6 %all-to-all-done.11.got = s16[32,8,768]{2,1,0:T(8,128)(2,1)S(1)} async-done(((s16[32,8,768]{2,1,0:T(8,128)(2,1)}), s16[32,8,768]{2,1,0:T(8,128)(2,1)S(1)}, u32[]{:S(2)}, u32[]{:S(2)}) %all-to-all-start.11) | async-done | bytes 393248 | tf_op jit(solution)/shard_map/all_to_all | solution.py:431
  132.6 271.7 %conditional.1 = (f32[]{:T(128)}, bf16[4,1280]{1,0:T(4,128)(2,1)}) conditional(s32[]{:T(128)} %bitcast.26, (s32[4]{0:T(128)S(1)}, s32[4]{0:T(128)S(1)}, bf16[4,1024]{1,0:T(4,128)(2,1)S(1)}, bf16[1024,2374]{0,1:T(8,128)(2,1)}, bf16[4,1280]{1,0:T(4,128)(2,1)S(1)}, /*index=5*/bf16[1280,2374]{0,1:T(8,128)(2,1)}) %tuple.41, (f32[1,1]{1,0:T(1,128)}, ...), branch_computations={%region_0.19_spmd, %region_19.20_spmd} | conditional | flops 4360781312 | bytes 75924464 | solution.py:499
  132.7 15.2 %all_to_all.51 = s32[64,8,128]{2,1,0:T(8,128)S(1)} all-to-all(s32[64,8,128]{2,1,0:T(8,128)S(1)} %broadcast_in_dim.1), channel_id=1, replica_groups=mesh['y'=4,'x'=4,'zl'=2,'c'=2,'t'=4] {'y','x','zl','c'}, dimensions={0} | all-to-all | bytes 524288 | tf_op jit(solution)/shard_map/cond/branch_0_fun/all_to_all | solution.py:353
  148.0 16.9 %all_to_all.52 = bf16[64,4,1024]{2,1,0:T(4,128)(2,1)S(1)} all-to-all(bf16[64,4,1024]{2,1,0:T(4,128)(2,1)S(1)} %broadcast_in_dim.2), channel_id=1, replica_groups=mesh['y'=4,'x'=4,'zl'=2,'c'=2,'t'=4] {'y','x','zl','c'}, dimensions={0} | all-to-all | bytes 1048576 | tf_op jit(solution)/shard_map/cond/branch_0_fun/all_to_all | solution.py:353
  166.0 4.5 %all-to-all-start.3 = ((bf16[64,4,1280]{2,1,0:T(4,128)(2,1)}), bf16[64,4,1280]{2,1,0:T(4,128)(2,1)S(1)}, u32[]{:S(2)}, u32[]{:S(2)}) async-start(bf16[64,4,1280]{2,1,0:T(4,128)(2,1)} %broadcast_in_dim.3), calls=%async_computation.3 | async-start | bytes 1310720 | tf_op jit(solution)/shard_map/cond/branch_0_fun/all_to_all | solution.py:353
  170.7 5.4 %fusion.4 = f32[4,64,2374]{2,1,0:T(8,128)} fusion(bf16[4,64,1024]{2,1,0:T(8,128)(2,1)S(1)} %dot_general.0, bf16[1024,2374]{0,1:T(8,128)(2,1)} %get-tuple-element.22), kind=kOutput, calls=%fused_computation.4 | convolution fusion | flops 1244659712 | bytes 7817216 | tf_op jit(solution)/shard_map/cond/branch_0_fun/dot_general | solution.py:447
  176.0 8.8 %all-to-all-done.3 = bf16[64,4,1280]{2,1,0:T(4,128)(2,1)S(1)} async-done(((bf16[64,4,1280]{2,1,0:T(4,128)(2,1)}), bf16[64,4,1280]{2,1,0:T(4,128)(2,1)S(1)}, u32[]{:S(2)}, u32[]{:S(2)}) %all-to-all-start.3) | async-done | bytes 655392 | tf_op jit(solution)/shard_map/cond/branch_0_fun/all_to_all | solution.py:353
  185.7 5.2 %all-to-all-start.2 = ((f32[4,64,2374]{2,1,0:T(8,128)}), f32[4,64,2374]{2,1,0:T(8,128)S(1)}, u32[]{:S(2)}, u32[]{:S(2)}) async-start(f32[4,64,2374]{2,1,0:T(8,128)} %fusion.4), calls=%async_computation.2 | async-start | bytes 4980736 | tf_op jit(solution)/shard_map/cond/branch_0_fun/all_to_all | solution.py:448
  193.1 6.3 %fusion.2 = f32[4,64,2374]{2,1,0:T(8,128)} fusion(bf16[4,64,1280]{2,1,0:T(8,128)(2,1)} %dot_general.2, bf16[1280,2374]{0,1:T(8,128)(2,1)} %get-tuple-element.24), kind=kOutput, calls=%fused_computation.2 | convolution fusion | flops 1555824640 | bytes 9163776 | tf_op jit(solution)/shard_map/cond/branch_0_fun/dot_general | solution.py:447
  199.4 47.9 %all-to-all-done.2 = f32[4,64,2374]{2,1,0:T(8,128)S(1)} async-done(((f32[4,64,2374]{2,1,0:T(8,128)}), f32[4,64,2374]{2,1,0:T(8,128)S(1)}, u32[]{:S(2)}, u32[]{:S(2)}) %all-to-all-start.2) | async-done | bytes 2431008 | tf_op jit(solution)/shard_map/cond/branch_0_fun/all_to_all | solution.py:448
  247.3 5.5 %all-to-all-start.4 = ((f32[4,64,2374]{2,1,0:T(8,128)}), f32[4,64,2374]{2,1,0:T(8,128)}, u32[]{:S(2)}, u32[]{:S(2)}) async-start(f32[4,64,2374]{2,1,0:T(8,128)} %fusion.2), calls=%async_computation.4 | async-start | bytes 4980736 | tf_op jit(solution)/shard_map/cond/branch_0_fun/all_to_all | solution.py:448
  253.3 50.2 %all-to-all-done.4 = f32[4,64,2374]{2,1,0:T(8,128)} async-done(((f32[4,64,2374]{2,1,0:T(8,128)}), f32[4,64,2374]{2,1,0:T(8,128)}, u32[]{:S(2)}, u32[]{:S(2)}) %all-to-all-start.4) | async-done | bytes 2431008 | tf_op jit(solution)/shard_map/cond/branch_0_fun/all_to_all | solution.py:448
  306.0 21.5 %all_to_all.53 = f32[64,8,128]{2,1,0:T(8,128)S(1)} all-to-all(f32[64,8,128]{2,1,0:T(8,128)S(1)} %broadcast_in_dim.5), channel_id=1, replica_groups=mesh['y'=4,'x'=4,'zl'=2,'c'=2,'t'=4] {'y','x','zl','c'}, dimensions={0} | all-to-all | bytes 524288 | tf_op jit(solution)/shard_map/cond/branch_0_fun/all_to_all | solution.py:353
  328.9 34.1 %all_to_all.54 = bf16[4,64,2374]{2,1,0:T(8,128)(2,1)S(1)} all-to-all(bf16[4,64,2374]{2,1,0:T(8,128)(2,1)S(1)} %broadcast_in_dim.14), channel_id=1, replica_groups=mesh['y'=4,'x'=4,'zl'=2,'c'=2,'t'=4] {'t'}, dimensions={0} | all-to-all | bytes 2430976 | tf_op jit(solution)/shard_map/cond/branch_0_fun/all_to_all | solution.py:353
  368.5 4.6 %fusion = f32[64,4,1280]{2,0,1:T(8,128)S(1)} fusion(bf16[1280,2374]{0,1:T(8,128)(2,1)} %get-tuple-element.24, bf16[64,4,2374]{2,1,0:T(4,128)(2,1)S(1)} %dot_general.13), kind=kOutput, calls=%fused_computation | convolution fusion | flops 1555824640 | bytes 8603648 | tf_op jit(solution)/shard_map/cond/branch_0_fun/dot_general | solution.py:489
  375.1 7.4 %all-to-all-start.8 = ((f32[64,4,1280]{2,1,0:T(4,128)}), f32[64,4,1280]{2,1,0:T(4,128)S(1)}, u32[]{:S(2)}, u32[]{:S(2)}) async-start(f32[64,4,1280]{2,1,0:T(4,128)} %copy.35), calls=%async_computation.8 | async-start | bytes 2621440 | tf_op jit(solution)/shard_map/cond/branch_0_fun/all_to_all | solution.py:493
  385.1 18.5 %all-to-all-done.8 = f32[64,4,1280]{2,1,0:T(4,128)S(1)} async-done(((f32[64,4,1280]{2,1,0:T(4,128)}), f32[64,4,1280]{2,1,0:T(4,128)S(1)}, u32[]{:S(2)}, u32[]{:S(2)}) %all-to-all-start.8) | async-done | bytes 1310752 | tf_op jit(solution)/shard_map/cond/branch_0_fun/all_to_all | solution.py:493
  (89 shorter events, 72.2 us)
Async XLA Ops:
  23.0 3.8 collective-permute-start
  26.8 81.1 %slice-start = ((s8[6082560]{0:T(1024)(128)(4,1)}), s8[4194304]{0:T(1024)(128)(4,1)S(1)}, s32[]{:S(2)}) async-start(s8[6082560]{0:T(1024)(128)(4,1)} %bitcast.50), calls=%async_computation.12 | async-start | bytes 8388608
  26.8 81.1 %slice-start.1 = ((s8[6082560]{0:T(1024)(128)(4,1)}), s8[1888256]{0:T(1024)(128)(4,1)S(1)}, s32[]{:S(2)}) async-start(s8[6082560]{0:T(1024)(128)(4,1)} %bitcast.50), calls=%async_computation.13 | async-start | bytes 3776512
  35.0 12.1 %collective-permute-start.2 = (s16[48,2432]{1,0:T(8,128)(2,1)S(1)}, s16[48,2432]{1,0:T(8,128)(2,1)S(1)}, u32[]{:S(2)}, u32[]{:S(2)}) collective-permute-start(s16[48,2432]{1,0:T(8,128)(2,1)S(1)} %get-tuple-element.58), channel_id=1, source_target_pairs={{0,1},{1,2},{2,3},{3,0},{4,7},{5,4},{6,5},{7,6},{8,9},{9,10},{10,1... | collective-permute-start | bytes 700424 | tf_op jit(solution)/shard_map/ppermute | solution.py:345
  40.2 15.4 %collective-permute-start.5 = (s16[48,2432]{1,0:T(8,128)(2,1)S(1)}, s16[48,2432]{1,0:T(8,128)(2,1)S(1)}, u32[]{:S(2)}, u32[]{:S(2)}) collective-permute-start(s16[48,2432]{1,0:T(8,128)(2,1)S(1)} %get-tuple-element.63), channel_id=1, source_target_pairs={{0,3},{1,0},{2,1},{3,2},{4,5},{5,6},{6,7},{7,4},{8,11},{9,8},{10,9... | collective-permute-start | bytes 700424 | tf_op jit(solution)/shard_map/ppermute | solution.py:345
  40.2 27.7 %collective-permute-start.1 = (s16[48,2432]{1,0:T(8,128)(2,1)S(1)}, s16[48,2432]{1,0:T(8,128)(2,1)S(1)}, u32[]{:S(2)}, u32[]{:S(2)}) collective-permute-start(s16[48,2432]{1,0:T(8,128)(2,1)S(1)} %get-tuple-element.57), channel_id=1, source_target_pairs={{0,3},{1,0},{2,1},{3,2},{4,5},{5,6},{6,7},{7,4},{8,11},{9,8},{10,9... | collective-permute-start | bytes 700424 | tf_op jit(solution)/shard_map/ppermute | solution.py:345
  41.6 26.3 %collective-permute-start.4 = (s16[48,2432]{1,0:T(8,128)(2,1)S(1)}, s16[48,2432]{1,0:T(8,128)(2,1)S(1)}, u32[]{:S(2)}, u32[]{:S(2)}) collective-permute-start(s16[48,2432]{1,0:T(8,128)(2,1)S(1)} %get-tuple-element.62), channel_id=1, source_target_pairs={{0,1},{1,2},{2,3},{3,0},{4,7},{5,4},{6,5},{7,6},{8,9},{9,10},{10,1... | collective-permute-start | bytes 700424 | tf_op jit(solution)/shard_map/ppermute | solution.py:345
  47.9 20.1 %collective-permute-start.3 = (s16[48,2432]{1,0:T(8,128)(2,1)S(1)}, s16[48,2432]{1,0:T(8,128)(2,1)S(1)}, u32[]{:S(2)}, u32[]{:S(2)}) collective-permute-start(s16[48,2432]{1,0:T(8,128)(2,1)S(1)} %get-tuple-element.60), channel_id=1, source_target_pairs={{0,1},{1,2},{2,3},{3,0},{4,7},{5,4},{6,5},{7,6},{8,9},{9,10},{10,1... | collective-permute-start | bytes 700424 | tf_op jit(solution)/shard_map/ppermute | solution.py:345
  56.4 15.4 %collective-permute-start.6 = (s16[48,2432]{1,0:T(8,128)(2,1)S(1)}, s16[48,2432]{1,0:T(8,128)(2,1)S(1)}, u32[]{:S(2)}, u32[]{:S(2)}) collective-permute-start(s16[48,2432]{1,0:T(8,128)(2,1)S(1)} %get-tuple-element.65), channel_id=1, source_target_pairs={{0,3},{1,0},{2,1},{3,2},{4,5},{5,6},{6,7},{7,4},{8,11},{9,8},{10,9... | collective-permute-start | bytes 700424 | tf_op jit(solution)/shard_map/ppermute | solution.py:345
  73.0 1.2 collective-permute-start.7
  87.0 6.7 %collective-permute-start.10 = (bf16[48,1280]{1,0:T(8,128)(2,1)S(1)}, bf16[48,1280]{1,0:T(8,128)(2,1)S(1)}, u32[]{:S(2)}, u32[]{:S(2)}) collective-permute-start(bf16[48,1280]{1,0:T(8,128)(2,1)S(1)} %get-tuple-element.75.a0), channel_id=1, source_target_pairs={{0,1},{1,2},{2,3},{3,0},{4,7},{5,4},{6,5},{7,6},{8,9},{9,10},{10,1... | collective-permute-start | bytes 368648 | tf_op jit(solution)/shard_map/ppermute | solution.py:345
  89.8 10.1 %collective-permute-start.9 = (bf16[48,1152]{1,0:T(8,128)(2,1)S(1)}, bf16[48,1152]{1,0:T(8,128)(2,1)S(1)}, u32[]{:S(2)}, u32[]{:S(2)}) collective-permute-start(bf16[48,1152]{1,0:T(8,128)(2,1)S(1)} %get-tuple-element.76.b0), channel_id=1, source_target_pairs={{0,3},{1,0},{2,1},{3,2},{4,5},{5,6},{6,7},{7,4},{8,11},{9,8},{10,9... | collective-permute-start | bytes 331784 | tf_op jit(solution)/shard_map/ppermute | solution.py:345
  90.2 15.8 %collective-permute-start.8 = (bf16[48,1280]{1,0:T(8,128)(2,1)S(1)}, bf16[48,1280]{1,0:T(8,128)(2,1)S(1)}, u32[]{:S(2)}, u32[]{:S(2)}) collective-permute-start(bf16[48,1280]{1,0:T(8,128)(2,1)S(1)} %get-tuple-element.75.a0), channel_id=1, source_target_pairs={{0,3},{1,0},{2,1},{3,2},{4,5},{5,6},{6,7},{7,4},{8,11},{9,8},{10,9... | collective-permute-start | bytes 368648 | tf_op jit(solution)/shard_map/ppermute | solution.py:345
  93.7 14.2 %collective-permute-start.11 = (bf16[48,1280]{1,0:T(8,128)(2,1)S(1)}, bf16[48,1280]{1,0:T(8,128)(2,1)S(1)}, u32[]{:S(2)}, u32[]{:S(2)}) collective-permute-start(bf16[48,1280]{1,0:T(8,128)(2,1)S(1)} %collective-permute-done.10.a3), channel_id=1, source_target_pairs={{0,1},{1,2},{2,3},{3,0},{4,7},{5,4},{6,5},{7,6},{8,9},{9,10},{10,1... | collective-permute-start | bytes 368648 | tf_op jit(solution)/shard_map/ppermute | solution.py:345
  96.9 9.0 %collective-permute-start.13 = (bf16[48,1152]{1,0:T(8,128)(2,1)S(1)}, bf16[48,1152]{1,0:T(8,128)(2,1)S(1)}, u32[]{:S(2)}, u32[]{:S(2)}) collective-permute-start(bf16[48,1152]{1,0:T(8,128)(2,1)S(1)} %get-tuple-element.76.b0), channel_id=1, source_target_pairs={{0,1},{1,2},{2,3},{3,0},{4,7},{5,4},{6,5},{7,6},{8,9},{9,10},{10,1... | collective-permute-start | bytes 331784 | tf_op jit(solution)/shard_map/ppermute | solution.py:345
  99.9 8.0 %collective-permute-start.12 = (bf16[48,1152]{1,0:T(8,128)(2,1)S(1)}, bf16[48,1152]{1,0:T(8,128)(2,1)S(1)}, u32[]{:S(2)}, u32[]{:S(2)}) collective-permute-start(bf16[48,1152]{1,0:T(8,128)(2,1)S(1)} %collective-permute-done.9.b1), channel_id=1, source_target_pairs={{0,3},{1,0},{2,1},{3,2},{4,5},{5,6},{6,7},{7,4},{8,11},{9,8},{10,9... | collective-permute-start | bytes 331784 | tf_op jit(solution)/shard_map/ppermute | solution.py:345
  111.1 21.5 %copy-start.1 = (bf16[4,1280]{1,0:T(4,128)(2,1)S(1)}, bf16[4,1280]{1,0:T(4,128)(2,1)}, u32[]{:S(2)}) copy-start(bf16[4,1280]{1,0:T(4,128)(2,1)} %student.1) | copy-start | bytes 30724
  111.1 4.4 %collective-permute-start.14 = (f32[128,1280]{1,0:T(8,128)S(1)}, f32[128,1280]{1,0:T(8,128)S(1)}, u32[]{:S(2)}, u32[]{:S(2)}) collective-permute-start(f32[128,1280]{1,0:T(8,128)S(1)} %get-tuple-element.82), channel_id=1, source_target_pairs={{0,4},{4,0},{1,5},{5,1},{2,6},{6,2},{3,7},{7,3},{8,12},{12,8},{9,1... | collective-permute-start | bytes 1966088 | tf_op jit(solution)/shard_map/ppermute | solution.py:349
  117.2 14.2 %all-to-all-start.11 = ((s16[32,8,768]{2,1,0:T(8,128)(2,1)}), s16[32,8,768]{2,1,0:T(8,128)(2,1)S(1)}, u32[]{:S(2)}, u32[]{:S(2)}) async-start(s16[32,8,768]{2,1,0:T(8,128)(2,1)} %bitcast.27), calls=%async_computation.11 | async-start | bytes 786432 | tf_op jit(solution)/shard_map/all_to_all | solution.py:431
  166.0 18.8 %all-to-all-start.3 = ((bf16[64,4,1280]{2,1,0:T(4,128)(2,1)}), bf16[64,4,1280]{2,1,0:T(4,128)(2,1)S(1)}, u32[]{:S(2)}, u32[]{:S(2)}) async-start(bf16[64,4,1280]{2,1,0:T(4,128)(2,1)} %broadcast_in_dim.3), calls=%async_computation.3 | async-start | bytes 1310720 | tf_op jit(solution)/shard_map/cond/branch_0_fun/all_to_all | solution.py:353
  185.7 61.6 %all-to-all-start.2 = ((f32[4,64,2374]{2,1,0:T(8,128)}), f32[4,64,2374]{2,1,0:T(8,128)S(1)}, u32[]{:S(2)}, u32[]{:S(2)}) async-start(f32[4,64,2374]{2,1,0:T(8,128)} %fusion.4), calls=%async_computation.2 | async-start | bytes 4980736 | tf_op jit(solution)/shard_map/cond/branch_0_fun/all_to_all | solution.py:448
  247.3 56.2 %all-to-all-start.4 = ((f32[4,64,2374]{2,1,0:T(8,128)}), f32[4,64,2374]{2,1,0:T(8,128)}, u32[]{:S(2)}, u32[]{:S(2)}) async-start(f32[4,64,2374]{2,1,0:T(8,128)} %fusion.2), calls=%async_computation.4 | async-start | bytes 4980736 | tf_op jit(solution)/shard_map/cond/branch_0_fun/all_to_all | solution.py:448
  364.3 10.8 %all-to-all-start.6 = ((f32[4,8,128]{2,1,0:T(8,128)}), f32[4,8,128]{2,1,0:T(8,128)S(1)}, u32[]{:S(2)}, u32[]{:S(2)}) async-start(f32[4,8,128]{2,1,0:T(8,128)} %broadcast_in_dim.6), calls=%async_computation.6 | async-start | bytes 32768 | tf_op jit(solution)/shard_map/cond/branch_0_fun/all_to_all | solution.py:353
  375.1 28.5 %all-to-all-start.8 = ((f32[64,4,1280]{2,1,0:T(4,128)}), f32[64,4,1280]{2,1,0:T(4,128)S(1)}, u32[]{:S(2)}, u32[]{:S(2)}) async-start(f32[64,4,1280]{2,1,0:T(4,128)} %copy.35), calls=%async_computation.8 | async-start | bytes 2621440 | tf_op jit(solution)/shard_map/cond/branch_0_fun/all_to_all | solution.py:493
  (4 other events, 65.4 us)

commit v5 on v4

--- a/solution.py
+++ b/solution.py
@@ -236,8 +236,8 @@
 
 
 def back_kernel(
-    width, scal, a0, b0, a1, b1, a2, b2, a3, b3, total, back_own, back_other, head,
-    mine, theirs, loss, fits, grads, parts,
+    width, scal, a0, b0, a1, b1, a2, b2, a3, b3, total, back_other, head,
+    theirs, parts, loss, fits, grads,
 ):
     for k, (a, b) in enumerate(((a0, b0), (a1, b1), (a2, b2), (a3, b3))):
         grads[k * GROUP : (k + 1) * GROUP, :LEFT] = a[...]
@@ -248,8 +248,7 @@
     for k, part in enumerate((high, low)):
         parts[k * ROWS : k * ROWS + LIVE] = part
         parts[k * ROWS + LIVE : (k + 1) * ROWS] = jnp.zeros((ROWS - LIVE, x.shape[1]), BF16)
-    for back, out in ((back_own, mine), (back_other, theirs)):
-        out[...] = jnp.dot(back[...], parts[...], preferred_element_type=F32)
+    theirs[...] = jnp.dot(back_other[...], parts[...], preferred_element_type=F32)
     block = width // 128 * 128
     line, lane = iota((16, 128), 0), iota((16, 128), 1) + block - width
     block -= LEFT
@@ -266,20 +265,26 @@
     fits[0, 0] = jnp.sum(good).astype(jnp.int32)
 
 
+def place_kernel(scal, back, parts, out):
+    out[...] = jnp.dot(back[...], parts[...], preferred_element_type=F32)
+
+
 def hidden_grad(scal, a0, b0, total, backs, head_t):
     width, depth = head_t.shape
     full = padded(width)
     a3, b1 = hop(a0, 1), hop(b0, -1)
     b3, a1 = hop(b0, 1), hop(a0, -1)
     a2, b2 = hop(a3, 1), hop(b1, -1)
-    outs = (struct((ROWS // 2, depth), F32),) * 2 + (
+    outs = (
+        struct((ROWS // 2, depth), F32),
+        struct((2 * ROWS, depth), BF16),
         struct((1, 1), F32),
         struct((1, 1), jnp.int32),
     )
     return call(
         functools.partial(back_kernel, width),
-        outs, scal, a0, b0, a1, b1, a2, b2, a3, b3, total, *backs, head_t,
-        scratch=[pltpu.VMEM((LIVE, full), BF16), pltpu.VMEM((2 * ROWS, depth), BF16)],
+        outs, scal, a0, b0, a1, b1, a2, b2, a3, b3, total, backs[1], head_t,
+        scratch=[pltpu.VMEM((LIVE, full), BF16)],
         scalars=2,
     )
 
@@ -420,9 +425,10 @@
         (struct((GROUP, LEFT), BF16), struct((GROUP, full - LEFT), BF16)),
         scal, every, t_logits, s_logits, sampled, total,
     )
-    mine, theirs, loss, fits = hidden_grad(
+    theirs, parts, loss, fits = hidden_grad(
         scal, a0, b0, total, (back_own, back_other), s_head
     )
+    (mine,) = call(place_kernel, (struct(theirs.shape, F32),), scal, back_own, parts)
     (pair,) = call(
         pair_kernel, (struct((ROWS, ds // 2 + 128), I16),), scal, mine, swap_cores(theirs),
         scratch=[pltpu.VMEM((ds // 256, ROWS, 128), F32)],

time: 407 us -> 406 us (level)
    pallas_call x9 -> x10, Pallas kernels: 18.6 us -> 19.1 us  [call(): pl.pallas_call(body, out_shape=outs, in_specs=[SMEM] + [VMEM] * (len(args...]
  transfers between devices with their start and end apart: 21 -> 21, of which waited for: 15 -> 15; matrix products, arithmetic and copies ran while one was open for 6% -> 6% of each run, Pallas kernels for 0% -> 1%
where the time goes in v5:
time: 406 us; the launch traced here: 405 us
  waiting for transfers between devices  171 us (42%)
  blocking collectives  120 us (30%)
  starting transfers between devices  58.8 us (14%)
  Pallas kernels  19.9 us (5%)
  matrix products  16.3 us (4%)
  local copies, waits for them, and re-layouts  8.4 us (2%)
  other arithmetic  6.3 us (2%)
    all_to_all x2, waiting for transfers between devices, logits(): lax.all_to_all(part, 't', split_axis=0, concat_axis=0, tiled=True)  98 us
    all_to_all x4, blocking collectives, spread(): lax.all_to_all(jnp.broadcast_to(x[None], (n,) + x.shape), axes, split_axi...  87.6 us
    ppermute x12, waiting for transfers between devices, hop(): return lax.ppermute(x, ('c', 't'), pairs)  32.5 us
    ppermute x12, starting transfers between devices, hop(): return lax.ppermute(x, ('c', 't'), pairs)  23.6 us
    all_to_all x1, blocking collectives, short_way(): own = lax.all_to_all(packed, CHIPS, split_axis=0, concat_axis=0, tiled=True)  21.5 us
    pallas_call x10, Pallas kernels, call(): pl.pallas_call(body, out_shape=outs, in_specs=[SMEM] + [VMEM] * (len(args...  19.1 us
    all_to_all x1, waiting for transfers between devices, long_way(): lax.all_to_all(part.reshape(64, 4, ds), VOCAB, split_axis=0, concat_axis=...  18.5 us
    dot_general x2, matrix products, logits(): jnp.dot(rows, head, preferred_element_type=F32).reshape(4, group, width)  11.7 us
  transfers between devices with their start and end apart: 21, of which 15 were waited for; matrix products, arithmetic and copies ran while one was open for 6% of the time, Pallas kernels for 1%

profile of v5, /device:TPU:1, one launch (start us, length us, event | category | flops | bytes accessed | tf_op | source)
XLA Modules:
  0.0 405.1 jit_solution(1930518831950471858)
XLA Ops:
  1.4 21.5 %all_to_all.55 = bf16[32,8,1280]{2,1,0:T(8,128)(2,1)S(1)} all-to-all(bf16[32,8,1280]{2,1,0:T(8,128)(2,1)S(1)} %shard_map.81), channel_id=1, replica_groups=mesh['y'=4,'x'=4,'zl'=2,'c'=2,'t'=4] {'y','x','zl'}, dimensions={0} | all-to-all | bytes 1310720 | tf_op jit(solution)/shard_map/all_to_all | solution.py:378
  26.8 8.1 %shard_map.82 = (bf16[128,512]{1,0:T(8,128)(2,1)S(1)}, bf16[128,512]{1,0:T(8,128)(2,1)S(1)}, f32[48,128]{1,0:T(8,128)S(1)}, f32[8,128]{1,0:T(8,128)S(1)}, s16[48...) custom-call(s32[3]{0:T(128)S(1)} %pad_add_fusion.1.scal, ...), custom_call_target="tpu_custom_call" | custom-call | tf_op jit(solution)/shard_map/pallas_call | solution.py:33
  35.0 5.2 %collective-permute-start.2 = (s16[48,2432]{1,0:T(8,128)(2,1)S(1)}, s16[48,2432]{1,0:T(8,128)(2,1)S(1)}, u32[]{:S(2)}, u32[]{:S(2)}) collective-permute-start(s16[48,2432]{1,0:T(8,128)(2,1)S(1)} %get-tuple-element.58), channel_id=1, source_target_pairs={{0,1},{1,2},{2,3},{3,0},{4,7},{5,4},{6,5},{7,6},{8,9},{9,10},{10,1... | collective-permute-start | bytes 700424 | tf_op jit(solution)/shard_map/ppermute | solution.py:350
  47.9 4.4 %collective-permute-start.3 = (s16[48,2432]{1,0:T(8,128)(2,1)S(1)}, s16[48,2432]{1,0:T(8,128)(2,1)S(1)}, u32[]{:S(2)}, u32[]{:S(2)}) collective-permute-start(s16[48,2432]{1,0:T(8,128)(2,1)S(1)} %get-tuple-element.60), channel_id=1, source_target_pairs={{0,1},{1,2},{2,3},{3,0},{4,7},{5,4},{6,5},{7,6},{8,9},{9,10},{10,1... | collective-permute-start | bytes 700424 | tf_op jit(solution)/shard_map/ppermute | solution.py:350
  56.5 11.4 %collective-permute-done.1.t_direct = s16[48,2432]{1,0:T(8,128)(2,1)S(1)} collective-permute-done((s16[48,2432]{1,0:T(8,128)(2,1)S(1)}, s16[48,2432]{1,0:T(8,128)(2,1)S(1)}, u32[]{:S(2)}, u32[]{:S(2)}) %collective-permute-start.1) | collective-permute-done | bytes 233504 | tf_op jit(solution)/shard_map/ppermute | solution.py:350
  74.8 11.2 %all_to_all.56.every = f32[32,8,128]{2,1,0:T(8,128)S(1)} all-to-all(f32[32,8,128]{2,1,0:T(8,128)S(1)} %shard_map.86), channel_id=1, replica_groups=mesh['y'=4,'x'=4,'zl'=2,'c'=2,'t'=4] {'y','x','zl'}, dimensions={0} | all-to-all | bytes 262144 | tf_op jit(solution)/shard_map/all_to_all | solution.py:422
  99.9 6.1 %collective-permute-done.13.b3 = bf16[48,1152]{1,0:T(8,128)(2,1)S(1)} collective-permute-done((bf16[48,1152]{1,0:T(8,128)(2,1)S(1)}, bf16[48,1152]{1,0:T(8,128)(2,1)S(1)}, u32[]{:S(2)}, u32[]{:S(2)}) %collective-permute-start.13) | collective-permute-done | bytes 110624 | tf_op jit(solution)/shard_map/ppermute | solution.py:350
  121.3 9.6 %all-to-all-done.11.got = s16[32,8,768]{2,1,0:T(8,128)(2,1)S(1)} async-done(((s16[32,8,768]{2,1,0:T(8,128)(2,1)}), s16[32,8,768]{2,1,0:T(8,128)(2,1)S(1)}, u32[]{:S(2)}, u32[]{:S(2)}) %all-to-all-start.11) | async-done | bytes 393248 | tf_op jit(solution)/shard_map/all_to_all | solution.py:437
  132.3 271.7 %conditional.1 = (f32[]{:T(128)}, bf16[4,1280]{1,0:T(4,128)(2,1)}) conditional(s32[]{:T(128)} %bitcast.26, (s32[4]{0:T(128)S(1)}, s32[4]{0:T(128)S(1)}, bf16[4,1024]{1,0:T(4,128)(2,1)S(1)}, bf16[1024,2374]{0,1:T(8,128)(2,1)}, bf16[4,1280]{1,0:T(4,128)(2,1)S(1)}, /*index=5*/bf16[1280,2374]{0,1:T(8,128)(2,1)}) %tuple.41, (f32[1,1]{1,0:T(1,128)}, ...), branch_computations={%region_0.19_spmd, %region_19.20_spmd} | conditional | flops 4360781312 | bytes 75924464 | solution.py:505
  132.3 15.2 %all_to_all.51 = s32[64,8,128]{2,1,0:T(8,128)S(1)} all-to-all(s32[64,8,128]{2,1,0:T(8,128)S(1)} %broadcast_in_dim.1), channel_id=1, replica_groups=mesh['y'=4,'x'=4,'zl'=2,'c'=2,'t'=4] {'y','x','zl','c'}, dimensions={0} | all-to-all | bytes 524288 | tf_op jit(solution)/shard_map/cond/branch_0_fun/all_to_all | solution.py:358
  147.6 16.9 %all_to_all.52 = bf16[64,4,1024]{2,1,0:T(4,128)(2,1)S(1)} all-to-all(bf16[64,4,1024]{2,1,0:T(4,128)(2,1)S(1)} %broadcast_in_dim.2), channel_id=1, replica_groups=mesh['y'=4,'x'=4,'zl'=2,'c'=2,'t'=4] {'y','x','zl','c'}, dimensions={0} | all-to-all | bytes 1048576 | tf_op jit(solution)/shard_map/cond/branch_0_fun/all_to_all | solution.py:358
  165.6 4.5 %all-to-all-start.3 = ((bf16[64,4,1280]{2,1,0:T(4,128)(2,1)}), bf16[64,4,1280]{2,1,0:T(4,128)(2,1)S(1)}, u32[]{:S(2)}, u32[]{:S(2)}) async-start(bf16[64,4,1280]{2,1,0:T(4,128)(2,1)} %broadcast_in_dim.3), calls=%async_computation.3 | async-start | bytes 1310720 | tf_op jit(solution)/shard_map/cond/branch_0_fun/all_to_all | solution.py:358
  170.3 5.4 %fusion.4 = f32[4,64,2374]{2,1,0:T(8,128)} fusion(bf16[4,64,1024]{2,1,0:T(8,128)(2,1)S(1)} %dot_general.0, bf16[1024,2374]{0,1:T(8,128)(2,1)} %get-tuple-element.22), kind=kOutput, calls=%fused_computation.4 | convolution fusion | flops 1244659712 | bytes 7817216 | tf_op jit(solution)/shard_map/cond/branch_0_fun/dot_general | solution.py:453
  175.7 8.8 %all-to-all-done.3 = bf16[64,4,1280]{2,1,0:T(4,128)(2,1)S(1)} async-done(((bf16[64,4,1280]{2,1,0:T(4,128)(2,1)}), bf16[64,4,1280]{2,1,0:T(4,128)(2,1)S(1)}, u32[]{:S(2)}, u32[]{:S(2)}) %all-to-all-start.3) | async-done | bytes 655392 | tf_op jit(solution)/shard_map/cond/branch_0_fun/all_to_all | solution.py:358
  185.3 5.2 %all-to-all-start.2 = ((f32[4,64,2374]{2,1,0:T(8,128)}), f32[4,64,2374]{2,1,0:T(8,128)S(1)}, u32[]{:S(2)}, u32[]{:S(2)}) async-start(f32[4,64,2374]{2,1,0:T(8,128)} %fusion.4), calls=%async_computation.2 | async-start | bytes 4980736 | tf_op jit(solution)/shard_map/cond/branch_0_fun/all_to_all | solution.py:454
  192.7 6.3 %fusion.2 = f32[4,64,2374]{2,1,0:T(8,128)} fusion(bf16[4,64,1280]{2,1,0:T(8,128)(2,1)} %dot_general.2, bf16[1280,2374]{0,1:T(8,128)(2,1)} %get-tuple-element.24), kind=kOutput, calls=%fused_computation.2 | convolution fusion | flops 1555824640 | bytes 9163776 | tf_op jit(solution)/shard_map/cond/branch_0_fun/dot_general | solution.py:453
  199.0 47.9 %all-to-all-done.2 = f32[4,64,2374]{2,1,0:T(8,128)S(1)} async-done(((f32[4,64,2374]{2,1,0:T(8,128)}), f32[4,64,2374]{2,1,0:T(8,128)S(1)}, u32[]{:S(2)}, u32[]{:S(2)}) %all-to-all-start.2) | async-done | bytes 2431008 | tf_op jit(solution)/shard_map/cond/branch_0_fun/all_to_all | solution.py:454
  246.9 5.5 %all-to-all-start.4 = ((f32[4,64,2374]{2,1,0:T(8,128)}), f32[4,64,2374]{2,1,0:T(8,128)}, u32[]{:S(2)}, u32[]{:S(2)}) async-start(f32[4,64,2374]{2,1,0:T(8,128)} %fusion.2), calls=%async_computation.4 | async-start | bytes 4980736 | tf_op jit(solution)/shard_map/cond/branch_0_fun/all_to_all | solution.py:454
  252.9 50.2 %all-to-all-done.4 = f32[4,64,2374]{2,1,0:T(8,128)} async-done(((f32[4,64,2374]{2,1,0:T(8,128)}), f32[4,64,2374]{2,1,0:T(8,128)}, u32[]{:S(2)}, u32[]{:S(2)}) %all-to-all-start.4) | async-done | bytes 2431008 | tf_op jit(solution)/shard_map/cond/branch_0_fun/all_to_all | solution.py:454
  305.6 21.5 %all_to_all.53 = f32[64,8,128]{2,1,0:T(8,128)S(1)} all-to-all(f32[64,8,128]{2,1,0:T(8,128)S(1)} %broadcast_in_dim.5), channel_id=1, replica_groups=mesh['y'=4,'x'=4,'zl'=2,'c'=2,'t'=4] {'y','x','zl','c'}, dimensions={0} | all-to-all | bytes 524288 | tf_op jit(solution)/shard_map/cond/branch_0_fun/all_to_all | solution.py:358
  328.6 34.1 %all_to_all.54 = bf16[4,64,2374]{2,1,0:T(8,128)(2,1)S(1)} all-to-all(bf16[4,64,2374]{2,1,0:T(8,128)(2,1)S(1)} %broadcast_in_dim.14), channel_id=1, replica_groups=mesh['y'=4,'x'=4,'zl'=2,'c'=2,'t'=4] {'t'}, dimensions={0} | all-to-all | bytes 2430976 | tf_op jit(solution)/shard_map/cond/branch_0_fun/all_to_all | solution.py:358
  368.1 4.6 %fusion = f32[64,4,1280]{2,0,1:T(8,128)S(1)} fusion(bf16[1280,2374]{0,1:T(8,128)(2,1)} %get-tuple-element.24, bf16[64,4,2374]{2,1,0:T(4,128)(2,1)S(1)} %dot_general.13), kind=kOutput, calls=%fused_computation | convolution fusion | flops 1555824640 | bytes 8603648 | tf_op jit(solution)/shard_map/cond/branch_0_fun/dot_general | solution.py:495
  374.7 7.4 %all-to-all-start.8 = ((f32[64,4,1280]{2,1,0:T(4,128)}), f32[64,4,1280]{2,1,0:T(4,128)S(1)}, u32[]{:S(2)}, u32[]{:S(2)}) async-start(f32[64,4,1280]{2,1,0:T(4,128)} %copy.35), calls=%async_computation.8 | async-start | bytes 2621440 | tf_op jit(solution)/shard_map/cond/branch_0_fun/all_to_all | solution.py:499
  384.7 18.5 %all-to-all-done.8 = f32[64,4,1280]{2,1,0:T(4,128)S(1)} async-done(((f32[64,4,1280]{2,1,0:T(4,128)}), f32[64,4,1280]{2,1,0:T(4,128)S(1)}, u32[]{:S(2)}, u32[]{:S(2)}) %all-to-all-start.8) | async-done | bytes 1310752 | tf_op jit(solution)/shard_map/cond/branch_0_fun/all_to_all | solution.py:499
  (90 shorter events, 71.8 us)
Async XLA Ops:
  23.0 3.8 collective-permute-start
  26.8 81.1 %slice-start = ((s8[6082560]{0:T(1024)(128)(4,1)}), s8[4194304]{0:T(1024)(128)(4,1)S(1)}, s32[]{:S(2)}) async-start(s8[6082560]{0:T(1024)(128)(4,1)} %bitcast.50), calls=%async_computation.12 | async-start | bytes 8388608
  26.8 81.1 %slice-start.1 = ((s8[6082560]{0:T(1024)(128)(4,1)}), s8[1888256]{0:T(1024)(128)(4,1)S(1)}, s32[]{:S(2)}) async-start(s8[6082560]{0:T(1024)(128)(4,1)} %bitcast.50), calls=%async_computation.13 | async-start | bytes 3776512
  35.0 12.1 %collective-permute-start.2 = (s16[48,2432]{1,0:T(8,128)(2,1)S(1)}, s16[48,2432]{1,0:T(8,128)(2,1)S(1)}, u32[]{:S(2)}, u32[]{:S(2)}) collective-permute-start(s16[48,2432]{1,0:T(8,128)(2,1)S(1)} %get-tuple-element.58), channel_id=1, source_target_pairs={{0,1},{1,2},{2,3},{3,0},{4,7},{5,4},{6,5},{7,6},{8,9},{9,10},{10,1... | collective-permute-start | bytes 700424 | tf_op jit(solution)/shard_map/ppermute | solution.py:350
  40.2 15.4 %collective-permute-start.5 = (s16[48,2432]{1,0:T(8,128)(2,1)S(1)}, s16[48,2432]{1,0:T(8,128)(2,1)S(1)}, u32[]{:S(2)}, u32[]{:S(2)}) collective-permute-start(s16[48,2432]{1,0:T(8,128)(2,1)S(1)} %get-tuple-element.63), channel_id=1, source_target_pairs={{0,3},{1,0},{2,1},{3,2},{4,5},{5,6},{6,7},{7,4},{8,11},{9,8},{10,9... | collective-permute-start | bytes 700424 | tf_op jit(solution)/shard_map/ppermute | solution.py:350
  40.2 27.7 %collective-permute-start.1 = (s16[48,2432]{1,0:T(8,128)(2,1)S(1)}, s16[48,2432]{1,0:T(8,128)(2,1)S(1)}, u32[]{:S(2)}, u32[]{:S(2)}) collective-permute-start(s16[48,2432]{1,0:T(8,128)(2,1)S(1)} %get-tuple-element.57), channel_id=1, source_target_pairs={{0,3},{1,0},{2,1},{3,2},{4,5},{5,6},{6,7},{7,4},{8,11},{9,8},{10,9... | collective-permute-start | bytes 700424 | tf_op jit(solution)/shard_map/ppermute | solution.py:350
  41.6 26.3 %collective-permute-start.4 = (s16[48,2432]{1,0:T(8,128)(2,1)S(1)}, s16[48,2432]{1,0:T(8,128)(2,1)S(1)}, u32[]{:S(2)}, u32[]{:S(2)}) collective-permute-start(s16[48,2432]{1,0:T(8,128)(2,1)S(1)} %get-tuple-element.62), channel_id=1, source_target_pairs={{0,1},{1,2},{2,3},{3,0},{4,7},{5,4},{6,5},{7,6},{8,9},{9,10},{10,1... | collective-permute-start | bytes 700424 | tf_op jit(solution)/shard_map/ppermute | solution.py:350
  47.9 20.1 %collective-permute-start.3 = (s16[48,2432]{1,0:T(8,128)(2,1)S(1)}, s16[48,2432]{1,0:T(8,128)(2,1)S(1)}, u32[]{:S(2)}, u32[]{:S(2)}) collective-permute-start(s16[48,2432]{1,0:T(8,128)(2,1)S(1)} %get-tuple-element.60), channel_id=1, source_target_pairs={{0,1},{1,2},{2,3},{3,0},{4,7},{5,4},{6,5},{7,6},{8,9},{9,10},{10,1... | collective-permute-start | bytes 700424 | tf_op jit(solution)/shard_map/ppermute | solution.py:350
  56.4 15.4 %collective-permute-start.6 = (s16[48,2432]{1,0:T(8,128)(2,1)S(1)}, s16[48,2432]{1,0:T(8,128)(2,1)S(1)}, u32[]{:S(2)}, u32[]{:S(2)}) collective-permute-start(s16[48,2432]{1,0:T(8,128)(2,1)S(1)} %get-tuple-element.65), channel_id=1, source_target_pairs={{0,3},{1,0},{2,1},{3,2},{4,5},{5,6},{6,7},{7,4},{8,11},{9,8},{10,9... | collective-permute-start | bytes 700424 | tf_op jit(solution)/shard_map/ppermute | solution.py:350
  73.0 1.2 collective-permute-start.7
  87.0 6.7 %collective-permute-start.10 = (bf16[48,1280]{1,0:T(8,128)(2,1)S(1)}, bf16[48,1280]{1,0:T(8,128)(2,1)S(1)}, u32[]{:S(2)}, u32[]{:S(2)}) collective-permute-start(bf16[48,1280]{1,0:T(8,128)(2,1)S(1)} %get-tuple-element.75.a0), channel_id=1, source_target_pairs={{0,1},{1,2},{2,3},{3,0},{4,7},{5,4},{6,5},{7,6},{8,9},{9,10},{10,1... | collective-permute-start | bytes 368648 | tf_op jit(solution)/shard_map/ppermute | solution.py:350
  89.8 10.1 %collective-permute-start.9 = (bf16[48,1152]{1,0:T(8,128)(2,1)S(1)}, bf16[48,1152]{1,0:T(8,128)(2,1)S(1)}, u32[]{:S(2)}, u32[]{:S(2)}) collective-permute-start(bf16[48,1152]{1,0:T(8,128)(2,1)S(1)} %get-tuple-element.76.b0), channel_id=1, source_target_pairs={{0,3},{1,0},{2,1},{3,2},{4,5},{5,6},{6,7},{7,4},{8,11},{9,8},{10,9... | collective-permute-start | bytes 331784 | tf_op jit(solution)/shard_map/ppermute | solution.py:350
  90.2 15.8 %collective-permute-start.8 = (bf16[48,1280]{1,0:T(8,128)(2,1)S(1)}, bf16[48,1280]{1,0:T(8,128)(2,1)S(1)}, u32[]{:S(2)}, u32[]{:S(2)}) collective-permute-start(bf16[48,1280]{1,0:T(8,128)(2,1)S(1)} %get-tuple-element.75.a0), channel_id=1, source_target_pairs={{0,3},{1,0},{2,1},{3,2},{4,5},{5,6},{6,7},{7,4},{8,11},{9,8},{10,9... | collective-permute-start | bytes 368648 | tf_op jit(solution)/shard_map/ppermute | solution.py:350
  93.7 14.2 %collective-permute-start.11 = (bf16[48,1280]{1,0:T(8,128)(2,1)S(1)}, bf16[48,1280]{1,0:T(8,128)(2,1)S(1)}, u32[]{:S(2)}, u32[]{:S(2)}) collective-permute-start(bf16[48,1280]{1,0:T(8,128)(2,1)S(1)} %collective-permute-done.10.a3), channel_id=1, source_target_pairs={{0,1},{1,2},{2,3},{3,0},{4,7},{5,4},{6,5},{7,6},{8,9},{9,10},{10,1... | collective-permute-start | bytes 368648 | tf_op jit(solution)/shard_map/ppermute | solution.py:350
  96.9 9.0 %collective-permute-start.13 = (bf16[48,1152]{1,0:T(8,128)(2,1)S(1)}, bf16[48,1152]{1,0:T(8,128)(2,1)S(1)}, u32[]{:S(2)}, u32[]{:S(2)}) collective-permute-start(bf16[48,1152]{1,0:T(8,128)(2,1)S(1)} %get-tuple-element.76.b0), channel_id=1, source_target_pairs={{0,1},{1,2},{2,3},{3,0},{4,7},{5,4},{6,5},{7,6},{8,9},{9,10},{10,1... | collective-permute-start | bytes 331784 | tf_op jit(solution)/shard_map/ppermute | solution.py:350
  99.9 8.0 %collective-permute-start.12 = (bf16[48,1152]{1,0:T(8,128)(2,1)S(1)}, bf16[48,1152]{1,0:T(8,128)(2,1)S(1)}, u32[]{:S(2)}, u32[]{:S(2)}) collective-permute-start(bf16[48,1152]{1,0:T(8,128)(2,1)S(1)} %collective-permute-done.9.b1), channel_id=1, source_target_pairs={{0,3},{1,0},{2,1},{3,2},{4,5},{5,6},{6,7},{7,4},{8,11},{9,8},{10,9... | collective-permute-start | bytes 331784 | tf_op jit(solution)/shard_map/ppermute | solution.py:350
  110.8 4.4 %collective-permute-start.14 = (f32[128,1280]{1,0:T(8,128)S(1)}, f32[128,1280]{1,0:T(8,128)S(1)}, u32[]{:S(2)}, u32[]{:S(2)}) collective-permute-start(f32[128,1280]{1,0:T(8,128)S(1)} %get-tuple-element.82), channel_id=1, source_target_pairs={{0,4},{4,0},{1,5},{5,1},{2,6},{6,2},{3,7},{7,3},{8,12},{12,8},{9,1... | collective-permute-start | bytes 1966088 | tf_op jit(solution)/shard_map/ppermute | solution.py:354
  113.5 18.8 %copy-start.4 = (s32[4]{0:T(128)S(1)}, s32[4]{0:T(128)}, u32[]{:S(2)}) copy-start(s32[4]{0:T(128)} %valid.1) | copy-start | bytes 52
  116.8 14.2 %all-to-all-start.11 = ((s16[32,8,768]{2,1,0:T(8,128)(2,1)}), s16[32,8,768]{2,1,0:T(8,128)(2,1)S(1)}, u32[]{:S(2)}, u32[]{:S(2)}) async-start(s16[32,8,768]{2,1,0:T(8,128)(2,1)} %bitcast.27), calls=%async_computation.11 | async-start | bytes 786432 | tf_op jit(solution)/shard_map/all_to_all | solution.py:437
  165.6 18.8 %all-to-all-start.3 = ((bf16[64,4,1280]{2,1,0:T(4,128)(2,1)}), bf16[64,4,1280]{2,1,0:T(4,128)(2,1)S(1)}, u32[]{:S(2)}, u32[]{:S(2)}) async-start(bf16[64,4,1280]{2,1,0:T(4,128)(2,1)} %broadcast_in_dim.3), calls=%async_computation.3 | async-start | bytes 1310720 | tf_op jit(solution)/shard_map/cond/branch_0_fun/all_to_all | solution.py:358
  185.3 61.6 %all-to-all-start.2 = ((f32[4,64,2374]{2,1,0:T(8,128)}), f32[4,64,2374]{2,1,0:T(8,128)S(1)}, u32[]{:S(2)}, u32[]{:S(2)}) async-start(f32[4,64,2374]{2,1,0:T(8,128)} %fusion.4), calls=%async_computation.2 | async-start | bytes 4980736 | tf_op jit(solution)/shard_map/cond/branch_0_fun/all_to_all | solution.py:454
  246.9 56.2 %all-to-all-start.4 = ((f32[4,64,2374]{2,1,0:T(8,128)}), f32[4,64,2374]{2,1,0:T(8,128)}, u32[]{:S(2)}, u32[]{:S(2)}) async-start(f32[4,64,2374]{2,1,0:T(8,128)} %fusion.2), calls=%async_computation.4 | async-start | bytes 4980736 | tf_op jit(solution)/shard_map/cond/branch_0_fun/all_to_all | solution.py:454
  363.9 10.8 %all-to-all-start.6 = ((f32[4,8,128]{2,1,0:T(8,128)}), f32[4,8,128]{2,1,0:T(8,128)S(1)}, u32[]{:S(2)}, u32[]{:S(2)}) async-start(f32[4,8,128]{2,1,0:T(8,128)} %broadcast_in_dim.6), calls=%async_computation.6 | async-start | bytes 32768 | tf_op jit(solution)/shard_map/cond/branch_0_fun/all_to_all | solution.py:358
  374.7 28.5 %all-to-all-start.8 = ((f32[64,4,1280]{2,1,0:T(4,128)}), f32[64,4,1280]{2,1,0:T(4,128)S(1)}, u32[]{:S(2)}, u32[]{:S(2)}) async-start(f32[64,4,1280]{2,1,0:T(4,128)} %copy.35), calls=%async_computation.8 | async-start | bytes 2621440 | tf_op jit(solution)/shard_map/cond/branch_0_fun/all_to_all | solution.py:499
  (4 other events, 57.2 us)
